TPU v7x, 32 devices: a whole 2x2x4 slice. The times are simulated.
32 devices in a mesh: ctx: 8 (over z, core), tp: 4 (over y, x).
Axes of the slice: x: 2, y: 2, z: 4, core: 2. Of those that a mesh axis runs over, the one named last changes fastest.
Arguments:
- queries: bfloat16 [1024, 8192], P('ctx', 'tp'), may hold values from -6 to 6
- keys_in: bfloat16 [1024, 8192], P('ctx', 'tp'), may hold values from -6 to 6
- values_in: bfloat16 [1024, 8192], P('ctx', 'tp'), may hold values from -6 to 6
- decay_rates: float32 [8192, 16], P('tp'), may hold values from 0.00029296876 to 0.03
- residues: float32 [8192, 16], P('tp'), may hold values from -1.5 to 1.5
- skip_gain: float32 [8192], P('tp'), may hold values from -4 to 4
- cotangent: bfloat16 [1024, 8192], P('ctx', 'tp'), may hold values from -6 to 6
Outputs:
- operator_out: bfloat16 [1024, 8192], P('ctx', 'tp')
- grad_queries: bfloat16 [1024, 8192], P('ctx', 'tp')
- grad_keys: bfloat16 [1024, 8192], P('ctx', 'tp')
- grad_values: bfloat16 [1024, 8192], P('ctx', 'tp')
- grad_residues: float32 [8192, 16], P('tp')
All inputs are finite; a program needn't handle non-finite values.
Results may differ from a plain program's by a relative error of at most 0.0054.
Values may be sent and summed in bfloat16 or wider, within the bound.
No kernel may reach another device: no remote copies, remote signals or barrier semaphores. Data moves between devices by JAX's collectives and lax.ppermute only.
A program may use at most 64 MiB of HBM per device.

v0:
```python
from functools import partial
import math

import jax
import jax.numpy as jnp
from jax import lax
from jax.experimental import pallas as pl
from jax.experimental.pallas import tpu as pltpu
from jax.sharding import PartitionSpec as P

F32 = jnp.float32
WIRE = jnp.bfloat16
LANES = 128
UNROLL = 8
STEP_ROWS = 32
KERNEL = pltpu.CompilerParams(vmem_limit_bytes=24 * 1024 * 1024)
HBM = pl.BlockSpec(memory_space=pltpu.HBM)
VMEM = pl.BlockSpec(memory_space=pltpu.VMEM)


def reorder(rows, inner):
    outer = rows // inner
    first = lax.broadcasted_iota(jnp.int32, (rows, rows), 0)
    second = lax.broadcasted_iota(jnp.int32, (rows, rows), 1)

    def matrix(to, fro):
        if inner & (inner - 1) == 0 and outer & (outer - 1) == 0:
            low, high = inner.bit_length() - 1, outer.bit_length() - 1
            same = (fro & (inner - 1)) * outer + (fro >> low) == to
        else:
            same = (fro % inner) * outer + fro // inner == to
        return jnp.where(same, 1.0, 0.0).astype(jnp.bfloat16)

    return matrix(first, second), matrix(second, first)


def tree_sum(items):
    items = list(items)
    while len(items) > 1:
        items = [
            items[i] + items[i + 1] if i + 1 < len(items) else items[i]
            for i in range(0, len(items), 2)
        ]
    return items[0]


def half_units(which, blocks, modes, sub):
    if blocks == 1:
        return [(0, which * (modes // 2 * sub), modes // 2)]
    count = blocks // 2
    return [
        (which * count + j, (which * count + j) * (modes * sub), modes) for j in range(count)
    ]


def to_scan_order(to_scan, pairs, part, i, block, targets):
    size, sub = to_scan.shape[0], to_scan.shape[0] // part
    rows = slice(i * part, (i + 1) * part)
    sides = []
    for left, right in pairs:
        stacked = []
        for s in range(sub):
            cols = pl.ds(pl.multiple_of((block * sub + s) * LANES, LANES), LANES)
            product = left[rows, cols].astype(F32) * right[rows, cols].astype(F32)
            stacked.append(product.astype(jnp.bfloat16))
        sides.append(jnp.concatenate(stacked, axis=0))
    ordered = jnp.dot(
        to_scan[...], jnp.concatenate(sides, axis=1), preferred_element_type=F32
    )
    for j, target in enumerate(targets):
        target[block, i * size : (i + 1) * size, :] = ordered[:, j * LANES : (j + 1) * LANES]


def scan_states(unit, sub, gated_ref, pulled_ref, decay_ref, out_ref, at_row):
    block, base, modes = unit
    seq = gated_ref.shape[1] // sub
    decay = [
        decay_ref[pl.ds(pl.multiple_of(base + n * sub, sub), sub), :] for n in range(modes)
    ]
    first = tuple(jnp.zeros((sub, LANES), F32) for _ in range(modes))

    def forward(j, carry):
        held, inner = list(carry[0]), list(carry[1])
        for u in range(UNROLL):
            at = pl.ds(pl.multiple_of((j * UNROLL + u) * sub, sub), sub)
            x = gated_ref[block, at, :]
            p = pulled_ref[block, at, :]
            for n in range(modes):
                held[n] = decay[n] * held[n] + x
                inner[n] = inner[n] + p * held[n]
        return tuple(held), tuple(inner)

    def backward(j, carry):
        held = list(carry)
        for u in range(UNROLL):
            at = pl.ds(pl.multiple_of((seq - 1 - (j * UNROLL + u)) * sub, sub), sub)
            p = pulled_ref[block, at, :]
            for n in range(modes):
                held[n] = decay[n] * held[n] + p
        return tuple(held)

    ends, inner = lax.fori_loop(0, seq // UNROLL, forward, (first, first))
    for n in range(modes):
        rows = slice(at_row + n * sub, at_row + (n + 1) * sub)
        out_ref[0, rows, :] = ends[n]
        out_ref[2, rows, :] = inner[n]
    starts = lax.fori_loop(0, seq // UNROLL, backward, first)
    for n in range(modes):
        out_ref[1, at_row + n * sub : at_row + (n + 1) * sub, :] = starts[n]


def send_kernel(
    q_hbm,
    k_hbm,
    v_hbm,
    ct_hbm,
    rate_hbm,
    res_hbm,
    send_ref,
    q_ref,
    k_ref,
    v_ref,
    ct_ref,
    gated_ref,
    pulled_ref,
    rate_ref,
    decay_ref,
    coef_ref,
    to_scan,
    from_scan,
    rate_cols,
    res_cols,
    sems,
):
    seq, channels = q_ref.shape
    modes = rate_cols.shape[0]
    blocks = gated_ref.shape[0]
    sub = channels // (blocks * LANES)
    part = math.gcd(seq, STEP_ROWS)
    parts = seq // part
    which = 1 - lax.axis_index("ctx") % 2
    pairs = ((k_hbm, k_ref), (v_hbm, v_ref), (ct_hbm, ct_ref), (q_hbm, q_ref))
    copies = []

    def start(source, target):
        copy = pltpu.make_async_copy(source, target, sems.at[len(copies)])
        copy.start()
        copies.append(copy)

    start(rate_hbm, rate_cols)
    start(res_hbm, res_cols)
    width = channels // min(blocks, 2)
    cols = pl.ds(pl.multiple_of(which * width, LANES) if blocks > 1 else 0, width)
    for i in range(parts):
        rows = pl.ds(i * part, part)
        for source, target in pairs:
            start(source.at[rows, cols], target.at[rows, cols])
    if blocks > 1:
        cols = pl.ds(pl.multiple_of((1 - which) * width, LANES), width)
        for source, target in pairs:
            start(source.at[:, cols], target.at[:, cols])

    def spread(source, target):
        for b in range(blocks):
            for s in range(sub):
                cols = slice((b * sub + s) * LANES, (b * sub + s + 1) * LANES)
                target[pl.ds(b * modes * sub + s, modes, stride=sub), :] = source[:, cols]

    to_scan[...], from_scan[...] = reorder(part * sub, part)
    copies[0].wait()
    spread(rate_cols, rate_ref)
    copies[1].wait()
    spread(res_cols, coef_ref)
    rate = rate_ref[...]
    decay_ref[...] = jnp.exp(-rate)
    coef_ref[...] = coef_ref[...] * jnp.sqrt(1.0 - jnp.exp(-2.0 * rate))
    units = half_units(which, blocks, modes, sub)
    lines = ((k_ref, v_ref), (ct_ref, q_ref))
    for i in range(parts):
        for copy in copies[2 + 4 * i : 6 + 4 * i]:
            copy.wait()
        for unit in units:
            to_scan_order(to_scan, lines, part, i, unit[0], (gated_ref, pulled_ref))
    for at, unit in enumerate(units):
        at_row = at * unit[2] * sub
        scan_states(unit, sub, gated_ref, pulled_ref, decay_ref, send_ref, at_row)
    for copy in copies[2 + 4 * parts :]:
        copy.wait()


def keep_kernel(
    q_ref,
    k_ref,
    v_ref,
    ct_ref,
    decay_ref,
    to_scan,
    gated_in,
    pulled_in,
    keep_ref,
    gated_ref,
    pulled_ref,
    sems,
):
    seq, channels = q_ref.shape
    blocks = gated_ref.shape[0]
    sub = channels // (blocks * LANES)
    modes = decay_ref.shape[0] // (blocks * sub)
    part = math.gcd(seq, STEP_ROWS)
    which = lax.axis_index("ctx") % 2
    count = max(blocks // 2, 1)
    done = pl.ds((1 - which) * count if blocks > 1 else 0, count)
    copies = [
        pltpu.make_async_copy(gated_in.at[done], gated_ref.at[done], sems.at[0]),
        pltpu.make_async_copy(pulled_in.at[done], pulled_ref.at[done], sems.at[1]),
    ]
    for copy in copies:
        copy.start()
    units = half_units(which, blocks, modes, sub)
    lines = (gated_in, pulled_in)
    if blocks > 1:
        lines = (gated_ref, pulled_ref)
        for i in range(seq // part):
            for unit in units:
                pairs = ((k_ref, v_ref), (ct_ref, q_ref))
                to_scan_order(to_scan, pairs, part, i, unit[0], lines)
    for at, unit in enumerate(units):
        scan_states(unit, sub, *lines, decay_ref, keep_ref, at * unit[2] * sub)
    for copy in copies:
        copy.wait()


def own_rows(rate_ref, half):
    core = lax.axis_index("ctx") % 2
    return rate_ref[pl.ds(pl.multiple_of(core * half, half), half), :]


def joined(is_right, mine, other, span, step):
    left = [jnp.where(is_right, o, m) for m, o in zip(mine, other)]
    right = [jnp.where(is_right, m, o) for m, o in zip(mine, other)]
    return (
        span * left[0] + right[0],
        left[1] + span * right[1],
        left[2] + right[2] + step * right[1] * left[0],
    )


def put_wire(wire_ref, is_last, next_right, block):
    if is_last:
        wire_ref[0] = jnp.where(next_right, block[1], block[0]).astype(wire_ref.dtype)
        wire_ref[1] = block[2].astype(wire_ref.dtype)
    else:
        for kind in range(3):
            wire_ref[kind] = block[kind].astype(wire_ref.dtype)


def pair_kernel(seq, is_last, keep_ref, got_ref, rate_ref, after_ref, block_ref, wire_ref):
    rate = own_rows(rate_ref, keep_ref.shape[1])
    place = lax.axis_index("ctx")
    block = joined(
        place % 2 == 1,
        [keep_ref[i] for i in range(3)],
        [got_ref[i] for i in range(3)],
        jnp.exp(-rate * seq),
        jnp.exp(-rate),
    )
    for kind in range(3):
        block_ref[kind] = block[kind]
    block_ref[3] = jnp.zeros_like(rate)
    block_ref[4] = jnp.zeros_like(rate)
    put_wire(wire_ref, is_last, (place // 2) % 2 == 1, block)


def carries_with(block_ref, end_state, start_state, level, seq, rate):
    place = lax.axis_index("ctx")
    is_right = (place >> level) % 2 == 1
    chips = 1 << (level - 1)
    at = (place // 2) % chips
    before = at * (2 * seq)
    behind = (chips - 1 - at) * (2 * seq)
    ahead = block_ref[3] + jnp.where(
        is_right, jnp.exp(-rate * before.astype(F32)) * end_state, 0.0
    )
    after = block_ref[4] + jnp.where(
        is_right, 0.0, jnp.exp(-rate * behind.astype(F32)) * start_state
    )
    return is_right, ahead, after


def level_kernel(
    seq, level, is_last, block_ref, got_ref, rate_ref, after_ref, out_ref, wire_ref
):
    rate = own_rows(rate_ref, block_ref.shape[1])
    got = [got_ref[i].astype(F32) for i in range(3)]
    is_right, ahead, after = carries_with(block_ref, got[0], got[1], level, seq, rate)
    block = joined(
        is_right,
        [block_ref[i] for i in range(3)],
        got,
        jnp.exp(-rate * (seq << level)),
        jnp.exp(-rate),
    )
    for kind in range(3):
        out_ref[kind] = block[kind]
    out_ref[3] = ahead
    out_ref[4] = after
    next_right = (lax.axis_index("ctx") >> (level + 1)) % 2 == 1
    put_wire(wire_ref, is_last, next_right, block)


def last_kernel(
    seq,
    level,
    block_ref,
    got_ref,
    rate_ref,
    keep_ref,
    sibling_ref,
    after_ref,
    mine_ref,
    other_ref,
    share_ref,
):
    half = block_ref.shape[1]
    rate = own_rows(rate_ref, half)
    edge, inner = got_ref[0].astype(F32), got_ref[1].astype(F32)
    is_right, ahead, after = carries_with(block_ref, edge, edge, level, seq, rate)
    own_edge = jnp.where(is_right, block_ref[1], block_ref[0])
    total = block_ref[2] + inner + jnp.exp(-rate) * own_edge * edge
    raw = jnp.sqrt(1.0 - jnp.exp(-2.0 * rate)) * total
    core = lax.axis_index("ctx") % 2
    first = core == 0
    span = jnp.exp(-rate * seq)
    end_first = jnp.where(first, keep_ref[0], sibling_ref[0])
    start_second = jnp.where(first, sibling_ref[1], keep_ref[1])
    ahead_second = span * ahead + end_first
    after_first = span * after + start_second
    mine_ref[0:half, :] = jnp.where(first, ahead, ahead_second)
    mine_ref[half : 2 * half, :] = jnp.where(first, after_first, after)
    other_ref[0:half, :] = jnp.where(first, ahead_second, ahead)
    other_ref[half : 2 * half, :] = jnp.where(first, after, after_first)
    squares = raw * raw
    share_ref[...] = tree_sum([squares[i : i + 8, :] for i in range(0, half, 8)])
    mine_ref[2 * half : 3 * half, :] = raw
    other_ref[2 * half : 3 * half, :] = raw


def place_halves(mine_ref, other_ref, first, target):
    half = target.shape[0] // 2
    core = lax.axis_index("ctx") % 2
    for ref, at in ((mine_ref, core), (other_ref, 1 - core)):
        rows = pl.ds(pl.multiple_of(at * half, half), half)
        target[rows, :] = ref[first : first + half, :]


def mode_rows(block, modes, sub):
    return [slice((block * modes + n) * sub, (block * modes + n + 1) * sub) for n in range(modes)]


def local_kernel(reverse, modes, lines_ref, decay_ref, coef_ref, after_ref, out_ref):
    blocks = lines_ref.shape[0]
    sub = decay_ref.shape[0] // (blocks * modes)
    seq = lines_ref.shape[1] // sub
    for b in range(blocks):
        rows = mode_rows(b, modes, sub)
        decay = [decay_ref[r, :] for r in rows]
        coef = [coef_ref[r, :] for r in rows]

        def body(j, carry):
            held = list(carry)
            for u in range(UNROLL):
                t = j * UNROLL + u
                if reverse:
                    t = seq - 1 - t
                at = pl.ds(pl.multiple_of(t * sub, sub), sub)
                x = lines_ref[b, at, :]
                total = [None] * 4
                for n in range(modes):
                    held[n] = decay[n] * held[n] + x
                    term = coef[n] * held[n]
                    total[n % 4] = term if n < 4 else total[n % 4] + term
                out_ref[b, at, :] = tree_sum(total)
            return tuple(held)

        first = tuple(jnp.zeros((sub, LANES), F32) for _ in range(modes))
        lax.fori_loop(0, seq // UNROLL, body, first)


def add_carries(reverse, unit, sub, decay_ref, coef_ref, states_ref, at_row, source, target, at):
    _, base, modes = unit
    seq = target.shape[1] // sub
    rows = [pl.ds(pl.multiple_of(base + n * sub, sub), sub) for n in range(modes)]
    decay = [decay_ref[r, :] for r in rows]
    first = tuple(
        coef_ref[r, :] * states_ref[at_row + n * sub : at_row + (n + 1) * sub, :]
        for n, r in enumerate(rows)
    )

    def body(j, carry):
        held = list(carry)
        for u in range(UNROLL):
            t = j * UNROLL + u
            if reverse:
                t = seq - 1 - t
            where = pl.ds(pl.multiple_of(t * sub, sub), sub)
            total = [source[where, :], None, None, None]
            for n in range(modes):
                held[n] = decay[n] * held[n]
                total[n % 4] = held[n] if total[n % 4] is None else total[n % 4] + held[n]
            target[at, where, :] = tree_sum(total)
        return tuple(held)

    lax.fori_loop(0, seq // UNROLL, body, first)


def own_kernel(modes, conv_ref, adj_ref, decay_ref, coef_ref, mine_ref, conv_own, adj_own):
    blocks = conv_ref.shape[0]
    sub = decay_ref.shape[0] // (blocks * modes)
    half = decay_ref.shape[0] // 2
    core = lax.axis_index("ctx") % 2
    for i, unit in enumerate(half_units(core, blocks, modes, sub)):
        at_row = i * unit[2] * sub
        for reverse, source, target in ((False, conv_ref, conv_own), (True, adj_ref, adj_own)):
            add_carries(
                reverse,
                unit,
                sub,
                decay_ref,
                coef_ref,
                mine_ref,
                at_row + half * reverse,
                source.at[unit[0]],
                target,
                i,
            )


def other_carries(reverse, modes, decay_ref, coef_ref, other_ref, local_ref, own_ref, whole, sem):
    blocks, own_blocks = local_ref.shape[0], own_ref.shape[0]
    sub = decay_ref.shape[0] // (blocks * modes)
    half = decay_ref.shape[0] // 2
    core = lax.axis_index("ctx") % 2
    copy = pltpu.make_async_copy(own_ref, whole.at[pl.ds(core * own_blocks, own_blocks)], sem)
    if blocks > 1:
        copy.start()
    for i, unit in enumerate(half_units(1 - core, blocks, modes, sub)):
        source = local_ref.at[unit[0]] if blocks > 1 else own_ref.at[0]
        at_row = i * unit[2] * sub + half * reverse
        add_carries(
            reverse, unit, sub, decay_ref, coef_ref, other_ref, at_row, source, whole, unit[0]
        )
    if blocks > 1:
        copy.wait()


def line_outputs(
    from_scan, left, right, scales, skip_ref, scanned, targets, which, done_with=None
):
    seq, channels = left.shape
    blocks = scanned.shape[0]
    sub = channels // (blocks * LANES)
    part = math.gcd(seq, STEP_ROWS)
    for i in which:
        rows = slice(i * part, (i + 1) * part)
        to_rows = slice((i - which[0]) * part, (i - which[0] + 1) * part)
        stacked = jnp.concatenate(
            [scanned[b, i * part * sub : (i + 1) * part * sub, :] for b in range(blocks)], axis=1
        ).astype(jnp.bfloat16)
        ordered = jnp.dot(from_scan[...], stacked, preferred_element_type=F32)
        for b in range(blocks):
            for s in range(sub):
                cols = slice((b * sub + s) * LANES, (b * sub + s + 1) * LANES)
                own = ordered[s * part : (s + 1) * part, b * LANES : (b + 1) * LANES]
                line = left[rows, cols].astype(F32) * right[rows, cols].astype(F32)
                mixed = own + skip_ref[:, cols] * line.astype(jnp.bfloat16).astype(F32)
                for scale, target in zip(scales, targets):
                    target[to_rows, cols] = (scale[rows, cols].astype(F32) * mixed).astype(
                        jnp.bfloat16
                    )
        if done_with is not None:
            done_with(pl.ds((i - which[0]) * part, part), pl.ds(i * part, part))


def forward_kernel(
    modes,
    q_ref,
    k_ref,
    v_ref,
    ct_ref,
    decay_ref,
    coef_ref,
    skip_ref,
    other_ref,
    from_scan,
    conv_ref,
    conv_own,
    after_ref,
    out_ref,
    gq_ref,
    token_ref,
    scanned,
    sem,
):
    token_ref[...] = jnp.zeros_like(token_ref)
    other_carries(
        False, modes, decay_ref, coef_ref, other_ref, conv_ref, conv_own, scanned, sem
    )
    line_outputs(
        from_scan,
        k_ref,
        v_ref,
        (q_ref, ct_ref),
        skip_ref,
        scanned,
        (out_ref, gq_ref),
        range(k_ref.shape[0] // math.gcd(k_ref.shape[0], STEP_ROWS)),
    )


def early_parts(seq):
    parts = seq // math.gcd(seq, STEP_ROWS)
    return range((parts + 1) // 2), range((parts + 1) // 2, parts)


def adjoint_kernel(
    modes,
    q_ref,
    k_ref,
    v_ref,
    ct_ref,
    decay_ref,
    coef_ref,
    skip_ref,
    other_ref,
    from_scan,
    adj_ref,
    adj_own,
    out_rows,
    gq_rows,
    after_ref,
    out_hbm,
    gq_hbm,
    scanned,
    gk_ref,
    gv_ref,
    token_ref,
    sems,
):
    token_ref[...] = jnp.zeros_like(token_ref)
    copies = [
        pltpu.make_async_copy(out_rows, out_hbm, sems.at[0]),
        pltpu.make_async_copy(gq_rows, gq_hbm, sems.at[1]),
    ]
    for copy in copies:
        copy.start()
    other_carries(
        True, modes, decay_ref, coef_ref, other_ref, adj_ref, adj_own, scanned, sems.at[2]
    )
    line_outputs(
        from_scan,
        ct_ref,
        q_ref,
        (v_ref, k_ref),
        skip_ref,
        scanned,
        (gk_ref, gv_ref),
        early_parts(q_ref.shape[0])[0],
    )
    for copy in copies:
        copy.wait()


def last_outputs_kernel(limit, *refs):
    q_ref, k_ref, v_ref, ct_ref, scanned, skip_ref, gk_early, gv_early = refs[:8]
    mine_ref, other_ref, from_scan = refs[8:11]
    share_refs = refs[12:-8]
    raw_hbm, gk_hbm, gv_hbm, gk_rows, gv_rows, raw_cols, states, sems = refs[-8:]
    copies = []

    def start(source, target):
        copy = pltpu.make_async_copy(source, target, sems.at[len(copies)])
        copy.start()
        copies.append(copy)

    early = pl.ds(0, gk_early.shape[0])
    start(gk_early, gk_hbm.at[early])
    start(gv_early, gv_hbm.at[early])
    clip(limit, scanned.shape[0], mine_ref, other_ref, share_refs, raw_cols, states)
    start(raw_cols, raw_hbm)

    def send(at, to):
        start(gk_rows.at[at], gk_hbm.at[to])
        start(gv_rows.at[at], gv_hbm.at[to])

    late = early_parts(q_ref.shape[0])[1]
    if len(late) > 0:
        sides, targets = (v_ref, k_ref), (gk_rows, gv_rows)
        line_outputs(
            from_scan, ct_ref, q_ref, sides, skip_ref, scanned, targets, late, send
        )
    for copy in copies:
        copy.wait()


def add_kernel(left_ref, right_ref, after_ref, out_ref):
    out_ref[...] = left_ref[...] + right_ref[...]


def clip(limit, blocks, mine_ref, other_ref, share_refs, out_ref, states):
    modes = out_ref.shape[0]
    sub = out_ref.shape[1] // (blocks * LANES)
    half = states.shape[0] // 2
    place_halves(mine_ref, other_ref, 2 * half, states)
    square = jnp.sum(tree_sum([ref[...] for ref in share_refs]))
    factor = jnp.minimum(1.0, limit * lax.rsqrt(jnp.full((1, LANES), square + 1e-06, F32)))
    for b in range(blocks):
        for s in range(sub):
            cols = slice((b * sub + s) * LANES, (b * sub + s + 1) * LANES)
            rows = pl.ds(b * modes * sub + s, modes, stride=sub)
            out_ref[:, cols] = states[rows, :] * factor


def shards(queries, keys_in, values_in, decay_rates, residues, skip_gain, cotangent):
    seq, channels = queries.shape
    modes = decay_rates.shape[1]
    ctx = lax.axis_size("ctx")
    tp = lax.axis_size("tp")
    levels = ctx.bit_length() - 1
    groups = channels // LANES
    sub = math.gcd(groups, 8)
    blocks = groups // sub
    half = modes * groups // 2
    part = math.gcd(seq, STEP_ROWS)
    parts, size = seq // part, part * sub

    def swap(value, bit):
        return lax.ppermute(value, "ctx", [(i, i ^ (1 << bit)) for i in range(ctx)])

    def rows(*shape, dtype=F32):
        return jax.ShapeDtypeStruct((*shape, LANES), dtype)

    line_shape = jax.ShapeDtypeStruct((seq, channels), jnp.bfloat16)
    table_shape = jax.ShapeDtypeStruct((modes, channels), F32)
    line_scratch = pltpu.VMEM((seq, channels), jnp.bfloat16)
    table_scratch = pltpu.VMEM((modes, channels), F32)
    elements = seq * channels * modes
    sources = (queries, keys_in, values_in, cotangent, decay_rates.T, residues.T)

    (
        send,
        q,
        k,
        v,
        ct,
        gated,
        pulled,
        row_rates,
        row_decay,
        row_coefs,
        to_scan,
        from_scan,
    ) = pl.pallas_call(
        send_kernel,
        in_specs=[HBM] * 6,
        out_specs=[VMEM] * 12,
        out_shape=[rows(3, half)]
        + [line_shape] * 4
        + [rows(blocks, seq * sub)] * 2
        + [rows(2 * half)] * 3
        + [jax.ShapeDtypeStruct((size, size), jnp.bfloat16)] * 2,
        scratch_shapes=[
            table_scratch,
            table_scratch,
            pltpu.SemaphoreType.DMA((4 * parts + 6,)),
        ],
        compiler_params=KERNEL,
        cost_estimate=pl.CostEstimate(
            flops=3 * elements, bytes_accessed=8 * seq * channels, transcendentals=0
        ),
        name="sent_states",
    )(*[pltpu.with_memory_space_constraint(item, pltpu.HBM) for item in sources])
    sibling = swap(send, 0)
    keep, gated, pulled = pl.pallas_call(
        keep_kernel,
        out_shape=[rows(3, half)] + [rows(blocks, seq * sub)] * 2,
        scratch_shapes=[pltpu.SemaphoreType.DMA((2,))],
        compiler_params=KERNEL,
        cost_estimate=pl.CostEstimate(
            flops=3 * elements, bytes_accessed=8 * seq * channels, transcendentals=0
        ),
        name="kept_states",
    )(q, k, v, ct, row_decay, to_scan, gated, pulled)

    def wire(level):
        return rows(2 if level == levels - 1 else 3, half, dtype=WIRE)

    whole = rows(blocks, seq * sub)
    whole_scratch = pltpu.VMEM((blocks, seq * sub, LANES), F32)
    states_scratch = pltpu.VMEM((2 * half, LANES), F32)
    def local(reverse, after, name):
        return pl.pallas_call(
            partial(local_kernel, reverse, modes),
            out_shape=whole,
            compiler_params=KERNEL,
            cost_estimate=pl.CostEstimate(
                flops=4 * elements, bytes_accessed=8 * seq * channels, transcendentals=0
            ),
            name=name,
        )(pulled if reverse else gated, row_decay, row_coefs, after)

    block, packed = pl.pallas_call(
        partial(pair_kernel, seq, levels == 2),
        out_shape=[rows(5, half), wire(1)],
        compiler_params=KERNEL,
        name="chip_states",
    )(keep, sibling, row_rates, row_rates[:8])
    got = swap(packed, 1)
    conv = local(False, block[4, :8], "local_conv")
    for level in range(1, levels - 1):
        block, packed = pl.pallas_call(
            partial(level_kernel, seq, level, level + 1 == levels - 1),
            out_shape=[rows(5, half), wire(level + 1)],
            compiler_params=KERNEL,
            name="block_states",
        )(block, got, row_rates, conv[0, :8])
        got = swap(packed, level + 1)
    adj = local(True, block[4, :8], "local_adjoint")
    mine, other, square = pl.pallas_call(
        partial(last_kernel, seq, levels - 1),
        out_shape=[rows(3 * half)] * 2 + [rows(8)],
        compiler_params=KERNEL,
        name="carries",
    )(block, got, row_rates, keep, sibling, adj[0, :8])
    other = swap(other, 0)
    skip = skip_gain.reshape(1, channels)
    early, late = early_parts(seq)
    early_shape = jax.ShapeDtypeStruct((seq * len(early) // parts, channels), jnp.bfloat16)
    late_scratch = pltpu.VMEM((seq * max(len(late), 1) // parts, channels), jnp.bfloat16)
    own_shape = rows(max(blocks // 2, 1), seq * sub)
    kept = {}

    def add_own(after):
        kept["conv"], kept["adj"] = pl.pallas_call(
            partial(own_kernel, modes),
            out_shape=[own_shape] * 2,
            compiler_params=KERNEL,
            cost_estimate=pl.CostEstimate(
                flops=2 * elements, bytes_accessed=8 * seq * channels, transcendentals=0
            ),
            name="own_carries",
        )(conv, adj, row_decay, row_coefs, mine)
        return kept["adj"][0, :8]

    def forward_outputs(after):
        kept["out"], kept["gq"], token = pl.pallas_call(
            partial(forward_kernel, modes),
            out_shape=[line_shape] * 2 + [rows(8)],
            scratch_shapes=[whole_scratch, pltpu.SemaphoreType.DMA],
            compiler_params=KERNEL,
            cost_estimate=pl.CostEstimate(
                flops=2 * elements, bytes_accessed=16 * seq * channels, transcendentals=0
            ),
            name="forward_outputs",
        )(
            q,
            k,
            v,
            ct,
            row_decay,
            row_coefs,
            skip,
            other,
            from_scan,
            conv,
            kept["conv"],
            after,
        )
        return token

    def adjoint_outputs(after):
        results = (
            pl.pallas_call(
                partial(adjoint_kernel, modes),
                in_specs=[VMEM] * 14,
                out_specs=[HBM] * 2 + [VMEM] * 4,
                out_shape=[line_shape] * 2 + [whole] + [early_shape] * 2 + [rows(8)],
                scratch_shapes=[pltpu.SemaphoreType.DMA((3,))],
                compiler_params=KERNEL,
                cost_estimate=pl.CostEstimate(
                    flops=2 * elements, bytes_accessed=8 * seq * channels, transcendentals=0
                ),
                name="adjoint_outputs",
            )(
                q,
                k,
                v,
                ct,
                row_decay,
                row_coefs,
                skip,
                other,
                from_scan,
                adj,
                kept["adj"],
                kept["out"],
                kept["gq"],
                after,
            )
        )
        kept["final"] = results[:-1]
        return results[-1]

    def plus(left, right, after):
        return pl.pallas_call(
            add_kernel,
            in_specs=[VMEM] * 3,
            out_shape=rows(8),
            compiler_params=KERNEL,
            name="square_sum",
        )(left, right, after)

    def tp_swap(value, bit):
        return lax.ppermute(value, "tp", [(i, i ^ (1 << bit)) for i in range(tp)])

    works = [add_own, forward_outputs, adjoint_outputs]
    rounds = [partial(tp_swap, bit=bit) for bit in range(tp.bit_length() - 1)]
    for at, exchange in enumerate(rounds + [partial(swap, bit=0)]):
        if at > 0:
            square = plus(square, share, after)
        share = exchange(square)
        after = works.pop(0)(square) if works else square
    for work in works:
        after = work(after)
    operator_out, grad_queries, scanned, early_keys, early_values = kept["final"]
    grad_residues, grad_keys, grad_values = pl.pallas_call(
        partial(last_outputs_kernel, math.sqrt(channels * tp * modes)),
        in_specs=[VMEM] * 14,
        out_specs=[HBM] * 3,
        out_shape=[table_shape] + [line_shape] * 2,
        scratch_shapes=[
            late_scratch,
            late_scratch,
            table_scratch,
            states_scratch,
            pltpu.SemaphoreType.DMA((2 * parts + 3,)),
        ],
        compiler_params=KERNEL,
        cost_estimate=pl.CostEstimate(
            flops=elements, bytes_accessed=8 * seq * channels, transcendentals=0
        ),
        name="last_outputs",
    )(
        q,
        k,
        v,
        ct,
        scanned,
        skip,
        early_keys,
        early_values,
        mine,
        other,
        from_scan,
        after,
        square,
        share,
    )
    return (operator_out, grad_queries, grad_keys, grad_values, grad_residues.T)


def solution(mesh):
    lines, tables = P("ctx", "tp"), P("tp", None)
    in_specs = (lines, lines, lines, tables, tables, P("tp"), lines)
    out_specs = (lines, lines, lines, lines, tables)
    return jax.shard_map(shards, mesh=mesh, in_specs=in_specs, out_specs=out_specs, check_vma=False)
```

profile of v0, /device:TPU:0, one launch (start us, length us, event | category | flops | bytes accessed | tf_op | source)
XLA Modules:
  0.0 30.6 jit_solution(18125688873725167503)
XLA Ops:
  0.6 4.2 %sent_states.1 = (f32[3,128,128]{2,1,0:T(8,128)S(1)}, bf16[128,2048]{1,0:T(8,128)(2,1)S(1)}, bf16[128,2048]{1,0:T(8,128)(2,1)S(1)}, bf16[128,2048]{1,0:T(8,128)(...) custom-call(bf16[128,2048]{1,0:T(8,128)(2,1)} %q_hbm.1, ...), custom_call_target="tpu_custom_call" | custom-call | flops 12582912 | bytes 2097152 | tf_op jit(solution)/shard_map/sent_states/pallas_call | solution.py:662
  4.9 0.5 %collective-permute-start = (f32[3,128,128]{2,1,0:T(8,128)S(1)}, f32[3,128,128]{2,1,0:T(8,128)S(1)}, u32[]{:S(2)}, u32[]{:S(2)}) collective-permute-start(f32[3,128,128]{2,1,0:T(8,128)S(1)} %get-tuple-element.51), channel_id=1, source_target_pairs={{0,4},{4,0},{8,12},{12,8},{16,20},{20,16},{24,28},{28,24},{1,5},{5... | collective-permute-start | bytes 589832 | tf_op jit(solution)/shard_map/ppermute | solution.py:637
  5.4 2.6 %kept_states.1 = (f32[3,128,128]{2,1,0:T(8,128)S(1)}, f32[2,1024,128]{2,1,0:T(8,128)S(1)}, f32[2,1024,128]{2,1,0:T(8,128)S(1)}) custom-call(bf16[128,2048]{1,0:T(8,128)(2,1)S(1)} %get-tuple-element.41.q_ref.refs_0_, bf16[128,2048]{1,0:T(8,128)(2,1)S(1)} %get-tuple-element.42.k_ref.refs_1_, bf16[128,2048]{1,0:T(8,128)(2,1)S(1)} %get-tuple-element.43.v_ref.refs_2_, ...), custom_call_target="tpu_custom_call" | custom-call | flops 12582912 | bytes 2097152 | tf_op jit(solution)/shard_map/kept_states/pallas_call | solution.py:683
  7.9 0.0 collective-permute-done.got_ref.sibling_ref
  7.9 0.1 chip_states.1
  8.0 2.7 %collective-permute-start.1 = (bf16[3,128,128]{2,1,0:T(8,128)(2,1)S(1)}, bf16[3,128,128]{2,1,0:T(8,128)(2,1)S(1)}, u32[]{:S(2)}, u32[]{:S(2)}) collective-permute-start(bf16[3,128,128]{2,1,0:T(8,128)(2,1)S(1)} %get-tuple-element.54), channel_id=1, source_target_pairs={{0,8},{4,12},{8,0},{12,4},{16,24},{20,28},{24,16},{28,20},{1,9},{5... | collective-permute-start | bytes 294920 | tf_op jit(solution)/shard_map/ppermute | solution.py:637
  10.7 2.3 %local_conv.1.conv_ref = f32[2,1024,128]{2,1,0:T(8,128)S(1)} custom-call(f32[2,1024,128]{2,1,0:T(8,128)S(1)} %get-tuple-element.55.lines_ref, f32[256,128]{1,0:T(8,128)S(1)} %get-tuple-element.45.decay_ref, f32[256,128]{1,0:T(8,128)S(1)} %get-tuple-element.46.coef_ref, f32[8,128]{1,0:T(8,128)S(1)} %slice_bitcast_fusion.4.after_ref), custom_call_target="tpu_custom_call" | custom-call | flops 16777216 | bytes 2097152 | tf_op jit(solution)/shard_map/local_conv/pallas_call | solution.py:701
  13.0 1.1 %collective-permute-done.1.got_ref = bf16[3,128,128]{2,1,0:T(8,128)(2,1)S(1)} collective-permute-done((bf16[3,128,128]{2,1,0:T(8,128)(2,1)S(1)}, bf16[3,128,128]{2,1,0:T(8,128)(2,1)S(1)}, u32[]{:S(2)}, u32[]{:S(2)}) %collective-permute-start.1) | collective-permute-done | bytes 98336 | tf_op jit(solution)/shard_map/ppermute | solution.py:637
  14.1 0.1 block_states.1
  14.2 2.8 %collective-permute-start.2 = (bf16[2,128,128]{2,1,0:T(8,128)(2,1)S(1)}, bf16[2,128,128]{2,1,0:T(8,128)(2,1)S(1)}, u32[]{:S(2)}, u32[]{:S(2)}) collective-permute-start(bf16[2,128,128]{2,1,0:T(8,128)(2,1)S(1)} %get-tuple-element.57), channel_id=1, source_target_pairs={{0,16},{4,20},{8,24},{12,28},{16,0},{20,4},{24,8},{28,12},{1,17},{... | collective-permute-start | bytes 196616 | tf_op jit(solution)/shard_map/ppermute | solution.py:637
  17.1 2.3 %local_adjoint.1.adj_ref = f32[2,1024,128]{2,1,0:T(8,128)S(1)} custom-call(f32[2,1024,128]{2,1,0:T(8,128)S(1)} %get-tuple-element.58.lines_ref, f32[256,128]{1,0:T(8,128)S(1)} %get-tuple-element.45.decay_ref, f32[256,128]{1,0:T(8,128)S(1)} %get-tuple-element.46.coef_ref, f32[8,128]{1,0:T(8,128)S(1)} %slice_bitcast_fusion.3.after_ref), custom_call_target="tpu_custom_call" | custom-call | flops 16777216 | bytes 2097152 | tf_op jit(solution)/shard_map/local_adjoint/pallas_call | solution.py:701
  19.4 1.4 %collective-permute-done.2.got_ref = bf16[2,128,128]{2,1,0:T(8,128)(2,1)S(1)} collective-permute-done((bf16[2,128,128]{2,1,0:T(8,128)(2,1)S(1)}, bf16[2,128,128]{2,1,0:T(8,128)(2,1)S(1)}, u32[]{:S(2)}, u32[]{:S(2)}) %collective-permute-start.2) | collective-permute-done | bytes 65568 | tf_op jit(solution)/shard_map/ppermute | solution.py:637
  20.8 0.1 carries.1
  20.9 1.6 %collective-permute-start.4 = (f32[8,128]{1,0:T(8,128)S(1)}, f32[8,128]{1,0:T(8,128)S(1)}, u32[]{:S(2)}, u32[]{:S(2)}) collective-permute-start(f32[8,128]{1,0:T(8,128)S(1)} %get-tuple-element.64.left_ref), channel_id=1, source_target_pairs={{0,1},{1,0},{2,3},{3,2},{4,5},{5,4},{6,7},{7,6},{8,9},{9,8},{10,11... | collective-permute-start | bytes 12296 | tf_op jit(solution)/shard_map/ppermute | solution.py:823
  22.4 0.0 collective-permute-start.3
  22.4 1.2 %own_carries.1 = (f32[1,1024,128]{2,1,0:T(8,128)S(1)}, f32[1,1024,128]{2,1,0:T(8,128)S(1)}) custom-call(f32[2,1024,128]{2,1,0:T(8,128)S(1)} %local_conv.1.conv_ref, f32[2,1024,128]{2,1,0:T(8,128)S(1)} %local_adjoint.1.adj_ref, f32[256,128]{1,0:T(8,128)S(1)} %get-tuple-element.45.decay_ref, f32[256,128]{1,0:T(8,128)S(1)} %get-tuple-element.46.coef_ref, ...), custom_call_target="tpu_custom_call" | custom-call | flops 8388608 | bytes 2097152 | tf_op jit(solution)/shard_map/own_carries/pallas_call | solution.py:743
  23.7 0.0 copy-start
  23.7 0.9 %collective-permute-done.4.right_ref = f32[8,128]{1,0:T(8,128)S(1)} collective-permute-done((f32[8,128]{1,0:T(8,128)S(1)}, f32[8,128]{1,0:T(8,128)S(1)}, u32[]{:S(2)}, u32[]{:S(2)}) %collective-permute-start.4) | collective-permute-done | bytes 4128 | tf_op jit(solution)/shard_map/ppermute | solution.py:823
  24.6 1.5 %collective-permute-start.5 = (f32[8,128]{1,0:T(8,128)S(1)}, f32[8,128]{1,0:T(8,128)S(1)}, u32[]{:S(2)}, u32[]{:S(2)}) collective-permute-start(f32[8,128]{1,0:T(8,128)S(1)} %square_sum.2.after_ref.left_ref), channel_id=1, source_target_pairs={{0,2},{1,3},{2,0},{3,1},{4,6},{5,7},{6,4},{7,5},{8,10},{9,11},{10,... | collective-permute-start | bytes 12296 | tf_op jit(solution)/shard_map/ppermute | solution.py:823
  26.1 1.3 %forward_outputs.1 = (bf16[128,2048]{1,0:T(8,128)(2,1)S(1)}, bf16[128,2048]{1,0:T(8,128)(2,1)S(1)}, f32[8,128]{1,0:T(8,128)S(1)}) custom-call(bf16[128,2048]{1,0:T(8,128)(2,1)S(1)} %get-tuple-element.41.q_ref.refs_0_, bf16[128,2048]{1,0:T(8,128)(2,1)S(1)} %get-tuple-element.42.k_ref.refs_1_, bf16[128,2048]{1,0:T(8,128)(2,1)S(1)} %get-tuple-element.43.v_ref.refs_2_, ...), custom_call_target="tpu_custom_call" | custom-call | flops 8388608 | bytes 4194304 | tf_op jit(solution)/shard_map/forward_outputs/pallas_call | solution.py:755
  27.4 0.8 %collective-permute-done.5.right_ref = f32[8,128]{1,0:T(8,128)S(1)} collective-permute-done((f32[8,128]{1,0:T(8,128)S(1)}, f32[8,128]{1,0:T(8,128)S(1)}, u32[]{:S(2)}, u32[]{:S(2)}) %collective-permute-start.5) | collective-permute-done | bytes 4128 | tf_op jit(solution)/shard_map/ppermute | solution.py:823
  28.2 1.1 %adjoint_outputs.1 = (bf16[128,2048]{1,0:T(8,128)(2,1)}, bf16[128,2048]{1,0:T(8,128)(2,1)}, f32[2,1024,128]{2,1,0:T(8,128)S(1)}, bf16[64,2048]{1,0:T(8,128)(2,1)...) custom-call(bf16[128,2048]{1,0:T(8,128)(2,1)S(1)} %get-tuple-element.41.q_ref.refs_0_, ...), custom_call_target="tpu_custom_call" | custom-call | flops 8388608 | bytes 2097152 | tf_op jit(solution)/shard_map/adjoint_outputs/pallas_call | solution.py:782
  29.3 0.1 collective-permute-done.6.refs_13_
  29.3 1.3 %last_outputs.1 = (f32[16,2048]{1,0:T(8,128)}, bf16[128,2048]{1,0:T(8,128)(2,1)}, bf16[128,2048]{1,0:T(8,128)(2,1)}) custom-call(bf16[128,2048]{1,0:T(8,128)(2,1)S(1)} %get-tuple-element.41.q_ref.refs_0_, bf16[128,2048]{1,0:T(8,128)(2,1)S(1)} %get-tuple-element.42.k_ref.refs_1_, bf16[128,2048]{1,0:T(8,128)(2,1)S(1)} %get-tuple-element.43.v_ref.refs_2_, ...), custom_call_target="tpu_custom_call" | custom-call | flops 4194304 | bytes 2097152 | tf_op jit(solution)/shard_map/last_outputs/pallas_call | solution.py:835
  (11 shorter events, 0.0 us)
Async XLA Ops:
  4.9 3.1 %collective-permute-start = (f32[3,128,128]{2,1,0:T(8,128)S(1)}, f32[3,128,128]{2,1,0:T(8,128)S(1)}, u32[]{:S(2)}, u32[]{:S(2)}) collective-permute-start(f32[3,128,128]{2,1,0:T(8,128)S(1)} %get-tuple-element.51), channel_id=1, source_target_pairs={{0,4},{4,0},{8,12},{12,8},{16,20},{20,16},{24,28},{28,24},{1,5},{5... | collective-permute-start | bytes 589832 | tf_op jit(solution)/shard_map/ppermute | solution.py:637
  8.0 6.1 %collective-permute-start.1 = (bf16[3,128,128]{2,1,0:T(8,128)(2,1)S(1)}, bf16[3,128,128]{2,1,0:T(8,128)(2,1)S(1)}, u32[]{:S(2)}, u32[]{:S(2)}) collective-permute-start(bf16[3,128,128]{2,1,0:T(8,128)(2,1)S(1)} %get-tuple-element.54), channel_id=1, source_target_pairs={{0,8},{4,12},{8,0},{12,4},{16,24},{20,28},{24,16},{28,20},{1,9},{5... | collective-permute-start | bytes 294920 | tf_op jit(solution)/shard_map/ppermute | solution.py:637
  14.2 6.5 %collective-permute-start.2 = (bf16[2,128,128]{2,1,0:T(8,128)(2,1)S(1)}, bf16[2,128,128]{2,1,0:T(8,128)(2,1)S(1)}, u32[]{:S(2)}, u32[]{:S(2)}) collective-permute-start(bf16[2,128,128]{2,1,0:T(8,128)(2,1)S(1)} %get-tuple-element.57), channel_id=1, source_target_pairs={{0,16},{4,20},{8,24},{12,28},{16,0},{20,4},{24,8},{28,12},{1,17},{... | collective-permute-start | bytes 196616 | tf_op jit(solution)/shard_map/ppermute | solution.py:637
  20.9 3.7 %collective-permute-start.4 = (f32[8,128]{1,0:T(8,128)S(1)}, f32[8,128]{1,0:T(8,128)S(1)}, u32[]{:S(2)}, u32[]{:S(2)}) collective-permute-start(f32[8,128]{1,0:T(8,128)S(1)} %get-tuple-element.64.left_ref), channel_id=1, source_target_pairs={{0,1},{1,0},{2,3},{3,2},{4,5},{5,4},{6,7},{7,6},{8,9},{9,8},{10,11... | collective-permute-start | bytes 12296 | tf_op jit(solution)/shard_map/ppermute | solution.py:823
  22.4 3.6 %collective-permute-start.3 = (f32[384,128]{1,0:T(8,128)S(1)}, f32[384,128]{1,0:T(8,128)S(1)}, u32[]{:S(2)}, u32[]{:S(2)}) collective-permute-start(f32[384,128]{1,0:T(8,128)S(1)} %get-tuple-element.59), channel_id=1, source_target_pairs={{0,4},{4,0},{8,12},{12,8},{16,20},{20,16},{24,28},{28,24},{1,5},{5... | collective-permute-start | bytes 589832 | tf_op jit(solution)/shard_map/ppermute | solution.py:637
  23.7 2.4 %copy-start = (f32[2048]{0:T(1024)S(1)}, f32[2048]{0:T(1024)}, u32[]{:S(2)}) copy-start(f32[2048]{0:T(1024)} %param.12) | copy-start | bytes 24580
  24.6 3.6 %collective-permute-start.5 = (f32[8,128]{1,0:T(8,128)S(1)}, f32[8,128]{1,0:T(8,128)S(1)}, u32[]{:S(2)}, u32[]{:S(2)}) collective-permute-start(f32[8,128]{1,0:T(8,128)S(1)} %square_sum.2.after_ref.left_ref), channel_id=1, source_target_pairs={{0,2},{1,3},{2,0},{3,1},{4,6},{5,7},{6,4},{7,5},{8,10},{9,11},{10,... | collective-permute-start | bytes 12296 | tf_op jit(solution)/shard_map/ppermute | solution.py:823
  28.2 1.2 %collective-permute-start.6 = (f32[8,128]{1,0:T(8,128)S(1)}, f32[8,128]{1,0:T(8,128)S(1)}, u32[]{:S(2)}, u32[]{:S(2)}) collective-permute-start(f32[8,128]{1,0:T(8,128)S(1)} %square_sum.3.after_ref.refs_12_), channel_id=1, source_target_pairs={{0,4},{4,0},{8,12},{12,8},{16,20},{20,16},{24,28},{28,24},{1,5},{5... | collective-permute-start | bytes 12296 | tf_op jit(solution)/shard_map/ppermute | solution.py:637
where the time goes:
time: 30.8 us; the launch traced here: 30.6 us
  Pallas kernels  16.5 us (54%)
  starting transfers between devices  9.09 us (30%)
  waiting for transfers between devices  4.22 us (14%)
  between operations  0.75 us (2%)
    ppermute x5, starting transfers between devices, swap(): return lax.ppermute(value, 'ctx', [(i, i ^ 1 << bit) for i in range(ctx)])  6.02 us
    pallas_call x2, Pallas kernels, local(): pl.pallas_call(partial(local_kernel, reverse, modes), out_shape=whole, co...  4.6 us
    pallas_call x1, Pallas kernels, shards(): pl.pallas_call(send_kernel, in_specs=[HBM] * 6, out_specs=[VMEM] * 12, ou...  4.21 us
    ppermute x2, starting transfers between devices, tp_swap(): return lax.ppermute(value, 'tp', [(i, i ^ 1 << bit) for i in range(tp)])  3.07 us
    ppermute x5, waiting for transfers between devices, swap(): return lax.ppermute(value, 'ctx', [(i, i ^ 1 << bit) for i in range(ctx)])  2.58 us
    pallas_call x1, Pallas kernels, shards(): pl.pallas_call(keep_kernel, out_shape=[rows(3, half)] + [rows(blocks, seq...  2.55 us
    ppermute x2, waiting for transfers between devices, tp_swap(): return lax.ppermute(value, 'tp', [(i, i ^ 1 << bit) for i in range(tp)])  1.64 us
    pallas_call x1, Pallas kernels, forward_outputs(): pl.pallas_call(partial(forward_kernel, modes), out_shape=[line_shape] * 2...  1.28 us
  transfers between devices with their start and end apart: 7, of which 5 were waited for; matrix products, arithmetic and copies ran while one was open for 0% of the time, Pallas kernels for 35%

commit v1 on v0

--- a/solution.py
+++ b/solution.py
@@ -602,8 +602,8 @@
         copy.wait()
 
 
-def add_kernel(left_ref, right_ref, after_ref, out_ref):
-    out_ref[...] = left_ref[...] + right_ref[...]
+def add_kernel(after_ref, *refs):
+    refs[-1][...] = tree_sum([ref[...] for ref in refs[:-1]])
 
 
 def clip(limit, blocks, mine_ref, other_ref, share_refs, out_ref, states):
@@ -810,26 +810,29 @@
         kept["final"] = results[:-1]
         return results[-1]
 
-    def plus(left, right, after):
+    def plus(after, *shares):
         return pl.pallas_call(
             add_kernel,
-            in_specs=[VMEM] * 3,
+            in_specs=[VMEM] * (1 + len(shares)),
             out_shape=rows(8),
             compiler_params=KERNEL,
             name="square_sum",
-        )(left, right, after)
-
-    def tp_swap(value, bit):
-        return lax.ppermute(value, "tp", [(i, i ^ (1 << bit)) for i in range(tp)])
-
-    works = [add_own, forward_outputs, adjoint_outputs]
-    rounds = [partial(tp_swap, bit=bit) for bit in range(tp.bit_length() - 1)]
-    for at, exchange in enumerate(rounds + [partial(swap, bit=0)]):
-        if at > 0:
-            square = plus(square, share, after)
-        share = exchange(square)
-        after = works.pop(0)(square) if works else square
-    for work in works:
+        )(after, *shares)
+
+    def tp_swap(value, mask):
+        return lax.ppermute(value, "tp", [(i, i ^ mask) for i in range(tp)])
+
+    works = [add_own, forward_outputs]
+    for bit in range(0, tp.bit_length() - 1, 2):
+        masks = [m << bit for m in (1, 2, 3) if m << bit < tp]
+        shares = [tp_swap(square, mask) for mask in masks]
+        after = square
+        while works:
+            after = works.pop(0)(after)
+        square = plus(after, square, *shares)
+    share = swap(square, 0)
+    after = square
+    for work in works + [adjoint_outputs]:
         after = work(after)
     operator_out, grad_queries, scanned, early_keys, early_values = kept["final"]
     grad_residues, grad_keys, grad_values = pl.pallas_call(

time: 30.8 us -> 30.8 us (level)
  waiting for transfers between devices: 4.22 us -> 2.68 us
  starting transfers between devices: 9.09 us -> 10.1 us
  local copies, waits for them, and re-layouts: 0.02 us -> 0.52 us
    ppermute x2 -> x3, waiting for transfers between devices: 1.64 us -> 0.01 us  [tp_swap(): return lax.ppermute(value, 'tp', [(i, i ^ mask) for i in range(tp)])]
    ppermute x5, starting transfers between devices: 6.02 us -> 6.59 us  [swap(): return lax.ppermute(value, 'ctx', [(i, i ^ 1 << bit) for i in range(ctx)])]
    unnamed x2, local copies, waits for them, and re-layouts: 0.01 us -> 0.5 us
    ppermute x2 -> x3, starting transfers between devices: 3.07 us -> 3.55 us  [tp_swap(): return lax.ppermute(value, 'tp', [(i, i ^ mask) for i in range(tp)])]
  transfers between devices with their start and end apart: 7 -> 8, of which waited for: 5 -> 3; matrix products, arithmetic and copies ran while one was open for 0% -> 0% of each run, Pallas kernels for 35% -> 35%
where the time goes in v1:
time: 30.8 us; the launch traced here: 30.6 us
  Pallas kernels  16.5 us (54%)
  starting transfers between devices  10.1 us (33%)
  waiting for transfers between devices  2.68 us (9%)
  between operations  0.79 us (3%)
  local copies, waits for them, and re-layouts  0.52 us (2%)
    ppermute x5, starting transfers between devices, swap(): return lax.ppermute(value, 'ctx', [(i, i ^ 1 << bit) for i in range(ctx)])  6.59 us
    pallas_call x2, Pallas kernels, local(): pl.pallas_call(partial(local_kernel, reverse, modes), out_shape=whole, co...  4.6 us
    pallas_call x1, Pallas kernels, shards(): pl.pallas_call(send_kernel, in_specs=[HBM] * 6, out_specs=[VMEM] * 12, ou...  4.21 us
    ppermute x3, starting transfers between devices, tp_swap(): return lax.ppermute(value, 'tp', [(i, i ^ mask) for i in range(tp)])  3.55 us
    ppermute x5, waiting for transfers between devices, swap(): return lax.ppermute(value, 'ctx', [(i, i ^ 1 << bit) for i in range(ctx)])  2.67 us
    pallas_call x1, Pallas kernels, shards(): pl.pallas_call(keep_kernel, out_shape=[rows(3, half)] + [rows(blocks, seq...  2.55 us
    pallas_call x1, Pallas kernels, shards(): pl.pallas_call(partial(last_outputs_kernel, math.sqrt(channels * tp * mod...  1.29 us
    pallas_call x1, Pallas kernels, forward_outputs(): pl.pallas_call(partial(forward_kernel, modes), out_shape=[line_shape] * 2...  1.24 us
  transfers between devices with their start and end apart: 8, of which 3 were waited for; matrix products, arithmetic and copies ran while one was open for 0% of the time, Pallas kernels for 35%

profile of v1, /device:TPU:0, one launch (start us, length us, event | category | flops | bytes accessed | tf_op | source)
XLA Modules:
  0.0 30.6 jit_solution(7416297652268424102)
XLA Ops:
  0.6 4.2 %sent_states.1 = (f32[3,128,128]{2,1,0:T(8,128)S(1)}, bf16[128,2048]{1,0:T(8,128)(2,1)S(1)}, bf16[128,2048]{1,0:T(8,128)(2,1)S(1)}, bf16[128,2048]{1,0:T(8,128)(...) custom-call(bf16[128,2048]{1,0:T(8,128)(2,1)} %q_hbm.1, ...), custom_call_target="tpu_custom_call" | custom-call | flops 12582912 | bytes 2097152 | tf_op jit(solution)/shard_map/sent_states/pallas_call | solution.py:662
  4.9 0.5 %collective-permute-start = (f32[3,128,128]{2,1,0:T(8,128)S(1)}, f32[3,128,128]{2,1,0:T(8,128)S(1)}, u32[]{:S(2)}, u32[]{:S(2)}) collective-permute-start(f32[3,128,128]{2,1,0:T(8,128)S(1)} %get-tuple-element.51), channel_id=1, source_target_pairs={{0,4},{4,0},{8,12},{12,8},{16,20},{20,16},{24,28},{28,24},{1,5},{5... | collective-permute-start | bytes 589832 | tf_op jit(solution)/shard_map/ppermute | solution.py:637
  5.4 2.6 %kept_states.1 = (f32[3,128,128]{2,1,0:T(8,128)S(1)}, f32[2,1024,128]{2,1,0:T(8,128)S(1)}, f32[2,1024,128]{2,1,0:T(8,128)S(1)}) custom-call(bf16[128,2048]{1,0:T(8,128)(2,1)S(1)} %get-tuple-element.41.q_ref.refs_0_, bf16[128,2048]{1,0:T(8,128)(2,1)S(1)} %get-tuple-element.42.k_ref.refs_1_, bf16[128,2048]{1,0:T(8,128)(2,1)S(1)} %get-tuple-element.43.v_ref.refs_2_, ...), custom_call_target="tpu_custom_call" | custom-call | flops 12582912 | bytes 2097152 | tf_op jit(solution)/shard_map/kept_states/pallas_call | solution.py:683
  7.9 0.0 collective-permute-done.got_ref.sibling_ref
  7.9 0.1 chip_states.1
  8.0 2.7 %collective-permute-start.1 = (bf16[3,128,128]{2,1,0:T(8,128)(2,1)S(1)}, bf16[3,128,128]{2,1,0:T(8,128)(2,1)S(1)}, u32[]{:S(2)}, u32[]{:S(2)}) collective-permute-start(bf16[3,128,128]{2,1,0:T(8,128)(2,1)S(1)} %get-tuple-element.54), channel_id=1, source_target_pairs={{0,8},{4,12},{8,0},{12,4},{16,24},{20,28},{24,16},{28,20},{1,9},{5... | collective-permute-start | bytes 294920 | tf_op jit(solution)/shard_map/ppermute | solution.py:637
  10.7 2.3 %local_conv.1.conv_ref = f32[2,1024,128]{2,1,0:T(8,128)S(1)} custom-call(f32[2,1024,128]{2,1,0:T(8,128)S(1)} %get-tuple-element.55.lines_ref, f32[256,128]{1,0:T(8,128)S(1)} %get-tuple-element.45.decay_ref, f32[256,128]{1,0:T(8,128)S(1)} %get-tuple-element.46.coef_ref, f32[8,128]{1,0:T(8,128)S(1)} %slice_bitcast_fusion.4.after_ref), custom_call_target="tpu_custom_call" | custom-call | flops 16777216 | bytes 2097152 | tf_op jit(solution)/shard_map/local_conv/pallas_call | solution.py:701
  13.0 1.1 %collective-permute-done.1.got_ref = bf16[3,128,128]{2,1,0:T(8,128)(2,1)S(1)} collective-permute-done((bf16[3,128,128]{2,1,0:T(8,128)(2,1)S(1)}, bf16[3,128,128]{2,1,0:T(8,128)(2,1)S(1)}, u32[]{:S(2)}, u32[]{:S(2)}) %collective-permute-start.1) | collective-permute-done | bytes 98336 | tf_op jit(solution)/shard_map/ppermute | solution.py:637
  14.1 0.1 block_states.1
  14.2 2.8 %collective-permute-start.2 = (bf16[2,128,128]{2,1,0:T(8,128)(2,1)S(1)}, bf16[2,128,128]{2,1,0:T(8,128)(2,1)S(1)}, u32[]{:S(2)}, u32[]{:S(2)}) collective-permute-start(bf16[2,128,128]{2,1,0:T(8,128)(2,1)S(1)} %get-tuple-element.57), channel_id=1, source_target_pairs={{0,16},{4,20},{8,24},{12,28},{16,0},{20,4},{24,8},{28,12},{1,17},{... | collective-permute-start | bytes 196616 | tf_op jit(solution)/shard_map/ppermute | solution.py:637
  17.1 2.3 %local_adjoint.1.adj_ref = f32[2,1024,128]{2,1,0:T(8,128)S(1)} custom-call(f32[2,1024,128]{2,1,0:T(8,128)S(1)} %get-tuple-element.58.lines_ref, f32[256,128]{1,0:T(8,128)S(1)} %get-tuple-element.45.decay_ref, f32[256,128]{1,0:T(8,128)S(1)} %get-tuple-element.46.coef_ref, f32[8,128]{1,0:T(8,128)S(1)} %slice_bitcast_fusion.3.after_ref), custom_call_target="tpu_custom_call" | custom-call | flops 16777216 | bytes 2097152 | tf_op jit(solution)/shard_map/local_adjoint/pallas_call | solution.py:701
  19.4 1.4 %collective-permute-done.2.got_ref = bf16[2,128,128]{2,1,0:T(8,128)(2,1)S(1)} collective-permute-done((bf16[2,128,128]{2,1,0:T(8,128)(2,1)S(1)}, bf16[2,128,128]{2,1,0:T(8,128)(2,1)S(1)}, u32[]{:S(2)}, u32[]{:S(2)}) %collective-permute-start.2) | collective-permute-done | bytes 65568 | tf_op jit(solution)/shard_map/ppermute | solution.py:637
  20.8 0.1 carries.1
  20.9 2.5 %collective-permute-start.6 = (f32[8,128]{1,0:T(8,128)S(1)}, f32[8,128]{1,0:T(8,128)S(1)}, u32[]{:S(2)}, u32[]{:S(2)}) collective-permute-start(f32[8,128]{1,0:T(8,128)S(1)} %get-tuple-element.67.refs_0_), channel_id=1, source_target_pairs={{0,3},{1,2},{2,1},{3,0},{4,7},{5,6},{6,5},{7,4},{8,11},{9,10},{10,... | collective-permute-start | bytes 12296 | tf_op jit(solution)/shard_map/ppermute | solution.py:823
  23.4 0.5 %collective-permute-start.5 = (f32[8,128]{1,0:T(8,128)S(1)}, f32[8,128]{1,0:T(8,128)S(1)}, u32[]{:S(2)}, u32[]{:S(2)}) collective-permute-start(f32[8,128]{1,0:T(8,128)S(1)} %get-tuple-element.67.refs_0_), channel_id=1, source_target_pairs={{0,2},{1,3},{2,0},{3,1},{4,6},{5,7},{6,4},{7,5},{8,10},{9,11},{10,... | collective-permute-start | bytes 12296 | tf_op jit(solution)/shard_map/ppermute | solution.py:823
  23.9 0.5 %collective-permute-start.4 = (f32[8,128]{1,0:T(8,128)S(1)}, f32[8,128]{1,0:T(8,128)S(1)}, u32[]{:S(2)}, u32[]{:S(2)}) collective-permute-start(f32[8,128]{1,0:T(8,128)S(1)} %get-tuple-element.67.refs_0_), channel_id=1, source_target_pairs={{0,1},{1,0},{2,3},{3,2},{4,5},{5,4},{6,7},{7,6},{8,9},{9,8},{10,11... | collective-permute-start | bytes 12296 | tf_op jit(solution)/shard_map/ppermute | solution.py:823
  24.5 1.2 %own_carries.1 = (f32[1,1024,128]{2,1,0:T(8,128)S(1)}, f32[1,1024,128]{2,1,0:T(8,128)S(1)}) custom-call(f32[2,1024,128]{2,1,0:T(8,128)S(1)} %local_conv.1.conv_ref, f32[2,1024,128]{2,1,0:T(8,128)S(1)} %local_adjoint.1.adj_ref, f32[256,128]{1,0:T(8,128)S(1)} %get-tuple-element.45.decay_ref, f32[256,128]{1,0:T(8,128)S(1)} %get-tuple-element.46.coef_ref, ...), custom_call_target="tpu_custom_call" | custom-call | flops 8388608 | bytes 2097152 | tf_op jit(solution)/shard_map/own_carries/pallas_call | solution.py:743
  25.7 0.0 copy-start
  25.7 0.2 collective-permute-done.3.other_ref.refs_9_
  25.9 0.5 %copy-done = f32[2048]{0:T(1024)S(1)} copy-done((f32[2048]{0:T(1024)S(1)}, f32[2048]{0:T(1024)}, u32[]{:S(2)}) %copy-start) | copy-done | bytes 8216
  26.4 1.2 %forward_outputs.1 = (bf16[128,2048]{1,0:T(8,128)(2,1)S(1)}, bf16[128,2048]{1,0:T(8,128)(2,1)S(1)}, f32[8,128]{1,0:T(8,128)S(1)}) custom-call(bf16[128,2048]{1,0:T(8,128)(2,1)S(1)} %get-tuple-element.41.q_ref.refs_0_, bf16[128,2048]{1,0:T(8,128)(2,1)S(1)} %get-tuple-element.42.k_ref.refs_1_, bf16[128,2048]{1,0:T(8,128)(2,1)S(1)} %get-tuple-element.43.v_ref.refs_2_, ...), custom_call_target="tpu_custom_call" | custom-call | flops 8388608 | bytes 4194304 | tf_op jit(solution)/shard_map/forward_outputs/pallas_call | solution.py:755
  27.7 0.6 %collective-permute-start.7 = (f32[8,128]{1,0:T(8,128)S(1)}, f32[8,128]{1,0:T(8,128)S(1)}, u32[]{:S(2)}, u32[]{:S(2)}) collective-permute-start(f32[8,128]{1,0:T(8,128)S(1)} %square_sum.1.after_ref.refs_12_), channel_id=1, source_target_pairs={{0,4},{4,0},{8,12},{12,8},{16,20},{20,16},{24,28},{28,24},{1,5},{5... | collective-permute-start | bytes 12296 | tf_op jit(solution)/shard_map/ppermute | solution.py:637
  28.3 1.1 %adjoint_outputs.1 = (bf16[128,2048]{1,0:T(8,128)(2,1)}, bf16[128,2048]{1,0:T(8,128)(2,1)}, f32[2,1024,128]{2,1,0:T(8,128)S(1)}, bf16[64,2048]{1,0:T(8,128)(2,1)...) custom-call(bf16[128,2048]{1,0:T(8,128)(2,1)S(1)} %get-tuple-element.41.q_ref.refs_0_, ...), custom_call_target="tpu_custom_call" | custom-call | flops 8388608 | bytes 2097152 | tf_op jit(solution)/shard_map/adjoint_outputs/pallas_call | solution.py:782
  29.3 1.3 %last_outputs.1 = (f32[16,2048]{1,0:T(8,128)}, bf16[128,2048]{1,0:T(8,128)(2,1)}, bf16[128,2048]{1,0:T(8,128)(2,1)}) custom-call(bf16[128,2048]{1,0:T(8,128)(2,1)S(1)} %get-tuple-element.41.q_ref.refs_0_, bf16[128,2048]{1,0:T(8,128)(2,1)S(1)} %get-tuple-element.42.k_ref.refs_1_, bf16[128,2048]{1,0:T(8,128)(2,1)S(1)} %get-tuple-element.43.v_ref.refs_2_, ...), custom_call_target="tpu_custom_call" | custom-call | flops 4194304 | bytes 2097152 | tf_op jit(solution)/shard_map/last_outputs/pallas_call | solution.py:838
  (12 shorter events, 0.0 us)
Async XLA Ops:
  4.9 3.1 %collective-permute-start = (f32[3,128,128]{2,1,0:T(8,128)S(1)}, f32[3,128,128]{2,1,0:T(8,128)S(1)}, u32[]{:S(2)}, u32[]{:S(2)}) collective-permute-start(f32[3,128,128]{2,1,0:T(8,128)S(1)} %get-tuple-element.51), channel_id=1, source_target_pairs={{0,4},{4,0},{8,12},{12,8},{16,20},{20,16},{24,28},{28,24},{1,5},{5... | collective-permute-start | bytes 589832 | tf_op jit(solution)/shard_map/ppermute | solution.py:637
  8.0 6.1 %collective-permute-start.1 = (bf16[3,128,128]{2,1,0:T(8,128)(2,1)S(1)}, bf16[3,128,128]{2,1,0:T(8,128)(2,1)S(1)}, u32[]{:S(2)}, u32[]{:S(2)}) collective-permute-start(bf16[3,128,128]{2,1,0:T(8,128)(2,1)S(1)} %get-tuple-element.54), channel_id=1, source_target_pairs={{0,8},{4,12},{8,0},{12,4},{16,24},{20,28},{24,16},{28,20},{1,9},{5... | collective-permute-start | bytes 294920 | tf_op jit(solution)/shard_map/ppermute | solution.py:637
  14.2 6.5 %collective-permute-start.2 = (bf16[2,128,128]{2,1,0:T(8,128)(2,1)S(1)}, bf16[2,128,128]{2,1,0:T(8,128)(2,1)S(1)}, u32[]{:S(2)}, u32[]{:S(2)}) collective-permute-start(bf16[2,128,128]{2,1,0:T(8,128)(2,1)S(1)} %get-tuple-element.57), channel_id=1, source_target_pairs={{0,16},{4,20},{8,24},{12,28},{16,0},{20,4},{24,8},{28,12},{1,17},{... | collective-permute-start | bytes 196616 | tf_op jit(solution)/shard_map/ppermute | solution.py:637
  20.9 6.8 %collective-permute-start.6 = (f32[8,128]{1,0:T(8,128)S(1)}, f32[8,128]{1,0:T(8,128)S(1)}, u32[]{:S(2)}, u32[]{:S(2)}) collective-permute-start(f32[8,128]{1,0:T(8,128)S(1)} %get-tuple-element.67.refs_0_), channel_id=1, source_target_pairs={{0,3},{1,2},{2,1},{3,0},{4,7},{5,6},{6,5},{7,4},{8,11},{9,10},{10,... | collective-permute-start | bytes 12296 | tf_op jit(solution)/shard_map/ppermute | solution.py:823
  23.4 4.3 %collective-permute-start.5 = (f32[8,128]{1,0:T(8,128)S(1)}, f32[8,128]{1,0:T(8,128)S(1)}, u32[]{:S(2)}, u32[]{:S(2)}) collective-permute-start(f32[8,128]{1,0:T(8,128)S(1)} %get-tuple-element.67.refs_0_), channel_id=1, source_target_pairs={{0,2},{1,3},{2,0},{3,1},{4,6},{5,7},{6,4},{7,5},{8,10},{9,11},{10,... | collective-permute-start | bytes 12296 | tf_op jit(solution)/shard_map/ppermute | solution.py:823
  23.9 3.8 %collective-permute-start.4 = (f32[8,128]{1,0:T(8,128)S(1)}, f32[8,128]{1,0:T(8,128)S(1)}, u32[]{:S(2)}, u32[]{:S(2)}) collective-permute-start(f32[8,128]{1,0:T(8,128)S(1)} %get-tuple-element.67.refs_0_), channel_id=1, source_target_pairs={{0,1},{1,0},{2,3},{3,2},{4,5},{5,4},{6,7},{7,6},{8,9},{9,8},{10,11... | collective-permute-start | bytes 12296 | tf_op jit(solution)/shard_map/ppermute | solution.py:823
  24.4 1.4 %collective-permute-start.3 = (f32[384,128]{1,0:T(8,128)S(1)}, f32[384,128]{1,0:T(8,128)S(1)}, u32[]{:S(2)}, u32[]{:S(2)}) collective-permute-start(f32[384,128]{1,0:T(8,128)S(1)} %get-tuple-element.59), channel_id=1, source_target_pairs={{0,4},{4,0},{8,12},{12,8},{16,20},{20,16},{24,28},{28,24},{1,5},{5... | collective-permute-start | bytes 589832 | tf_op jit(solution)/shard_map/ppermute | solution.py:637
  25.7 0.7 %copy-start = (f32[2048]{0:T(1024)S(1)}, f32[2048]{0:T(1024)}, u32[]{:S(2)}) copy-start(f32[2048]{0:T(1024)} %param.12) | copy-start | bytes 24580
  27.7 1.6 %collective-permute-start.7 = (f32[8,128]{1,0:T(8,128)S(1)}, f32[8,128]{1,0:T(8,128)S(1)}, u32[]{:S(2)}, u32[]{:S(2)}) collective-permute-start(f32[8,128]{1,0:T(8,128)S(1)} %square_sum.1.after_ref.refs_12_), channel_id=1, source_target_pairs={{0,4},{4,0},{8,12},{12,8},{16,20},{20,16},{24,28},{28,24},{1,5},{5... | collective-permute-start | bytes 12296 | tf_op jit(solution)/shard_map/ppermute | solution.py:637

commit v2 on v1

--- a/solution.py
+++ b/solution.py
@@ -42,6 +42,13 @@
             for i in range(0, len(items), 2)
         ]
     return items[0]
+
+
+def spread(source, target, modes, sub):
+    for group in range(source.shape[1] // LANES):
+        cols = slice(group * LANES, (group + 1) * LANES)
+        first = group // sub * (modes * sub) + group % sub
+        target[pl.ds(first, modes, stride=sub), :] = source[:, cols]
 
 
 def half_units(which, blocks, modes, sub):
@@ -116,6 +123,7 @@
     ct_hbm,
     rate_hbm,
     res_hbm,
+    skip_hbm,
     send_ref,
     q_ref,
     k_ref,
@@ -125,11 +133,11 @@
     pulled_ref,
     rate_ref,
     decay_ref,
-    coef_ref,
     to_scan,
     from_scan,
+    res_cols,
+    skip_ref,
     rate_cols,
-    res_cols,
     sems,
 ):
     seq, channels = q_ref.shape
@@ -147,44 +155,34 @@
         copy.start()
         copies.append(copy)
 
-    start(rate_hbm, rate_cols)
-    start(res_hbm, res_cols)
     width = channels // min(blocks, 2)
     cols = pl.ds(pl.multiple_of(which * width, LANES) if blocks > 1 else 0, width)
     for i in range(parts):
         rows = pl.ds(i * part, part)
         for source, target in pairs:
             start(source.at[rows, cols], target.at[rows, cols])
+    start(rate_hbm, rate_cols)
     if blocks > 1:
         cols = pl.ds(pl.multiple_of((1 - which) * width, LANES), width)
         for source, target in pairs:
             start(source.at[:, cols], target.at[:, cols])
-
-    def spread(source, target):
-        for b in range(blocks):
-            for s in range(sub):
-                cols = slice((b * sub + s) * LANES, (b * sub + s + 1) * LANES)
-                target[pl.ds(b * modes * sub + s, modes, stride=sub), :] = source[:, cols]
-
+    start(res_hbm, res_cols)
+    start(skip_hbm, skip_ref)
     to_scan[...], from_scan[...] = reorder(part * sub, part)
-    copies[0].wait()
-    spread(rate_cols, rate_ref)
-    copies[1].wait()
-    spread(res_cols, coef_ref)
-    rate = rate_ref[...]
-    decay_ref[...] = jnp.exp(-rate)
-    coef_ref[...] = coef_ref[...] * jnp.sqrt(1.0 - jnp.exp(-2.0 * rate))
     units = half_units(which, blocks, modes, sub)
     lines = ((k_ref, v_ref), (ct_ref, q_ref))
     for i in range(parts):
-        for copy in copies[2 + 4 * i : 6 + 4 * i]:
+        for copy in copies[4 * i : 4 * i + 4]:
             copy.wait()
         for unit in units:
             to_scan_order(to_scan, lines, part, i, unit[0], (gated_ref, pulled_ref))
+    copies[4 * parts].wait()
+    spread(rate_cols, rate_ref, modes, sub)
+    decay_ref[...] = jnp.exp(-rate_ref[...])
     for at, unit in enumerate(units):
         at_row = at * unit[2] * sub
         scan_states(unit, sub, gated_ref, pulled_ref, decay_ref, send_ref, at_row)
-    for copy in copies[2 + 4 * parts :]:
+    for copy in copies[4 * parts + 1 :]:
         copy.wait()
 
 
@@ -357,6 +355,13 @@
     return [slice((block * modes + n) * sub, (block * modes + n + 1) * sub) for n in range(modes)]
 
 
+def first_local_kernel(modes, lines_ref, decay_ref, rate_ref, res_cols, after_ref, out_ref, coef_ref):
+    sub = decay_ref.shape[0] // (lines_ref.shape[0] * modes)
+    spread(res_cols, coef_ref, modes, sub)
+    coef_ref[...] = coef_ref[...] * jnp.sqrt(1.0 - jnp.exp(-2.0 * rate_ref[...]))
+    local_kernel(False, modes, lines_ref, decay_ref, coef_ref, after_ref, out_ref)
+
+
 def local_kernel(reverse, modes, lines_ref, decay_ref, coef_ref, after_ref, out_ref):
     blocks = lines_ref.shape[0]
     sub = decay_ref.shape[0] // (blocks * modes)
@@ -644,7 +649,8 @@
     line_scratch = pltpu.VMEM((seq, channels), jnp.bfloat16)
     table_scratch = pltpu.VMEM((modes, channels), F32)
     elements = seq * channels * modes
-    sources = (queries, keys_in, values_in, cotangent, decay_rates.T, residues.T)
+    tables = (decay_rates.T, residues.T, skip_gain.reshape(1, channels))
+    sources = (queries, keys_in, values_in, cotangent, *tables)
 
     (
         send,
@@ -656,23 +662,21 @@
         pulled,
         row_rates,
         row_decay,
-        row_coefs,
         to_scan,
         from_scan,
+        res_cols,
+        skip,
     ) = pl.pallas_call(
         send_kernel,
-        in_specs=[HBM] * 6,
-        out_specs=[VMEM] * 12,
+        in_specs=[HBM] * 7,
+        out_specs=[VMEM] * 13,
         out_shape=[rows(3, half)]
         + [line_shape] * 4
         + [rows(blocks, seq * sub)] * 2
-        + [rows(2 * half)] * 3
-        + [jax.ShapeDtypeStruct((size, size), jnp.bfloat16)] * 2,
-        scratch_shapes=[
-            table_scratch,
-            table_scratch,
-            pltpu.SemaphoreType.DMA((4 * parts + 6,)),
-        ],
+        + [rows(2 * half)] * 2
+        + [jax.ShapeDtypeStruct((size, size), jnp.bfloat16)] * 2
+        + [table_shape, jax.ShapeDtypeStruct((1, channels), F32)],
+        scratch_shapes=[table_scratch, pltpu.SemaphoreType.DMA((4 * parts + 7,))],
         compiler_params=KERNEL,
         cost_estimate=pl.CostEstimate(
             flops=3 * elements, bytes_accessed=8 * seq * channels, transcendentals=0
@@ -697,16 +701,9 @@
     whole = rows(blocks, seq * sub)
     whole_scratch = pltpu.VMEM((blocks, seq * sub, LANES), F32)
     states_scratch = pltpu.VMEM((2 * half, LANES), F32)
-    def local(reverse, after, name):
-        return pl.pallas_call(
-            partial(local_kernel, reverse, modes),
-            out_shape=whole,
-            compiler_params=KERNEL,
-            cost_estimate=pl.CostEstimate(
-                flops=4 * elements, bytes_accessed=8 * seq * channels, transcendentals=0
-            ),
-            name=name,
-        )(pulled if reverse else gated, row_decay, row_coefs, after)
+    local_cost = pl.CostEstimate(
+        flops=4 * elements, bytes_accessed=8 * seq * channels, transcendentals=0
+    )
 
     block, packed = pl.pallas_call(
         partial(pair_kernel, seq, levels == 2),
@@ -715,7 +712,13 @@
         name="chip_states",
     )(keep, sibling, row_rates, row_rates[:8])
     got = swap(packed, 1)
-    conv = local(False, block[4, :8], "local_conv")
+    conv, row_coefs = pl.pallas_call(
+        partial(first_local_kernel, modes),
+        out_shape=[whole, rows(2 * half)],
+        compiler_params=KERNEL,
+        cost_estimate=local_cost,
+        name="local_conv",
+    )(gated, row_decay, row_rates, res_cols, block[4, :8])
     for level in range(1, levels - 1):
         block, packed = pl.pallas_call(
             partial(level_kernel, seq, level, level + 1 == levels - 1),
@@ -724,7 +727,13 @@
             name="block_states",
         )(block, got, row_rates, conv[0, :8])
         got = swap(packed, level + 1)
-    adj = local(True, block[4, :8], "local_adjoint")
+    adj = pl.pallas_call(
+        partial(local_kernel, True, modes),
+        out_shape=whole,
+        compiler_params=KERNEL,
+        cost_estimate=local_cost,
+        name="local_adjoint",
+    )(pulled, row_decay, row_coefs, block[4, :8])
     mine, other, square = pl.pallas_call(
         partial(last_kernel, seq, levels - 1),
         out_shape=[rows(3 * half)] * 2 + [rows(8)],
@@ -732,7 +741,6 @@
         name="carries",
     )(block, got, row_rates, keep, sibling, adj[0, :8])
     other = swap(other, 0)
-    skip = skip_gain.reshape(1, channels)
     early, late = early_parts(seq)
     early_shape = jax.ShapeDtypeStruct((seq * len(early) // parts, channels), jnp.bfloat16)
     late_scratch = pltpu.VMEM((seq * max(len(late), 1) // parts, channels), jnp.bfloat16)

time: 30.8 us -> 30.1 us (0.977)
  local copies, waits for them, and re-layouts: 0.52 us -> 0.01 us
  starting transfers between devices: 10.1 us -> 9.68 us
    unnamed x2 -> x0, local copies, waits for them, and re-layouts: 0.5 us -> none
    ppermute x5, starting transfers between devices: 6.59 us -> 6.13 us  [swap(): return lax.ppermute(value, 'ctx', [(i, i ^ 1 << bit) for i in range(ctx)])]
    ppermute x3, waiting for transfers between devices: 0.01 us -> 0.33 us  [tp_swap(): return lax.ppermute(value, 'tp', [(i, i ^ mask) for i in range(tp)])]
  transfers between devices with their start and end apart: 8 -> 8, of which waited for: 3 -> 4; matrix products, arithmetic and copies ran while one was open for 0% -> 0% of each run, Pallas kernels for 35% -> 36%
where the time goes in v2:
time: 30.1 us; the launch traced here: 30 us
  Pallas kernels  16.6 us (55%)
  starting transfers between devices  9.68 us (32%)
  waiting for transfers between devices  2.93 us (10%)
  between operations  0.77 us (3%)
    ppermute x5, starting transfers between devices, swap(): return lax.ppermute(value, 'ctx', [(i, i ^ 1 << bit) for i in range(ctx)])  6.13 us
    pallas_call x1, Pallas kernels, shards(): pl.pallas_call(send_kernel, in_specs=[HBM] * 7, out_specs=[VMEM] * 13, ou...  4.17 us
    ppermute x3, starting transfers between devices, tp_swap(): return lax.ppermute(value, 'tp', [(i, i ^ mask) for i in range(tp)])  3.55 us
    ppermute x5, waiting for transfers between devices, swap(): return lax.ppermute(value, 'ctx', [(i, i ^ 1 << bit) for i in range(ctx)])  2.6 us
    pallas_call x1, Pallas kernels, shards(): pl.pallas_call(keep_kernel, out_shape=[rows(3, half)] + [rows(blocks, seq...  2.54 us
    pallas_call x1, Pallas kernels, shards(): pl.pallas_call(partial(first_local_kernel, modes), out_shape=[whole, rows...  2.39 us
    pallas_call x1, Pallas kernels, shards(): pl.pallas_call(partial(local_kernel, True, modes), out_shape=whole, compi...  2.3 us
    pallas_call x1, Pallas kernels, shards(): pl.pallas_call(partial(last_outputs_kernel, math.sqrt(channels * tp * mod...  1.29 us
  transfers between devices with their start and end apart: 8, of which 4 were waited for; matrix products, arithmetic and copies ran while one was open for 0% of the time, Pallas kernels for 36%

profile of v2, /device:TPU:0, one launch (start us, length us, event | category | flops | bytes accessed | tf_op | source)
XLA Modules:
  0.0 30.0 jit_solution(1836404271925728405)
XLA Ops:
  0.6 4.2 %sent_states.1 = (f32[3,128,128]{2,1,0:T(8,128)S(1)}, bf16[128,2048]{1,0:T(8,128)(2,1)S(1)}, bf16[128,2048]{1,0:T(8,128)(2,1)S(1)}, bf16[128,2048]{1,0:T(8,128)(...) custom-call(bf16[128,2048]{1,0:T(8,128)(2,1)} %q_hbm.1, ...), custom_call_target="tpu_custom_call" | custom-call | flops 12582912 | bytes 2097152 | tf_op jit(solution)/shard_map/sent_states/pallas_call | solution.py:669
  4.8 0.5 %collective-permute-start = (f32[3,128,128]{2,1,0:T(8,128)S(1)}, f32[3,128,128]{2,1,0:T(8,128)S(1)}, u32[]{:S(2)}, u32[]{:S(2)}) collective-permute-start(f32[3,128,128]{2,1,0:T(8,128)S(1)} %get-tuple-element.56), channel_id=1, source_target_pairs={{0,4},{4,0},{8,12},{12,8},{16,20},{20,16},{24,28},{28,24},{1,5},{5... | collective-permute-start | bytes 589832 | tf_op jit(solution)/shard_map/ppermute | solution.py:642
  5.3 2.5 %kept_states.1 = (f32[3,128,128]{2,1,0:T(8,128)S(1)}, f32[2,1024,128]{2,1,0:T(8,128)S(1)}, f32[2,1024,128]{2,1,0:T(8,128)S(1)}) custom-call(bf16[128,2048]{1,0:T(8,128)(2,1)S(1)} %get-tuple-element.44.q_ref.refs_0_, bf16[128,2048]{1,0:T(8,128)(2,1)S(1)} %get-tuple-element.45.k_ref.refs_1_, bf16[128,2048]{1,0:T(8,128)(2,1)S(1)} %get-tuple-element.46.v_ref.refs_2_, ...), custom_call_target="tpu_custom_call" | custom-call | flops 12582912 | bytes 2097152 | tf_op jit(solution)/shard_map/kept_states/pallas_call | solution.py:687
  7.9 0.0 collective-permute-done.got_ref.sibling_ref
  7.9 0.1 chip_states.1
  8.0 2.7 %collective-permute-start.1 = (bf16[3,128,128]{2,1,0:T(8,128)(2,1)S(1)}, bf16[3,128,128]{2,1,0:T(8,128)(2,1)S(1)}, u32[]{:S(2)}, u32[]{:S(2)}) collective-permute-start(bf16[3,128,128]{2,1,0:T(8,128)(2,1)S(1)} %get-tuple-element.60), channel_id=1, source_target_pairs={{0,8},{4,12},{8,0},{12,4},{16,24},{20,28},{24,16},{28,20},{1,9},{5... | collective-permute-start | bytes 294920 | tf_op jit(solution)/shard_map/ppermute | solution.py:642
  10.7 2.4 %local_conv.1 = (f32[2,1024,128]{2,1,0:T(8,128)S(1)}, f32[256,128]{1,0:T(8,128)S(1)}) custom-call(f32[2,1024,128]{2,1,0:T(8,128)S(1)} %get-tuple-element.52.lines_ref, f32[256,128]{1,0:T(8,128)S(1)} %get-tuple-element.48.decay_ref, f32[256,128]{1,0:T(8,128)S(1)} %get-tuple-element.53.rate_ref, f32[16,2048]{1,0:T(8,128)S(1)} %get-tuple-element.54.res_cols, ...), custom_call_target="tpu_custom_call" | custom-call | flops 16777216 | bytes 2097152 | tf_op jit(solution)/shard_map/local_conv/pallas_call | solution.py:715
  13.1 1.0 %collective-permute-done.1.got_ref = bf16[3,128,128]{2,1,0:T(8,128)(2,1)S(1)} collective-permute-done((bf16[3,128,128]{2,1,0:T(8,128)(2,1)S(1)}, bf16[3,128,128]{2,1,0:T(8,128)(2,1)S(1)}, u32[]{:S(2)}, u32[]{:S(2)}) %collective-permute-start.1) | collective-permute-done | bytes 98336 | tf_op jit(solution)/shard_map/ppermute | solution.py:642
  14.1 0.1 block_states.1
  14.2 2.8 %collective-permute-start.2 = (bf16[2,128,128]{2,1,0:T(8,128)(2,1)S(1)}, bf16[2,128,128]{2,1,0:T(8,128)(2,1)S(1)}, u32[]{:S(2)}, u32[]{:S(2)}) collective-permute-start(bf16[2,128,128]{2,1,0:T(8,128)(2,1)S(1)} %get-tuple-element.63), channel_id=1, source_target_pairs={{0,16},{4,20},{8,24},{12,28},{16,0},{20,4},{24,8},{28,12},{1,17},{... | collective-permute-start | bytes 196616 | tf_op jit(solution)/shard_map/ppermute | solution.py:642
  17.0 2.3 %local_adjoint.1.adj_ref = f32[2,1024,128]{2,1,0:T(8,128)S(1)} custom-call(f32[2,1024,128]{2,1,0:T(8,128)S(1)} %get-tuple-element.64.lines_ref, f32[256,128]{1,0:T(8,128)S(1)} %get-tuple-element.48.decay_ref, f32[256,128]{1,0:T(8,128)S(1)} %get-tuple-element.58.coef_ref, f32[8,128]{1,0:T(8,128)S(1)} %slice_bitcast_fusion.2.after_ref), custom_call_target="tpu_custom_call" | custom-call | flops 16777216 | bytes 2097152 | tf_op jit(solution)/shard_map/local_adjoint/pallas_call | solution.py:730
  19.3 1.4 %collective-permute-done.2.got_ref = bf16[2,128,128]{2,1,0:T(8,128)(2,1)S(1)} collective-permute-done((bf16[2,128,128]{2,1,0:T(8,128)(2,1)S(1)}, bf16[2,128,128]{2,1,0:T(8,128)(2,1)S(1)}, u32[]{:S(2)}, u32[]{:S(2)}) %collective-permute-start.2) | collective-permute-done | bytes 65568 | tf_op jit(solution)/shard_map/ppermute | solution.py:642
  20.7 0.1 carries.1
  20.8 2.5 %collective-permute-start.6 = (f32[8,128]{1,0:T(8,128)S(1)}, f32[8,128]{1,0:T(8,128)S(1)}, u32[]{:S(2)}, u32[]{:S(2)}) collective-permute-start(f32[8,128]{1,0:T(8,128)S(1)} %get-tuple-element.73.refs_0_), channel_id=1, source_target_pairs={{0,3},{1,2},{2,1},{3,0},{4,7},{5,6},{6,5},{7,4},{8,11},{9,10},{10,... | collective-permute-start | bytes 12296 | tf_op jit(solution)/shard_map/ppermute | solution.py:831
  23.4 0.5 %collective-permute-start.5 = (f32[8,128]{1,0:T(8,128)S(1)}, f32[8,128]{1,0:T(8,128)S(1)}, u32[]{:S(2)}, u32[]{:S(2)}) collective-permute-start(f32[8,128]{1,0:T(8,128)S(1)} %get-tuple-element.73.refs_0_), channel_id=1, source_target_pairs={{0,2},{1,3},{2,0},{3,1},{4,6},{5,7},{6,4},{7,5},{8,10},{9,11},{10,... | collective-permute-start | bytes 12296 | tf_op jit(solution)/shard_map/ppermute | solution.py:831
  23.9 0.5 %collective-permute-start.4 = (f32[8,128]{1,0:T(8,128)S(1)}, f32[8,128]{1,0:T(8,128)S(1)}, u32[]{:S(2)}, u32[]{:S(2)}) collective-permute-start(f32[8,128]{1,0:T(8,128)S(1)} %get-tuple-element.73.refs_0_), channel_id=1, source_target_pairs={{0,1},{1,0},{2,3},{3,2},{4,5},{5,4},{6,7},{7,6},{8,9},{9,8},{10,11... | collective-permute-start | bytes 12296 | tf_op jit(solution)/shard_map/ppermute | solution.py:831
  24.4 0.0 collective-permute-start.3
  24.4 1.2 %own_carries.1 = (f32[1,1024,128]{2,1,0:T(8,128)S(1)}, f32[1,1024,128]{2,1,0:T(8,128)S(1)}) custom-call(f32[2,1024,128]{2,1,0:T(8,128)S(1)} %get-tuple-element.61.conv_ref, f32[2,1024,128]{2,1,0:T(8,128)S(1)} %local_adjoint.1.adj_ref, f32[256,128]{1,0:T(8,128)S(1)} %get-tuple-element.48.decay_ref, f32[256,128]{1,0:T(8,128)S(1)} %get-tuple-element.58.coef_ref, ...), custom_call_target="tpu_custom_call" | custom-call | flops 8388608 | bytes 2097152 | tf_op jit(solution)/shard_map/own_carries/pallas_call | solution.py:751
  25.7 0.2 collective-permute-done.3.other_ref.refs_9_
  25.8 1.3 %forward_outputs.1 = (bf16[128,2048]{1,0:T(8,128)(2,1)S(1)}, bf16[128,2048]{1,0:T(8,128)(2,1)S(1)}, f32[8,128]{1,0:T(8,128)S(1)}) custom-call(bf16[128,2048]{1,0:T(8,128)(2,1)S(1)} %get-tuple-element.44.q_ref.refs_0_, bf16[128,2048]{1,0:T(8,128)(2,1)S(1)} %get-tuple-element.45.k_ref.refs_1_, bf16[128,2048]{1,0:T(8,128)(2,1)S(1)} %get-tuple-element.46.v_ref.refs_2_, ...), custom_call_target="tpu_custom_call" | custom-call | flops 8388608 | bytes 4194304 | tf_op jit(solution)/shard_map/forward_outputs/pallas_call | solution.py:763
  27.2 0.3 %collective-permute-done.4.refs_1_ = f32[8,128]{1,0:T(8,128)S(1)} collective-permute-done((f32[8,128]{1,0:T(8,128)S(1)}, f32[8,128]{1,0:T(8,128)S(1)}, u32[]{:S(2)}, u32[]{:S(2)}) %collective-permute-start.4) | collective-permute-done | bytes 4128 | tf_op jit(solution)/shard_map/ppermute | solution.py:831
  27.5 0.1 collective-permute-start.7
  27.6 1.1 %adjoint_outputs.1 = (bf16[128,2048]{1,0:T(8,128)(2,1)}, bf16[128,2048]{1,0:T(8,128)(2,1)}, f32[2,1024,128]{2,1,0:T(8,128)S(1)}, bf16[64,2048]{1,0:T(8,128)(2,1)...) custom-call(bf16[128,2048]{1,0:T(8,128)(2,1)S(1)} %get-tuple-element.44.q_ref.refs_0_, ...), custom_call_target="tpu_custom_call" | custom-call | flops 8388608 | bytes 2097152 | tf_op jit(solution)/shard_map/adjoint_outputs/pallas_call | solution.py:790
  28.7 1.3 %last_outputs.1 = (f32[16,2048]{1,0:T(8,128)}, bf16[128,2048]{1,0:T(8,128)(2,1)}, bf16[128,2048]{1,0:T(8,128)(2,1)}) custom-call(bf16[128,2048]{1,0:T(8,128)(2,1)S(1)} %get-tuple-element.44.q_ref.refs_0_, bf16[128,2048]{1,0:T(8,128)(2,1)S(1)} %get-tuple-element.45.k_ref.refs_1_, bf16[128,2048]{1,0:T(8,128)(2,1)S(1)} %get-tuple-element.46.v_ref.refs_2_, ...), custom_call_target="tpu_custom_call" | custom-call | flops 4194304 | bytes 2097152 | tf_op jit(solution)/shard_map/last_outputs/pallas_call | solution.py:846
  (10 shorter events, 0.0 us)
Async XLA Ops:
  4.8 3.1 %collective-permute-start = (f32[3,128,128]{2,1,0:T(8,128)S(1)}, f32[3,128,128]{2,1,0:T(8,128)S(1)}, u32[]{:S(2)}, u32[]{:S(2)}) collective-permute-start(f32[3,128,128]{2,1,0:T(8,128)S(1)} %get-tuple-element.56), channel_id=1, source_target_pairs={{0,4},{4,0},{8,12},{12,8},{16,20},{20,16},{24,28},{28,24},{1,5},{5... | collective-permute-start | bytes 589832 | tf_op jit(solution)/shard_map/ppermute | solution.py:642
  8.0 6.1 %collective-permute-start.1 = (bf16[3,128,128]{2,1,0:T(8,128)(2,1)S(1)}, bf16[3,128,128]{2,1,0:T(8,128)(2,1)S(1)}, u32[]{:S(2)}, u32[]{:S(2)}) collective-permute-start(bf16[3,128,128]{2,1,0:T(8,128)(2,1)S(1)} %get-tuple-element.60), channel_id=1, source_target_pairs={{0,8},{4,12},{8,0},{12,4},{16,24},{20,28},{24,16},{28,20},{1,9},{5... | collective-permute-start | bytes 294920 | tf_op jit(solution)/shard_map/ppermute | solution.py:642
  14.2 6.5 %collective-permute-start.2 = (bf16[2,128,128]{2,1,0:T(8,128)(2,1)S(1)}, bf16[2,128,128]{2,1,0:T(8,128)(2,1)S(1)}, u32[]{:S(2)}, u32[]{:S(2)}) collective-permute-start(bf16[2,128,128]{2,1,0:T(8,128)(2,1)S(1)} %get-tuple-element.63), channel_id=1, source_target_pairs={{0,16},{4,20},{8,24},{12,28},{16,0},{20,4},{24,8},{28,12},{1,17},{... | collective-permute-start | bytes 196616 | tf_op jit(solution)/shard_map/ppermute | solution.py:642
  20.8 6.3 %collective-permute-start.6 = (f32[8,128]{1,0:T(8,128)S(1)}, f32[8,128]{1,0:T(8,128)S(1)}, u32[]{:S(2)}, u32[]{:S(2)}) collective-permute-start(f32[8,128]{1,0:T(8,128)S(1)} %get-tuple-element.73.refs_0_), channel_id=1, source_target_pairs={{0,3},{1,2},{2,1},{3,0},{4,7},{5,6},{6,5},{7,4},{8,11},{9,10},{10,... | collective-permute-start | bytes 12296 | tf_op jit(solution)/shard_map/ppermute | solution.py:831
  23.4 3.8 %collective-permute-start.5 = (f32[8,128]{1,0:T(8,128)S(1)}, f32[8,128]{1,0:T(8,128)S(1)}, u32[]{:S(2)}, u32[]{:S(2)}) collective-permute-start(f32[8,128]{1,0:T(8,128)S(1)} %get-tuple-element.73.refs_0_), channel_id=1, source_target_pairs={{0,2},{1,3},{2,0},{3,1},{4,6},{5,7},{6,4},{7,5},{8,10},{9,11},{10,... | collective-permute-start | bytes 12296 | tf_op jit(solution)/shard_map/ppermute | solution.py:831
  23.9 3.6 %collective-permute-start.4 = (f32[8,128]{1,0:T(8,128)S(1)}, f32[8,128]{1,0:T(8,128)S(1)}, u32[]{:S(2)}, u32[]{:S(2)}) collective-permute-start(f32[8,128]{1,0:T(8,128)S(1)} %get-tuple-element.73.refs_0_), channel_id=1, source_target_pairs={{0,1},{1,0},{2,3},{3,2},{4,5},{5,4},{6,7},{7,6},{8,9},{9,8},{10,11... | collective-permute-start | bytes 12296 | tf_op jit(solution)/shard_map/ppermute | solution.py:831
  24.4 1.4 %collective-permute-start.3 = (f32[384,128]{1,0:T(8,128)S(1)}, f32[384,128]{1,0:T(8,128)S(1)}, u32[]{:S(2)}, u32[]{:S(2)}) collective-permute-start(f32[384,128]{1,0:T(8,128)S(1)} %get-tuple-element.65), channel_id=1, source_target_pairs={{0,4},{4,0},{8,12},{12,8},{16,20},{20,16},{24,28},{28,24},{1,5},{5... | collective-permute-start | bytes 589832 | tf_op jit(solution)/shard_map/ppermute | solution.py:642
  27.5 1.2 %collective-permute-start.7 = (f32[8,128]{1,0:T(8,128)S(1)}, f32[8,128]{1,0:T(8,128)S(1)}, u32[]{:S(2)}, u32[]{:S(2)}) collective-permute-start(f32[8,128]{1,0:T(8,128)S(1)} %square_sum.1.after_ref.refs_12_), channel_id=1, source_target_pairs={{0,4},{4,0},{8,12},{12,8},{16,20},{20,16},{24,28},{28,24},{1,5},{5... | collective-permute-start | bytes 12296 | tf_op jit(solution)/shard_map/ppermute | solution.py:642

commit v3 on v2

--- a/solution.py
+++ b/solution.py
@@ -12,6 +12,7 @@
 WIRE = jnp.bfloat16
 LANES = 128
 UNROLL = 8
+GROUP = 16
 STEP_ROWS = 32
 KERNEL = pltpu.CompilerParams(vmem_limit_bytes=24 * 1024 * 1024)
 HBM = pl.BlockSpec(memory_space=pltpu.HBM)
@@ -78,7 +79,36 @@
         target[block, i * size : (i + 1) * size, :] = ordered[:, j * LANES : (j + 1) * LANES]
 
 
-def scan_states(unit, sub, gated_ref, pulled_ref, decay_ref, out_ref, at_row):
+def exchange_rows(items):
+    size = len(items)
+    row = lax.broadcasted_iota(jnp.int32, items[0].shape, 0)
+    step = size // 2
+    while step:
+        low = (row & step) == 0
+        for i in range(size):
+            if i & step == 0:
+                first, second = items[i], items[i + step]
+                items[i] = jnp.where(low, first, pltpu.roll(second, step, 0))
+                items[i + step] = jnp.where(low, pltpu.roll(first, size - step, 0), second)
+        step //= 2
+    return items
+
+
+def fill_group(left, right, group, block, target):
+    rows = pl.ds(pl.multiple_of(group * GROUP, GROUP), GROUP)
+    products = []
+    for s in range(8):
+        cols = pl.ds(pl.multiple_of((block * 8 + s) * LANES, LANES), LANES)
+        product = left[rows, cols].astype(F32) * right[rows, cols].astype(F32)
+        products.append(product.astype(jnp.bfloat16).astype(F32))
+    for at in range(0, GROUP, 8):
+        ordered = exchange_rows([product[at : at + 8, :] for product in products])
+        for t in range(8):
+            where = pl.ds(pl.multiple_of((group * GROUP + at + t) * 8, 8), 8)
+            target[block, where, :] = ordered[t]
+
+
+def scan_states(unit, sub, gated_ref, pulled_ref, decay_ref, out_ref, at_row, pairs, waits):
     block, base, modes = unit
     seq = gated_ref.shape[1] // sub
     decay = [
@@ -97,23 +127,44 @@
                 inner[n] = inner[n] + p * held[n]
         return tuple(held), tuple(inner)
 
-    def backward(j, carry):
+    def backward(step, fill, last, j, carry):
         held = list(carry)
-        for u in range(UNROLL):
-            at = pl.ds(pl.multiple_of((seq - 1 - (j * UNROLL + u)) * sub, sub), sub)
+        group = last - j
+        for u in reversed(range(step)):
+            at = pl.ds(pl.multiple_of((group * step + u) * sub, sub), sub)
             p = pulled_ref[block, at, :]
             for n in range(modes):
                 held[n] = decay[n] * held[n] + p
+            if fill and u in (12, 6):
+                left, right, target = pairs[0 if u == 12 else 1]
+                fill_group(left, right, jnp.maximum(group - 1, 0), block, target)
         return tuple(held)
 
+    if pairs is None:
+        last = seq // UNROLL - 1
+        starts = lax.fori_loop(0, last + 1, partial(backward, UNROLL, False, last), first)
+    else:
+        starts = first
+        groups = seq // GROUP // len(waits)
+        waits[-1]()
+        for left, right, target in pairs:
+            fill_group(left, right, seq // GROUP - 1, block, target)
+        for i in reversed(range(len(waits))):
+            if i > 0:
+                waits[i - 1]()
+            last = (i + 1) * groups - 1
+            starts = lax.fori_loop(0, groups, partial(backward, GROUP, True, last), starts)
+    for n in range(modes):
+        out_ref[1, at_row + n * sub : at_row + (n + 1) * sub, :] = starts[n]
     ends, inner = lax.fori_loop(0, seq // UNROLL, forward, (first, first))
     for n in range(modes):
         rows = slice(at_row + n * sub, at_row + (n + 1) * sub)
         out_ref[0, rows, :] = ends[n]
         out_ref[2, rows, :] = inner[n]
-    starts = lax.fori_loop(0, seq // UNROLL, backward, first)
-    for n in range(modes):
-        out_ref[1, at_row + n * sub : at_row + (n + 1) * sub, :] = starts[n]
+
+
+def can_exchange(sub, part, units):
+    return sub == 8 and part % GROUP == 0 and len(units) == 1
 
 
 def send_kernel(
@@ -157,11 +208,11 @@
 
     width = channels // min(blocks, 2)
     cols = pl.ds(pl.multiple_of(which * width, LANES) if blocks > 1 else 0, width)
-    for i in range(parts):
+    start(rate_hbm, rate_cols)
+    for i in reversed(range(parts)):
         rows = pl.ds(i * part, part)
         for source, target in pairs:
             start(source.at[rows, cols], target.at[rows, cols])
-    start(rate_hbm, rate_cols)
     if blocks > 1:
         cols = pl.ds(pl.multiple_of((1 - which) * width, LANES), width)
         for source, target in pairs:
@@ -169,19 +220,30 @@
     start(res_hbm, res_cols)
     start(skip_hbm, skip_ref)
     to_scan[...], from_scan[...] = reorder(part * sub, part)
-    units = half_units(which, blocks, modes, sub)
-    lines = ((k_ref, v_ref), (ct_ref, q_ref))
-    for i in range(parts):
-        for copy in copies[4 * i : 4 * i + 4]:
-            copy.wait()
-        for unit in units:
-            to_scan_order(to_scan, lines, part, i, unit[0], (gated_ref, pulled_ref))
-    copies[4 * parts].wait()
+    copies[0].wait()
     spread(rate_cols, rate_ref, modes, sub)
     decay_ref[...] = jnp.exp(-rate_ref[...])
+    units = half_units(which, blocks, modes, sub)
+
+    def wait_part(i):
+        for copy in copies[4 * (parts - 1 - i) + 1 : 4 * (parts - i) + 1]:
+            copy.wait()
+
+    if can_exchange(sub, part, units):
+        waits = [partial(wait_part, i) for i in range(parts)]
+        lines = ((k_ref, v_ref, gated_ref), (ct_ref, q_ref, pulled_ref))
+    else:
+        waits, lines = None, None
+        for i in reversed(range(parts)):
+            wait_part(i)
+            for unit in units:
+                both = ((k_ref, v_ref), (ct_ref, q_ref))
+                to_scan_order(to_scan, both, part, i, unit[0], (gated_ref, pulled_ref))
     for at, unit in enumerate(units):
         at_row = at * unit[2] * sub
-        scan_states(unit, sub, gated_ref, pulled_ref, decay_ref, send_ref, at_row)
+        scan_states(
+            unit, sub, gated_ref, pulled_ref, decay_ref, send_ref, at_row, lines, waits
+        )
     for copy in copies[4 * parts + 1 :]:
         copy.wait()
 
@@ -215,15 +277,21 @@
     for copy in copies:
         copy.start()
     units = half_units(which, blocks, modes, sub)
-    lines = (gated_in, pulled_in)
+    lines, pairs = (gated_in, pulled_in), None
     if blocks > 1:
         lines = (gated_ref, pulled_ref)
-        for i in range(seq // part):
-            for unit in units:
-                pairs = ((k_ref, v_ref), (ct_ref, q_ref))
-                to_scan_order(to_scan, pairs, part, i, unit[0], lines)
+        if can_exchange(sub, part, units):
+            pairs = ((k_ref, v_ref, gated_ref), (ct_ref, q_ref, pulled_ref))
+        else:
+            for i in range(seq // part):
+                for unit in units:
+                    both = ((k_ref, v_ref), (ct_ref, q_ref))
+                    to_scan_order(to_scan, both, part, i, unit[0], lines)
     for at, unit in enumerate(units):
-        scan_states(unit, sub, *lines, decay_ref, keep_ref, at * unit[2] * sub)
+        at_row = at * unit[2] * sub
+        scan_states(
+            unit, sub, *lines, decay_ref, keep_ref, at_row, pairs, [lambda: None]
+        )
     for copy in copies:
         copy.wait()
 

time: 30.1 us -> 29.5 us (0.980)
  Pallas kernels: 16.6 us -> 15.9 us
    pallas_call x1, Pallas kernels: 4.17 us -> 3.62 us  [shards(): pl.pallas_call(send_kernel, in_specs=[HBM] * 7, out_specs=[VMEM] * 13, ou...]
where the time goes in v3:
time: 29.5 us; the launch traced here: 29.3 us
  Pallas kernels  15.9 us (54%)
  starting transfers between devices  9.68 us (33%)
  waiting for transfers between devices  2.93 us (10%)
  between operations  0.77 us (3%)
    ppermute x5, starting transfers between devices, swap(): return lax.ppermute(value, 'ctx', [(i, i ^ 1 << bit) for i in range(ctx)])  6.12 us
    pallas_call x1, Pallas kernels, shards(): pl.pallas_call(send_kernel, in_specs=[HBM] * 7, out_specs=[VMEM] * 13, ou...  3.62 us
    ppermute x3, starting transfers between devices, tp_swap(): return lax.ppermute(value, 'tp', [(i, i ^ mask) for i in range(tp)])  3.55 us
    ppermute x5, waiting for transfers between devices, swap(): return lax.ppermute(value, 'ctx', [(i, i ^ 1 << bit) for i in range(ctx)])  2.61 us
    pallas_call x1, Pallas kernels, shards(): pl.pallas_call(keep_kernel, out_shape=[rows(3, half)] + [rows(blocks, seq...  2.43 us
    pallas_call x1, Pallas kernels, shards(): pl.pallas_call(partial(first_local_kernel, modes), out_shape=[whole, rows...  2.39 us
    pallas_call x1, Pallas kernels, shards(): pl.pallas_call(partial(local_kernel, True, modes), out_shape=whole, compi...  2.3 us
    pallas_call x1, Pallas kernels, shards(): pl.pallas_call(partial(last_outputs_kernel, math.sqrt(channels * tp * mod...  1.29 us
  transfers between devices with their start and end apart: 8, of which 4 were waited for; matrix products, arithmetic and copies ran while one was open for 0% of the time, Pallas kernels for 36%

profile of v3, /device:TPU:0, one launch (start us, length us, event | category | flops | bytes accessed | tf_op | source)
XLA Modules:
  0.0 29.3 jit_solution(5200784913034767934)
XLA Ops:
  0.6 3.6 %sent_states.1 = (f32[3,128,128]{2,1,0:T(8,128)S(1)}, bf16[128,2048]{1,0:T(8,128)(2,1)S(1)}, bf16[128,2048]{1,0:T(8,128)(2,1)S(1)}, bf16[128,2048]{1,0:T(8,128)(...) custom-call(bf16[128,2048]{1,0:T(8,128)(2,1)} %q_hbm.1, ...), custom_call_target="tpu_custom_call" | custom-call | flops 12582912 | bytes 2097152 | tf_op jit(solution)/shard_map/sent_states/pallas_call | solution.py:737
  4.3 0.5 %collective-permute-start = (f32[3,128,128]{2,1,0:T(8,128)S(1)}, f32[3,128,128]{2,1,0:T(8,128)S(1)}, u32[]{:S(2)}, u32[]{:S(2)}) collective-permute-start(f32[3,128,128]{2,1,0:T(8,128)S(1)} %get-tuple-element.56), channel_id=1, source_target_pairs={{0,4},{4,0},{8,12},{12,8},{16,20},{20,16},{24,28},{28,24},{1,5},{5... | collective-permute-start | bytes 589832 | tf_op jit(solution)/shard_map/ppermute | solution.py:710
  4.8 2.4 %kept_states.1 = (f32[3,128,128]{2,1,0:T(8,128)S(1)}, f32[2,1024,128]{2,1,0:T(8,128)S(1)}, f32[2,1024,128]{2,1,0:T(8,128)S(1)}) custom-call(bf16[128,2048]{1,0:T(8,128)(2,1)S(1)} %get-tuple-element.44.q_ref.refs_0_, bf16[128,2048]{1,0:T(8,128)(2,1)S(1)} %get-tuple-element.45.k_ref.refs_1_, bf16[128,2048]{1,0:T(8,128)(2,1)S(1)} %get-tuple-element.46.v_ref.refs_2_, ...), custom_call_target="tpu_custom_call" | custom-call | flops 12582912 | bytes 2097152 | tf_op jit(solution)/shard_map/kept_states/pallas_call | solution.py:755
  7.2 0.0 collective-permute-done.got_ref.sibling_ref
  7.2 0.1 chip_states.1
  7.3 2.7 %collective-permute-start.1 = (bf16[3,128,128]{2,1,0:T(8,128)(2,1)S(1)}, bf16[3,128,128]{2,1,0:T(8,128)(2,1)S(1)}, u32[]{:S(2)}, u32[]{:S(2)}) collective-permute-start(bf16[3,128,128]{2,1,0:T(8,128)(2,1)S(1)} %get-tuple-element.60), channel_id=1, source_target_pairs={{0,8},{4,12},{8,0},{12,4},{16,24},{20,28},{24,16},{28,20},{1,9},{5... | collective-permute-start | bytes 294920 | tf_op jit(solution)/shard_map/ppermute | solution.py:710
  10.0 2.4 %local_conv.1 = (f32[2,1024,128]{2,1,0:T(8,128)S(1)}, f32[256,128]{1,0:T(8,128)S(1)}) custom-call(f32[2,1024,128]{2,1,0:T(8,128)S(1)} %get-tuple-element.52.lines_ref, f32[256,128]{1,0:T(8,128)S(1)} %get-tuple-element.48.decay_ref, f32[256,128]{1,0:T(8,128)S(1)} %get-tuple-element.53.rate_ref, f32[16,2048]{1,0:T(8,128)S(1)} %get-tuple-element.54.res_cols, ...), custom_call_target="tpu_custom_call" | custom-call | flops 16777216 | bytes 2097152 | tf_op jit(solution)/shard_map/local_conv/pallas_call | solution.py:783
  12.4 1.0 %collective-permute-done.1.got_ref = bf16[3,128,128]{2,1,0:T(8,128)(2,1)S(1)} collective-permute-done((bf16[3,128,128]{2,1,0:T(8,128)(2,1)S(1)}, bf16[3,128,128]{2,1,0:T(8,128)(2,1)S(1)}, u32[]{:S(2)}, u32[]{:S(2)}) %collective-permute-start.1) | collective-permute-done | bytes 98336 | tf_op jit(solution)/shard_map/ppermute | solution.py:710
  13.4 0.1 block_states.1
  13.5 2.8 %collective-permute-start.2 = (bf16[2,128,128]{2,1,0:T(8,128)(2,1)S(1)}, bf16[2,128,128]{2,1,0:T(8,128)(2,1)S(1)}, u32[]{:S(2)}, u32[]{:S(2)}) collective-permute-start(bf16[2,128,128]{2,1,0:T(8,128)(2,1)S(1)} %get-tuple-element.63), channel_id=1, source_target_pairs={{0,16},{4,20},{8,24},{12,28},{16,0},{20,4},{24,8},{28,12},{1,17},{... | collective-permute-start | bytes 196616 | tf_op jit(solution)/shard_map/ppermute | solution.py:710
  16.4 2.3 %local_adjoint.1.adj_ref = f32[2,1024,128]{2,1,0:T(8,128)S(1)} custom-call(f32[2,1024,128]{2,1,0:T(8,128)S(1)} %get-tuple-element.64.lines_ref, f32[256,128]{1,0:T(8,128)S(1)} %get-tuple-element.48.decay_ref, f32[256,128]{1,0:T(8,128)S(1)} %get-tuple-element.58.coef_ref, f32[8,128]{1,0:T(8,128)S(1)} %slice_bitcast_fusion.2.after_ref), custom_call_target="tpu_custom_call" | custom-call | flops 16777216 | bytes 2097152 | tf_op jit(solution)/shard_map/local_adjoint/pallas_call | solution.py:798
  18.7 1.4 %collective-permute-done.2.got_ref = bf16[2,128,128]{2,1,0:T(8,128)(2,1)S(1)} collective-permute-done((bf16[2,128,128]{2,1,0:T(8,128)(2,1)S(1)}, bf16[2,128,128]{2,1,0:T(8,128)(2,1)S(1)}, u32[]{:S(2)}, u32[]{:S(2)}) %collective-permute-start.2) | collective-permute-done | bytes 65568 | tf_op jit(solution)/shard_map/ppermute | solution.py:710
  20.1 0.1 carries.1
  20.2 2.5 %collective-permute-start.6 = (f32[8,128]{1,0:T(8,128)S(1)}, f32[8,128]{1,0:T(8,128)S(1)}, u32[]{:S(2)}, u32[]{:S(2)}) collective-permute-start(f32[8,128]{1,0:T(8,128)S(1)} %get-tuple-element.73.refs_0_), channel_id=1, source_target_pairs={{0,3},{1,2},{2,1},{3,0},{4,7},{5,6},{6,5},{7,4},{8,11},{9,10},{10,... | collective-permute-start | bytes 12296 | tf_op jit(solution)/shard_map/ppermute | solution.py:899
  22.7 0.5 %collective-permute-start.5 = (f32[8,128]{1,0:T(8,128)S(1)}, f32[8,128]{1,0:T(8,128)S(1)}, u32[]{:S(2)}, u32[]{:S(2)}) collective-permute-start(f32[8,128]{1,0:T(8,128)S(1)} %get-tuple-element.73.refs_0_), channel_id=1, source_target_pairs={{0,2},{1,3},{2,0},{3,1},{4,6},{5,7},{6,4},{7,5},{8,10},{9,11},{10,... | collective-permute-start | bytes 12296 | tf_op jit(solution)/shard_map/ppermute | solution.py:899
  23.2 0.5 %collective-permute-start.4 = (f32[8,128]{1,0:T(8,128)S(1)}, f32[8,128]{1,0:T(8,128)S(1)}, u32[]{:S(2)}, u32[]{:S(2)}) collective-permute-start(f32[8,128]{1,0:T(8,128)S(1)} %get-tuple-element.73.refs_0_), channel_id=1, source_target_pairs={{0,1},{1,0},{2,3},{3,2},{4,5},{5,4},{6,7},{7,6},{8,9},{9,8},{10,11... | collective-permute-start | bytes 12296 | tf_op jit(solution)/shard_map/ppermute | solution.py:899
  23.7 0.0 collective-permute-start.3
  23.7 1.2 %own_carries.1 = (f32[1,1024,128]{2,1,0:T(8,128)S(1)}, f32[1,1024,128]{2,1,0:T(8,128)S(1)}) custom-call(f32[2,1024,128]{2,1,0:T(8,128)S(1)} %get-tuple-element.61.conv_ref, f32[2,1024,128]{2,1,0:T(8,128)S(1)} %local_adjoint.1.adj_ref, f32[256,128]{1,0:T(8,128)S(1)} %get-tuple-element.48.decay_ref, f32[256,128]{1,0:T(8,128)S(1)} %get-tuple-element.58.coef_ref, ...), custom_call_target="tpu_custom_call" | custom-call | flops 8388608 | bytes 2097152 | tf_op jit(solution)/shard_map/own_carries/pallas_call | solution.py:819
  25.0 0.2 collective-permute-done.3.other_ref.refs_9_
  25.2 1.3 %forward_outputs.1 = (bf16[128,2048]{1,0:T(8,128)(2,1)S(1)}, bf16[128,2048]{1,0:T(8,128)(2,1)S(1)}, f32[8,128]{1,0:T(8,128)S(1)}) custom-call(bf16[128,2048]{1,0:T(8,128)(2,1)S(1)} %get-tuple-element.44.q_ref.refs_0_, bf16[128,2048]{1,0:T(8,128)(2,1)S(1)} %get-tuple-element.45.k_ref.refs_1_, bf16[128,2048]{1,0:T(8,128)(2,1)S(1)} %get-tuple-element.46.v_ref.refs_2_, ...), custom_call_target="tpu_custom_call" | custom-call | flops 8388608 | bytes 4194304 | tf_op jit(solution)/shard_map/forward_outputs/pallas_call | solution.py:831
  26.5 0.3 %collective-permute-done.4.refs_1_ = f32[8,128]{1,0:T(8,128)S(1)} collective-permute-done((f32[8,128]{1,0:T(8,128)S(1)}, f32[8,128]{1,0:T(8,128)S(1)}, u32[]{:S(2)}, u32[]{:S(2)}) %collective-permute-start.4) | collective-permute-done | bytes 4128 | tf_op jit(solution)/shard_map/ppermute | solution.py:899
  26.8 0.1 collective-permute-start.7
  26.9 1.1 %adjoint_outputs.1 = (bf16[128,2048]{1,0:T(8,128)(2,1)}, bf16[128,2048]{1,0:T(8,128)(2,1)}, f32[2,1024,128]{2,1,0:T(8,128)S(1)}, bf16[64,2048]{1,0:T(8,128)(2,1)...) custom-call(bf16[128,2048]{1,0:T(8,128)(2,1)S(1)} %get-tuple-element.44.q_ref.refs_0_, ...), custom_call_target="tpu_custom_call" | custom-call | flops 8388608 | bytes 2097152 | tf_op jit(solution)/shard_map/adjoint_outputs/pallas_call | solution.py:858
  28.0 1.3 %last_outputs.1 = (f32[16,2048]{1,0:T(8,128)}, bf16[128,2048]{1,0:T(8,128)(2,1)}, bf16[128,2048]{1,0:T(8,128)(2,1)}) custom-call(bf16[128,2048]{1,0:T(8,128)(2,1)S(1)} %get-tuple-element.44.q_ref.refs_0_, bf16[128,2048]{1,0:T(8,128)(2,1)S(1)} %get-tuple-element.45.k_ref.refs_1_, bf16[128,2048]{1,0:T(8,128)(2,1)S(1)} %get-tuple-element.46.v_ref.refs_2_, ...), custom_call_target="tpu_custom_call" | custom-call | flops 4194304 | bytes 2097152 | tf_op jit(solution)/shard_map/last_outputs/pallas_call | solution.py:914
  (10 shorter events, 0.0 us)
Async XLA Ops:
  4.3 3.0 %collective-permute-start = (f32[3,128,128]{2,1,0:T(8,128)S(1)}, f32[3,128,128]{2,1,0:T(8,128)S(1)}, u32[]{:S(2)}, u32[]{:S(2)}) collective-permute-start(f32[3,128,128]{2,1,0:T(8,128)S(1)} %get-tuple-element.56), channel_id=1, source_target_pairs={{0,4},{4,0},{8,12},{12,8},{16,20},{20,16},{24,28},{28,24},{1,5},{5... | collective-permute-start | bytes 589832 | tf_op jit(solution)/shard_map/ppermute | solution.py:710
  7.3 6.1 %collective-permute-start.1 = (bf16[3,128,128]{2,1,0:T(8,128)(2,1)S(1)}, bf16[3,128,128]{2,1,0:T(8,128)(2,1)S(1)}, u32[]{:S(2)}, u32[]{:S(2)}) collective-permute-start(bf16[3,128,128]{2,1,0:T(8,128)(2,1)S(1)} %get-tuple-element.60), channel_id=1, source_target_pairs={{0,8},{4,12},{8,0},{12,4},{16,24},{20,28},{24,16},{28,20},{1,9},{5... | collective-permute-start | bytes 294920 | tf_op jit(solution)/shard_map/ppermute | solution.py:710
  13.5 6.5 %collective-permute-start.2 = (bf16[2,128,128]{2,1,0:T(8,128)(2,1)S(1)}, bf16[2,128,128]{2,1,0:T(8,128)(2,1)S(1)}, u32[]{:S(2)}, u32[]{:S(2)}) collective-permute-start(bf16[2,128,128]{2,1,0:T(8,128)(2,1)S(1)} %get-tuple-element.63), channel_id=1, source_target_pairs={{0,16},{4,20},{8,24},{12,28},{16,0},{20,4},{24,8},{28,12},{1,17},{... | collective-permute-start | bytes 196616 | tf_op jit(solution)/shard_map/ppermute | solution.py:710
  20.2 6.3 %collective-permute-start.6 = (f32[8,128]{1,0:T(8,128)S(1)}, f32[8,128]{1,0:T(8,128)S(1)}, u32[]{:S(2)}, u32[]{:S(2)}) collective-permute-start(f32[8,128]{1,0:T(8,128)S(1)} %get-tuple-element.73.refs_0_), channel_id=1, source_target_pairs={{0,3},{1,2},{2,1},{3,0},{4,7},{5,6},{6,5},{7,4},{8,11},{9,10},{10,... | collective-permute-start | bytes 12296 | tf_op jit(solution)/shard_map/ppermute | solution.py:899
  22.7 3.8 %collective-permute-start.5 = (f32[8,128]{1,0:T(8,128)S(1)}, f32[8,128]{1,0:T(8,128)S(1)}, u32[]{:S(2)}, u32[]{:S(2)}) collective-permute-start(f32[8,128]{1,0:T(8,128)S(1)} %get-tuple-element.73.refs_0_), channel_id=1, source_target_pairs={{0,2},{1,3},{2,0},{3,1},{4,6},{5,7},{6,4},{7,5},{8,10},{9,11},{10,... | collective-permute-start | bytes 12296 | tf_op jit(solution)/shard_map/ppermute | solution.py:899
  23.2 3.6 %collective-permute-start.4 = (f32[8,128]{1,0:T(8,128)S(1)}, f32[8,128]{1,0:T(8,128)S(1)}, u32[]{:S(2)}, u32[]{:S(2)}) collective-permute-start(f32[8,128]{1,0:T(8,128)S(1)} %get-tuple-element.73.refs_0_), channel_id=1, source_target_pairs={{0,1},{1,0},{2,3},{3,2},{4,5},{5,4},{6,7},{7,6},{8,9},{9,8},{10,11... | collective-permute-start | bytes 12296 | tf_op jit(solution)/shard_map/ppermute | solution.py:899
  23.7 1.4 %collective-permute-start.3 = (f32[384,128]{1,0:T(8,128)S(1)}, f32[384,128]{1,0:T(8,128)S(1)}, u32[]{:S(2)}, u32[]{:S(2)}) collective-permute-start(f32[384,128]{1,0:T(8,128)S(1)} %get-tuple-element.65), channel_id=1, source_target_pairs={{0,4},{4,0},{8,12},{12,8},{16,20},{20,16},{24,28},{28,24},{1,5},{5... | collective-permute-start | bytes 589832 | tf_op jit(solution)/shard_map/ppermute | solution.py:710
  26.8 1.2 %collective-permute-start.7 = (f32[8,128]{1,0:T(8,128)S(1)}, f32[8,128]{1,0:T(8,128)S(1)}, u32[]{:S(2)}, u32[]{:S(2)}) collective-permute-start(f32[8,128]{1,0:T(8,128)S(1)} %square_sum.1.after_ref.refs_12_), channel_id=1, source_target_pairs={{0,4},{4,0},{8,12},{12,8},{16,20},{20,16},{24,28},{28,24},{1,5},{5... | collective-permute-start | bytes 12296 | tf_op jit(solution)/shard_map/ppermute | solution.py:710

commit v4 on v3

--- a/solution.py
+++ b/solution.py
@@ -61,7 +61,7 @@
     ]
 
 
-def to_scan_order(to_scan, pairs, part, i, block, targets):
+def to_scan_order(to_scan, pairs, part, i, block, targets, slot):
     size, sub = to_scan.shape[0], to_scan.shape[0] // part
     rows = slice(i * part, (i + 1) * part)
     sides = []
@@ -76,7 +76,7 @@
         to_scan[...], jnp.concatenate(sides, axis=1), preferred_element_type=F32
     )
     for j, target in enumerate(targets):
-        target[block, i * size : (i + 1) * size, :] = ordered[:, j * LANES : (j + 1) * LANES]
+        target[slot, i * size : (i + 1) * size, :] = ordered[:, j * LANES : (j + 1) * LANES]
 
 
 def exchange_rows(items):
@@ -94,7 +94,7 @@
     return items
 
 
-def fill_group(left, right, group, block, target):
+def fill_group(left, right, group, block, target, slot):
     rows = pl.ds(pl.multiple_of(group * GROUP, GROUP), GROUP)
     products = []
     for s in range(8):
@@ -105,12 +105,14 @@
         ordered = exchange_rows([product[at : at + 8, :] for product in products])
         for t in range(8):
             where = pl.ds(pl.multiple_of((group * GROUP + at + t) * 8, 8), 8)
-            target[block, where, :] = ordered[t]
-
-
-def scan_states(unit, sub, gated_ref, pulled_ref, decay_ref, out_ref, at_row, pairs, waits):
+            target[slot, where, :] = ordered[t]
+
+
+def scan_states(unit, slot, sub, gated_ref, pulled_ref, decay_ref, out_ref, pairs, waits):
     block, base, modes = unit
+    at_row = slot * modes * sub
     seq = gated_ref.shape[1] // sub
+    slot = slot % gated_ref.shape[0]
     decay = [
         decay_ref[pl.ds(pl.multiple_of(base + n * sub, sub), sub), :] for n in range(modes)
     ]
@@ -120,8 +122,8 @@
         held, inner = list(carry[0]), list(carry[1])
         for u in range(UNROLL):
             at = pl.ds(pl.multiple_of((j * UNROLL + u) * sub, sub), sub)
-            x = gated_ref[block, at, :]
-            p = pulled_ref[block, at, :]
+            x = gated_ref[slot, at, :]
+            p = pulled_ref[slot, at, :]
             for n in range(modes):
                 held[n] = decay[n] * held[n] + x
                 inner[n] = inner[n] + p * held[n]
@@ -132,12 +134,12 @@
         group = last - j
         for u in reversed(range(step)):
             at = pl.ds(pl.multiple_of((group * step + u) * sub, sub), sub)
-            p = pulled_ref[block, at, :]
+            p = pulled_ref[slot, at, :]
             for n in range(modes):
                 held[n] = decay[n] * held[n] + p
             if fill and u in (12, 6):
                 left, right, target = pairs[0 if u == 12 else 1]
-                fill_group(left, right, jnp.maximum(group - 1, 0), block, target)
+                fill_group(left, right, jnp.maximum(group - 1, 0), block, target, slot)
         return tuple(held)
 
     if pairs is None:
@@ -148,7 +150,7 @@
         groups = seq // GROUP // len(waits)
         waits[-1]()
         for left, right, target in pairs:
-            fill_group(left, right, seq // GROUP - 1, block, target)
+            fill_group(left, right, seq // GROUP - 1, block, target, slot)
         for i in reversed(range(len(waits))):
             if i > 0:
                 waits[i - 1]()
@@ -193,8 +195,8 @@
 ):
     seq, channels = q_ref.shape
     modes = rate_cols.shape[0]
-    blocks = gated_ref.shape[0]
-    sub = channels // (blocks * LANES)
+    sub = gated_ref.shape[1] // seq
+    blocks = channels // (sub * LANES)
     part = math.gcd(seq, STEP_ROWS)
     parts = seq // part
     which = 1 - lax.axis_index("ctx") % 2
@@ -236,64 +238,36 @@
         waits, lines = None, None
         for i in reversed(range(parts)):
             wait_part(i)
-            for unit in units:
+            for at, unit in enumerate(units):
                 both = ((k_ref, v_ref), (ct_ref, q_ref))
-                to_scan_order(to_scan, both, part, i, unit[0], (gated_ref, pulled_ref))
+                to_scan_order(to_scan, both, part, i, unit[0], (gated_ref, pulled_ref), at)
     for at, unit in enumerate(units):
-        at_row = at * unit[2] * sub
-        scan_states(
-            unit, sub, gated_ref, pulled_ref, decay_ref, send_ref, at_row, lines, waits
-        )
+        scan_states(unit, at, sub, gated_ref, pulled_ref, decay_ref, send_ref, lines, waits)
     for copy in copies[4 * parts + 1 :]:
         copy.wait()
 
 
 def keep_kernel(
-    q_ref,
-    k_ref,
-    v_ref,
-    ct_ref,
-    decay_ref,
-    to_scan,
-    gated_in,
-    pulled_in,
-    keep_ref,
-    gated_ref,
-    pulled_ref,
-    sems,
+    q_ref, k_ref, v_ref, ct_ref, decay_ref, to_scan, gated_in, pulled_in, keep_ref, *line_refs
 ):
     seq, channels = q_ref.shape
-    blocks = gated_ref.shape[0]
-    sub = channels // (blocks * LANES)
+    sub = gated_in.shape[1] // seq
+    blocks = channels // (sub * LANES)
     modes = decay_ref.shape[0] // (blocks * sub)
     part = math.gcd(seq, STEP_ROWS)
-    which = lax.axis_index("ctx") % 2
-    count = max(blocks // 2, 1)
-    done = pl.ds((1 - which) * count if blocks > 1 else 0, count)
-    copies = [
-        pltpu.make_async_copy(gated_in.at[done], gated_ref.at[done], sems.at[0]),
-        pltpu.make_async_copy(pulled_in.at[done], pulled_ref.at[done], sems.at[1]),
-    ]
-    for copy in copies:
-        copy.start()
-    units = half_units(which, blocks, modes, sub)
+    units = half_units(lax.axis_index("ctx") % 2, blocks, modes, sub)
     lines, pairs = (gated_in, pulled_in), None
     if blocks > 1:
-        lines = (gated_ref, pulled_ref)
+        lines = line_refs
         if can_exchange(sub, part, units):
-            pairs = ((k_ref, v_ref, gated_ref), (ct_ref, q_ref, pulled_ref))
+            pairs = ((k_ref, v_ref, line_refs[0]), (ct_ref, q_ref, line_refs[1]))
         else:
             for i in range(seq // part):
-                for unit in units:
+                for at, unit in enumerate(units):
                     both = ((k_ref, v_ref), (ct_ref, q_ref))
-                    to_scan_order(to_scan, both, part, i, unit[0], lines)
+                    to_scan_order(to_scan, both, part, i, unit[0], lines, at)
     for at, unit in enumerate(units):
-        at_row = at * unit[2] * sub
-        scan_states(
-            unit, sub, *lines, decay_ref, keep_ref, at_row, pairs, [lambda: None]
-        )
-    for copy in copies:
-        copy.wait()
+        scan_states(unit, at, sub, *lines, decay_ref, keep_ref, pairs, [lambda: None])
 
 
 def own_rows(rate_ref, half):
@@ -419,44 +393,47 @@
         target[rows, :] = ref[first : first + half, :]
 
 
-def mode_rows(block, modes, sub):
-    return [slice((block * modes + n) * sub, (block * modes + n + 1) * sub) for n in range(modes)]
-
-
-def first_local_kernel(modes, lines_ref, decay_ref, rate_ref, res_cols, after_ref, out_ref, coef_ref):
-    sub = decay_ref.shape[0] // (lines_ref.shape[0] * modes)
+def first_local_kernel(modes, *refs):
+    line_refs, (decay_ref, rate_ref, res_cols, after_ref, out_ref, coef_ref) = refs[:-6], refs[-6:]
+    sub = decay_ref.shape[0] // (out_ref.shape[0] * modes)
     spread(res_cols, coef_ref, modes, sub)
     coef_ref[...] = coef_ref[...] * jnp.sqrt(1.0 - jnp.exp(-2.0 * rate_ref[...]))
-    local_kernel(False, modes, lines_ref, decay_ref, coef_ref, after_ref, out_ref)
-
-
-def local_kernel(reverse, modes, lines_ref, decay_ref, coef_ref, after_ref, out_ref):
-    blocks = lines_ref.shape[0]
+    local_kernel(False, modes, *line_refs, decay_ref, coef_ref, after_ref, out_ref)
+
+
+def local_kernel(reverse, modes, *refs):
+    line_refs, (decay_ref, coef_ref, after_ref, out_ref) = refs[:-4], refs[-4:]
+    blocks = out_ref.shape[0]
     sub = decay_ref.shape[0] // (blocks * modes)
-    seq = lines_ref.shape[1] // sub
-    for b in range(blocks):
-        rows = mode_rows(b, modes, sub)
-        decay = [decay_ref[r, :] for r in rows]
-        coef = [coef_ref[r, :] for r in rows]
-
-        def body(j, carry):
-            held = list(carry)
-            for u in range(UNROLL):
-                t = j * UNROLL + u
-                if reverse:
-                    t = seq - 1 - t
-                at = pl.ds(pl.multiple_of(t * sub, sub), sub)
-                x = lines_ref[b, at, :]
-                total = [None] * 4
-                for n in range(modes):
-                    held[n] = decay[n] * held[n] + x
-                    term = coef[n] * held[n]
-                    total[n % 4] = term if n < 4 else total[n % 4] + term
-                out_ref[b, at, :] = tree_sum(total)
-            return tuple(held)
-
-        first = tuple(jnp.zeros((sub, LANES), F32) for _ in range(modes))
-        lax.fori_loop(0, seq // UNROLL, body, first)
+    seq = out_ref.shape[1] // sub
+    core = lax.axis_index("ctx") % 2
+    for ref, which in zip(line_refs, (1 - core, core)):
+        for slot in range(ref.shape[0]):
+            block = which * ref.shape[0] + slot if blocks > 1 else 0
+            rows = [
+                pl.ds(pl.multiple_of((block * modes + n) * sub, sub), sub) for n in range(modes)
+            ]
+            decay = [decay_ref[r, :] for r in rows]
+            coef = [coef_ref[r, :] for r in rows]
+
+            def body(j, carry):
+                held = list(carry)
+                for u in range(UNROLL):
+                    t = j * UNROLL + u
+                    if reverse:
+                        t = seq - 1 - t
+                    at = pl.ds(pl.multiple_of(t * sub, sub), sub)
+                    x = ref[slot, at, :]
+                    total = [None] * 4
+                    for n in range(modes):
+                        held[n] = decay[n] * held[n] + x
+                        term = coef[n] * held[n]
+                        total[n % 4] = term if n < 4 else total[n % 4] + term
+                    out_ref[block, at, :] = tree_sum(total)
+                return tuple(held)
+
+            first = tuple(jnp.zeros((sub, LANES), F32) for _ in range(modes))
+            lax.fori_loop(0, seq // UNROLL, body, first)
 
 
 def add_carries(reverse, unit, sub, decay_ref, coef_ref, states_ref, at_row, source, target, at):
@@ -716,6 +693,7 @@
     table_shape = jax.ShapeDtypeStruct((modes, channels), F32)
     line_scratch = pltpu.VMEM((seq, channels), jnp.bfloat16)
     table_scratch = pltpu.VMEM((modes, channels), F32)
+    own_shape = rows(max(blocks // 2, 1), seq * sub)
     elements = seq * channels * modes
     tables = (decay_rates.T, residues.T, skip_gain.reshape(1, channels))
     sources = (queries, keys_in, values_in, cotangent, *tables)
@@ -740,7 +718,7 @@
         out_specs=[VMEM] * 13,
         out_shape=[rows(3, half)]
         + [line_shape] * 4
-        + [rows(blocks, seq * sub)] * 2
+        + [own_shape] * 2
         + [rows(2 * half)] * 2
         + [jax.ShapeDtypeStruct((size, size), jnp.bfloat16)] * 2
         + [table_shape, jax.ShapeDtypeStruct((1, channels), F32)],
@@ -752,16 +730,16 @@
         name="sent_states",
     )(*[pltpu.with_memory_space_constraint(item, pltpu.HBM) for item in sources])
     sibling = swap(send, 0)
-    keep, gated, pulled = pl.pallas_call(
+    keep, *kept_lines = pl.pallas_call(
         keep_kernel,
-        out_shape=[rows(3, half)] + [rows(blocks, seq * sub)] * 2,
-        scratch_shapes=[pltpu.SemaphoreType.DMA((2,))],
+        out_shape=[rows(3, half)] + [own_shape] * (2 if blocks > 1 else 0),
         compiler_params=KERNEL,
         cost_estimate=pl.CostEstimate(
             flops=3 * elements, bytes_accessed=8 * seq * channels, transcendentals=0
         ),
         name="kept_states",
     )(q, k, v, ct, row_decay, to_scan, gated, pulled)
+    gated, pulled = (gated, *kept_lines[:1]), (pulled, *kept_lines[1:])
 
     def wire(level):
         return rows(2 if level == levels - 1 else 3, half, dtype=WIRE)
@@ -786,7 +764,7 @@
         compiler_params=KERNEL,
         cost_estimate=local_cost,
         name="local_conv",
-    )(gated, row_decay, row_rates, res_cols, block[4, :8])
+    )(*gated, row_decay, row_rates, res_cols, block[4, :8])
     for level in range(1, levels - 1):
         block, packed = pl.pallas_call(
             partial(level_kernel, seq, level, level + 1 == levels - 1),
@@ -801,7 +779,7 @@
         compiler_params=KERNEL,
         cost_estimate=local_cost,
         name="local_adjoint",
-    )(pulled, row_decay, row_coefs, block[4, :8])
+    )(*pulled, row_decay, row_coefs, block[4, :8])
     mine, other, square = pl.pallas_call(
         partial(last_kernel, seq, levels - 1),
         out_shape=[rows(3 * half)] * 2 + [rows(8)],
@@ -812,7 +790,6 @@
     early, late = early_parts(seq)
     early_shape = jax.ShapeDtypeStruct((seq * len(early) // parts, channels), jnp.bfloat16)
     late_scratch = pltpu.VMEM((seq * max(len(late), 1) // parts, channels), jnp.bfloat16)
-    own_shape = rows(max(blocks // 2, 1), seq * sub)
     kept = {}
 
     def add_own(after):

time: 29.5 us -> 29.3 us (level)
  no operation moved by 1% of the time
where the time goes in v4:
time: 29.3 us; the launch traced here: 29.2 us
  Pallas kernels  15.8 us (54%)
  starting transfers between devices  9.68 us (33%)
  waiting for transfers between devices  2.94 us (10%)
  between operations  0.77 us (3%)
    ppermute x5, starting transfers between devices, swap(): return lax.ppermute(value, 'ctx', [(i, i ^ 1 << bit) for i in range(ctx)])  6.12 us
    pallas_call x1, Pallas kernels, shards(): pl.pallas_call(send_kernel, in_specs=[HBM] * 7, out_specs=[VMEM] * 13, ou...  3.62 us
    ppermute x3, starting transfers between devices, tp_swap(): return lax.ppermute(value, 'tp', [(i, i ^ mask) for i in range(tp)])  3.55 us
    ppermute x5, waiting for transfers between devices, swap(): return lax.ppermute(value, 'ctx', [(i, i ^ 1 << bit) for i in range(ctx)])  2.62 us
    pallas_call x1, Pallas kernels, shards(): pl.pallas_call(partial(first_local_kernel, modes), out_shape=[whole, rows...  2.36 us
    pallas_call x1, Pallas kernels, shards(): pl.pallas_call(partial(local_kernel, True, modes), out_shape=whole, compi...  2.32 us
    pallas_call x1, Pallas kernels, shards(): pl.pallas_call(keep_kernel, out_shape=[rows(3, half)] + [own_shape] * (2...  2.31 us
    pallas_call x1, Pallas kernels, shards(): pl.pallas_call(partial(last_outputs_kernel, math.sqrt(channels * tp * mod...  1.29 us
  transfers between devices with their start and end apart: 8, of which 4 were waited for; matrix products, arithmetic and copies ran while one was open for 0% of the time, Pallas kernels for 36%

profile of v4, /device:TPU:0, one launch (start us, length us, event | category | flops | bytes accessed | tf_op | source)
XLA Modules:
  0.0 29.2 jit_solution(13848575036646767441)
XLA Ops:
  0.6 3.6 %sent_states.1 = (f32[3,128,128]{2,1,0:T(8,128)S(1)}, bf16[128,2048]{1,0:T(8,128)(2,1)S(1)}, bf16[128,2048]{1,0:T(8,128)(2,1)S(1)}, bf16[128,2048]{1,0:T(8,128)(...) custom-call(bf16[128,2048]{1,0:T(8,128)(2,1)} %q_hbm.1, ...), custom_call_target="tpu_custom_call" | custom-call | flops 12582912 | bytes 2097152 | tf_op jit(solution)/shard_map/sent_states/pallas_call | solution.py:715
  4.3 0.5 %collective-permute-start = (f32[3,128,128]{2,1,0:T(8,128)S(1)}, f32[3,128,128]{2,1,0:T(8,128)S(1)}, u32[]{:S(2)}, u32[]{:S(2)}) collective-permute-start(f32[3,128,128]{2,1,0:T(8,128)S(1)} %get-tuple-element.56), channel_id=1, source_target_pairs={{0,4},{4,0},{8,12},{12,8},{16,20},{20,16},{24,28},{28,24},{1,5},{5... | collective-permute-start | bytes 589832 | tf_op jit(solution)/shard_map/ppermute | solution.py:687
  4.8 2.3 %kept_states.1 = (f32[3,128,128]{2,1,0:T(8,128)S(1)}, f32[1,1024,128]{2,1,0:T(8,128)S(1)}, f32[1,1024,128]{2,1,0:T(8,128)S(1)}) custom-call(bf16[128,2048]{1,0:T(8,128)(2,1)S(1)} %get-tuple-element.44.q_ref.refs_0_, bf16[128,2048]{1,0:T(8,128)(2,1)S(1)} %get-tuple-element.45.k_ref.refs_1_, bf16[128,2048]{1,0:T(8,128)(2,1)S(1)} %get-tuple-element.46.v_ref.refs_2_, ...), custom_call_target="tpu_custom_call" | custom-call | flops 12582912 | bytes 2097152 | tf_op jit(solution)/shard_map/kept_states/pallas_call | solution.py:733
  7.1 0.0 collective-permute-done.got_ref.sibling_ref
  7.1 0.1 chip_states.1
  7.2 2.7 %collective-permute-start.1 = (bf16[3,128,128]{2,1,0:T(8,128)(2,1)S(1)}, bf16[3,128,128]{2,1,0:T(8,128)(2,1)S(1)}, u32[]{:S(2)}, u32[]{:S(2)}) collective-permute-start(bf16[3,128,128]{2,1,0:T(8,128)(2,1)S(1)} %get-tuple-element.60), channel_id=1, source_target_pairs={{0,8},{4,12},{8,0},{12,4},{16,24},{20,28},{24,16},{28,20},{1,9},{5... | collective-permute-start | bytes 294920 | tf_op jit(solution)/shard_map/ppermute | solution.py:687
  9.9 2.4 %local_conv.1 = (f32[2,1024,128]{2,1,0:T(8,128)S(1)}, f32[256,128]{1,0:T(8,128)S(1)}) custom-call(f32[1,1024,128]{2,1,0:T(8,128)S(1)} %get-tuple-element.49.gated_in.refs_0_, f32[1,1024,128]{2,1,0:T(8,128)S(1)} %get-tuple-element.52.refs_1_, f32[256,128]{1,0:T(8,128)S(1)} %get-tuple-element.48.decay_ref.refs_2_, ...), custom_call_target="tpu_custom_call" | custom-call | flops 16777216 | bytes 2097152 | tf_op jit(solution)/shard_map/local_conv/pallas_call | solution.py:761
  12.3 1.1 %collective-permute-done.1.got_ref = bf16[3,128,128]{2,1,0:T(8,128)(2,1)S(1)} collective-permute-done((bf16[3,128,128]{2,1,0:T(8,128)(2,1)S(1)}, bf16[3,128,128]{2,1,0:T(8,128)(2,1)S(1)}, u32[]{:S(2)}, u32[]{:S(2)}) %collective-permute-start.1) | collective-permute-done | bytes 98336 | tf_op jit(solution)/shard_map/ppermute | solution.py:687
  13.3 0.1 block_states.1
  13.4 2.8 %collective-permute-start.2 = (bf16[2,128,128]{2,1,0:T(8,128)(2,1)S(1)}, bf16[2,128,128]{2,1,0:T(8,128)(2,1)S(1)}, u32[]{:S(2)}, u32[]{:S(2)}) collective-permute-start(bf16[2,128,128]{2,1,0:T(8,128)(2,1)S(1)} %get-tuple-element.63), channel_id=1, source_target_pairs={{0,16},{4,20},{8,24},{12,28},{16,0},{20,4},{24,8},{28,12},{1,17},{... | collective-permute-start | bytes 196616 | tf_op jit(solution)/shard_map/ppermute | solution.py:687
  16.2 2.3 %local_adjoint.1.adj_ref = f32[2,1024,128]{2,1,0:T(8,128)S(1)} custom-call(f32[1,1024,128]{2,1,0:T(8,128)S(1)} %get-tuple-element.51.pulled_in.refs_0_, f32[1,1024,128]{2,1,0:T(8,128)S(1)} %get-tuple-element.64.refs_1_, f32[256,128]{1,0:T(8,128)S(1)} %get-tuple-element.48.decay_ref.refs_2_, f32[256,128]{1,0:T(8,128)S(1)} %get-tuple-element.58.refs_3_.coef_ref, ...), custom_call_target="tpu_custom_call" | custom-call | flops 16777216 | bytes 2097152 | tf_op jit(solution)/shard_map/local_adjoint/pallas_call | solution.py:776
  18.6 1.4 %collective-permute-done.2.got_ref = bf16[2,128,128]{2,1,0:T(8,128)(2,1)S(1)} collective-permute-done((bf16[2,128,128]{2,1,0:T(8,128)(2,1)S(1)}, bf16[2,128,128]{2,1,0:T(8,128)(2,1)S(1)}, u32[]{:S(2)}, u32[]{:S(2)}) %collective-permute-start.2) | collective-permute-done | bytes 65568 | tf_op jit(solution)/shard_map/ppermute | solution.py:687
  19.9 0.1 carries.1
  20.1 2.5 %collective-permute-start.6 = (f32[8,128]{1,0:T(8,128)S(1)}, f32[8,128]{1,0:T(8,128)S(1)}, u32[]{:S(2)}, u32[]{:S(2)}) collective-permute-start(f32[8,128]{1,0:T(8,128)S(1)} %get-tuple-element.73.refs_0_), channel_id=1, source_target_pairs={{0,3},{1,2},{2,1},{3,0},{4,7},{5,6},{6,5},{7,4},{8,11},{9,10},{10,... | collective-permute-start | bytes 12296 | tf_op jit(solution)/shard_map/ppermute | solution.py:876
  22.6 0.5 %collective-permute-start.5 = (f32[8,128]{1,0:T(8,128)S(1)}, f32[8,128]{1,0:T(8,128)S(1)}, u32[]{:S(2)}, u32[]{:S(2)}) collective-permute-start(f32[8,128]{1,0:T(8,128)S(1)} %get-tuple-element.73.refs_0_), channel_id=1, source_target_pairs={{0,2},{1,3},{2,0},{3,1},{4,6},{5,7},{6,4},{7,5},{8,10},{9,11},{10,... | collective-permute-start | bytes 12296 | tf_op jit(solution)/shard_map/ppermute | solution.py:876
  23.1 0.5 %collective-permute-start.4 = (f32[8,128]{1,0:T(8,128)S(1)}, f32[8,128]{1,0:T(8,128)S(1)}, u32[]{:S(2)}, u32[]{:S(2)}) collective-permute-start(f32[8,128]{1,0:T(8,128)S(1)} %get-tuple-element.73.refs_0_), channel_id=1, source_target_pairs={{0,1},{1,0},{2,3},{3,2},{4,5},{5,4},{6,7},{7,6},{8,9},{9,8},{10,11... | collective-permute-start | bytes 12296 | tf_op jit(solution)/shard_map/ppermute | solution.py:876
  23.6 0.0 collective-permute-start.3
  23.6 1.2 %own_carries.1 = (f32[1,1024,128]{2,1,0:T(8,128)S(1)}, f32[1,1024,128]{2,1,0:T(8,128)S(1)}) custom-call(f32[2,1024,128]{2,1,0:T(8,128)S(1)} %get-tuple-element.61.conv_ref, f32[2,1024,128]{2,1,0:T(8,128)S(1)} %local_adjoint.1.adj_ref, f32[256,128]{1,0:T(8,128)S(1)} %get-tuple-element.48.decay_ref.refs_2_, f32[256,128]{1,0:T(8,128)S(1)} %get-tuple-element.58.refs_3_.coef_ref, ...), custom_call_target="tpu_custom_call" | custom-call | flops 8388608 | bytes 2097152 | tf_op jit(solution)/shard_map/own_carries/pallas_call | solution.py:796
  24.9 0.2 collective-permute-done.3.other_ref.refs_9_
  25.1 1.3 %forward_outputs.1 = (bf16[128,2048]{1,0:T(8,128)(2,1)S(1)}, bf16[128,2048]{1,0:T(8,128)(2,1)S(1)}, f32[8,128]{1,0:T(8,128)S(1)}) custom-call(bf16[128,2048]{1,0:T(8,128)(2,1)S(1)} %get-tuple-element.44.q_ref.refs_0_, bf16[128,2048]{1,0:T(8,128)(2,1)S(1)} %get-tuple-element.45.k_ref.refs_1_, bf16[128,2048]{1,0:T(8,128)(2,1)S(1)} %get-tuple-element.46.v_ref.refs_2_, ...), custom_call_target="tpu_custom_call" | custom-call | flops 8388608 | bytes 4194304 | tf_op jit(solution)/shard_map/forward_outputs/pallas_call | solution.py:808
  26.4 0.3 %collective-permute-done.4.refs_1_ = f32[8,128]{1,0:T(8,128)S(1)} collective-permute-done((f32[8,128]{1,0:T(8,128)S(1)}, f32[8,128]{1,0:T(8,128)S(1)}, u32[]{:S(2)}, u32[]{:S(2)}) %collective-permute-start.4) | collective-permute-done | bytes 4128 | tf_op jit(solution)/shard_map/ppermute | solution.py:876
  26.7 0.1 collective-permute-start.7
  26.8 1.1 %adjoint_outputs.1 = (bf16[128,2048]{1,0:T(8,128)(2,1)}, bf16[128,2048]{1,0:T(8,128)(2,1)}, f32[2,1024,128]{2,1,0:T(8,128)S(1)}, bf16[64,2048]{1,0:T(8,128)(2,1)...) custom-call(bf16[128,2048]{1,0:T(8,128)(2,1)S(1)} %get-tuple-element.44.q_ref.refs_0_, ...), custom_call_target="tpu_custom_call" | custom-call | flops 8388608 | bytes 2097152 | tf_op jit(solution)/shard_map/adjoint_outputs/pallas_call | solution.py:835
  27.9 1.3 %last_outputs.1 = (f32[16,2048]{1,0:T(8,128)}, bf16[128,2048]{1,0:T(8,128)(2,1)}, bf16[128,2048]{1,0:T(8,128)(2,1)}) custom-call(bf16[128,2048]{1,0:T(8,128)(2,1)S(1)} %get-tuple-element.44.q_ref.refs_0_, bf16[128,2048]{1,0:T(8,128)(2,1)S(1)} %get-tuple-element.45.k_ref.refs_1_, bf16[128,2048]{1,0:T(8,128)(2,1)S(1)} %get-tuple-element.46.v_ref.refs_2_, ...), custom_call_target="tpu_custom_call" | custom-call | flops 4194304 | bytes 2097152 | tf_op jit(solution)/shard_map/last_outputs/pallas_call | solution.py:891
  (10 shorter events, 0.0 us)
Async XLA Ops:
  4.3 2.8 %collective-permute-start = (f32[3,128,128]{2,1,0:T(8,128)S(1)}, f32[3,128,128]{2,1,0:T(8,128)S(1)}, u32[]{:S(2)}, u32[]{:S(2)}) collective-permute-start(f32[3,128,128]{2,1,0:T(8,128)S(1)} %get-tuple-element.56), channel_id=1, source_target_pairs={{0,4},{4,0},{8,12},{12,8},{16,20},{20,16},{24,28},{28,24},{1,5},{5... | collective-permute-start | bytes 589832 | tf_op jit(solution)/shard_map/ppermute | solution.py:687
  7.2 6.1 %collective-permute-start.1 = (bf16[3,128,128]{2,1,0:T(8,128)(2,1)S(1)}, bf16[3,128,128]{2,1,0:T(8,128)(2,1)S(1)}, u32[]{:S(2)}, u32[]{:S(2)}) collective-permute-start(bf16[3,128,128]{2,1,0:T(8,128)(2,1)S(1)} %get-tuple-element.60), channel_id=1, source_target_pairs={{0,8},{4,12},{8,0},{12,4},{16,24},{20,28},{24,16},{28,20},{1,9},{5... | collective-permute-start | bytes 294920 | tf_op jit(solution)/shard_map/ppermute | solution.py:687
  13.4 6.5 %collective-permute-start.2 = (bf16[2,128,128]{2,1,0:T(8,128)(2,1)S(1)}, bf16[2,128,128]{2,1,0:T(8,128)(2,1)S(1)}, u32[]{:S(2)}, u32[]{:S(2)}) collective-permute-start(bf16[2,128,128]{2,1,0:T(8,128)(2,1)S(1)} %get-tuple-element.63), channel_id=1, source_target_pairs={{0,16},{4,20},{8,24},{12,28},{16,0},{20,4},{24,8},{28,12},{1,17},{... | collective-permute-start | bytes 196616 | tf_op jit(solution)/shard_map/ppermute | solution.py:687
  20.1 6.3 %collective-permute-start.6 = (f32[8,128]{1,0:T(8,128)S(1)}, f32[8,128]{1,0:T(8,128)S(1)}, u32[]{:S(2)}, u32[]{:S(2)}) collective-permute-start(f32[8,128]{1,0:T(8,128)S(1)} %get-tuple-element.73.refs_0_), channel_id=1, source_target_pairs={{0,3},{1,2},{2,1},{3,0},{4,7},{5,6},{6,5},{7,4},{8,11},{9,10},{10,... | collective-permute-start | bytes 12296 | tf_op jit(solution)/shard_map/ppermute | solution.py:876
  22.6 3.8 %collective-permute-start.5 = (f32[8,128]{1,0:T(8,128)S(1)}, f32[8,128]{1,0:T(8,128)S(1)}, u32[]{:S(2)}, u32[]{:S(2)}) collective-permute-start(f32[8,128]{1,0:T(8,128)S(1)} %get-tuple-element.73.refs_0_), channel_id=1, source_target_pairs={{0,2},{1,3},{2,0},{3,1},{4,6},{5,7},{6,4},{7,5},{8,10},{9,11},{10,... | collective-permute-start | bytes 12296 | tf_op jit(solution)/shard_map/ppermute | solution.py:876
  23.1 3.6 %collective-permute-start.4 = (f32[8,128]{1,0:T(8,128)S(1)}, f32[8,128]{1,0:T(8,128)S(1)}, u32[]{:S(2)}, u32[]{:S(2)}) collective-permute-start(f32[8,128]{1,0:T(8,128)S(1)} %get-tuple-element.73.refs_0_), channel_id=1, source_target_pairs={{0,1},{1,0},{2,3},{3,2},{4,5},{5,4},{6,7},{7,6},{8,9},{9,8},{10,11... | collective-permute-start | bytes 12296 | tf_op jit(solution)/shard_map/ppermute | solution.py:876
  23.6 1.4 %collective-permute-start.3 = (f32[384,128]{1,0:T(8,128)S(1)}, f32[384,128]{1,0:T(8,128)S(1)}, u32[]{:S(2)}, u32[]{:S(2)}) collective-permute-start(f32[384,128]{1,0:T(8,128)S(1)} %get-tuple-element.65), channel_id=1, source_target_pairs={{0,4},{4,0},{8,12},{12,8},{16,20},{20,16},{24,28},{28,24},{1,5},{5... | collective-permute-start | bytes 589832 | tf_op jit(solution)/shard_map/ppermute | solution.py:687
  26.7 1.2 %collective-permute-start.7 = (f32[8,128]{1,0:T(8,128)S(1)}, f32[8,128]{1,0:T(8,128)S(1)}, u32[]{:S(2)}, u32[]{:S(2)}) collective-permute-start(f32[8,128]{1,0:T(8,128)S(1)} %square_sum.1.after_ref.refs_12_), channel_id=1, source_target_pairs={{0,4},{4,0},{8,12},{12,8},{16,20},{20,16},{24,28},{28,24},{1,5},{5... | collective-permute-start | bytes 12296 | tf_op jit(solution)/shard_map/ppermute | solution.py:687

commit v5 on v4

--- a/solution.py
+++ b/solution.py
@@ -359,7 +359,6 @@
     after_ref,
     mine_ref,
     other_ref,
-    share_ref,
 ):
     half = block_ref.shape[1]
     rate = own_rows(rate_ref, half)
@@ -380,9 +379,10 @@
     other_ref[0:half, :] = jnp.where(first, ahead_second, ahead)
     other_ref[half : 2 * half, :] = jnp.where(first, after, after_first)
     squares = raw * raw
-    share_ref[...] = tree_sum([squares[i : i + 8, :] for i in range(0, half, 8)])
-    mine_ref[2 * half : 3 * half, :] = raw
-    other_ref[2 * half : 3 * half, :] = raw
+    share = tree_sum([squares[i : i + 8, :] for i in range(0, half, 8)])
+    for ref in (mine_ref, other_ref):
+        ref[2 * half : 3 * half, :] = raw
+        ref[3 * half : 3 * half + 8, :] = share
 
 
 def place_halves(mine_ref, other_ref, first, target):
@@ -620,11 +620,25 @@
         copy.wait()
 
 
-def last_outputs_kernel(limit, *refs):
-    q_ref, k_ref, v_ref, ct_ref, scanned, skip_ref, gk_early, gv_early = refs[:8]
-    mine_ref, other_ref, from_scan = refs[8:11]
-    share_refs = refs[12:-8]
-    raw_hbm, gk_hbm, gv_hbm, gk_rows, gv_rows, raw_cols, states, sems = refs[-8:]
+def late_kernel(
+    q_ref,
+    k_ref,
+    v_ref,
+    ct_ref,
+    scanned,
+    skip_ref,
+    gk_early,
+    gv_early,
+    from_scan,
+    after_ref,
+    gk_hbm,
+    gv_hbm,
+    token_ref,
+    gk_rows,
+    gv_rows,
+    sems,
+):
+    token_ref[...] = jnp.zeros_like(token_ref)
     copies = []
 
     def start(source, target):
@@ -635,8 +649,6 @@
     early = pl.ds(0, gk_early.shape[0])
     start(gk_early, gk_hbm.at[early])
     start(gv_early, gv_hbm.at[early])
-    clip(limit, scanned.shape[0], mine_ref, other_ref, share_refs, raw_cols, states)
-    start(raw_cols, raw_hbm)
 
     def send(at, to):
         start(gk_rows.at[at], gk_hbm.at[to])
@@ -652,11 +664,15 @@
         copy.wait()
 
 
-def add_kernel(after_ref, *refs):
-    refs[-1][...] = tree_sum([ref[...] for ref in refs[:-1]])
-
-
-def clip(limit, blocks, mine_ref, other_ref, share_refs, out_ref, states):
+def add_kernel(first_core_only, after_ref, *refs):
+    first, others, out_ref = refs[0][...], refs[1:-1], refs[-1]
+    if first_core_only:
+        first = jnp.where(lax.axis_index("ctx") % 2 == 0, first, 0.0)
+    out_ref[...] = tree_sum([first] + [ref[...] for ref in others])
+
+
+def clip_kernel(limit, blocks, mine_ref, other_ref, after_ref, *refs):
+    share_refs, (out_ref, states) = refs[:-2], refs[-2:]
     modes = out_ref.shape[0]
     sub = out_ref.shape[1] // (blocks * LANES)
     half = states.shape[0] // 2
@@ -780,9 +796,9 @@
         cost_estimate=local_cost,
         name="local_adjoint",
     )(*pulled, row_decay, row_coefs, block[4, :8])
-    mine, other, square = pl.pallas_call(
+    mine, other = pl.pallas_call(
         partial(last_kernel, seq, levels - 1),
-        out_shape=[rows(3 * half)] * 2 + [rows(8)],
+        out_shape=[rows(3 * half + 8)] * 2,
         compiler_params=KERNEL,
         name="carries",
     )(block, got, row_rates, keep, sibling, adj[0, :8])
@@ -802,7 +818,7 @@
             ),
             name="own_carries",
         )(conv, adj, row_decay, row_coefs, mine)
-        return kept["adj"][0, :8]
+        return kept["adj"]
 
     def forward_outputs(after):
         kept["out"], kept["gq"], token = pl.pallas_call(
@@ -863,64 +879,65 @@
         kept["final"] = results[:-1]
         return results[-1]
 
-    def plus(after, *shares):
+    def plus(first_core_only, after, *shares):
         return pl.pallas_call(
-            add_kernel,
+            partial(add_kernel, first_core_only),
             in_specs=[VMEM] * (1 + len(shares)),
             out_shape=rows(8),
             compiler_params=KERNEL,
             name="square_sum",
         )(after, *shares)
 
-    def tp_swap(value, mask):
-        return lax.ppermute(value, "tp", [(i, i ^ mask) for i in range(tp)])
-
-    works = [add_own, forward_outputs]
+    def core_swap(value, masks):
+        pairs = [
+            (i * tp + j, i * tp + (j ^ masks[i % 2]))
+            for i in range(ctx)
+            if i % 2 < len(masks)
+            for j in range(tp)
+        ]
+        return lax.ppermute(value, ("ctx", "tp"), pairs)
+
+    after = add_own(mine[:8])
+    square = plus(False, after, mine[3 * half :], other[3 * half :])
+    shares, after = [square], square
+    works = [forward_outputs, adjoint_outputs]
     for bit in range(0, tp.bit_length() - 1, 2):
+        if bit > 0:
+            square = plus(False, after, *shares)
         masks = [m << bit for m in (1, 2, 3) if m << bit < tp]
-        shares = [tp_swap(square, mask) for mask in masks]
+        got = [core_swap(square, masks[at : at + 2]) for at in range(0, len(masks), 2)]
+        for work in works:
+            after = work(after)
+        works = []
+        square = plus(True, after, square, *got)
+        shares = [square, swap(square, 0)]
         after = square
-        while works:
-            after = works.pop(0)(after)
-        square = plus(after, square, *shares)
-    share = swap(square, 0)
-    after = square
-    for work in works + [adjoint_outputs]:
+    for work in works:
         after = work(after)
     operator_out, grad_queries, scanned, early_keys, early_values = kept["final"]
-    grad_residues, grad_keys, grad_values = pl.pallas_call(
-        partial(last_outputs_kernel, math.sqrt(channels * tp * modes)),
-        in_specs=[VMEM] * 14,
-        out_specs=[HBM] * 3,
-        out_shape=[table_shape] + [line_shape] * 2,
+    grad_keys, grad_values, after = pl.pallas_call(
+        late_kernel,
+        in_specs=[VMEM] * 10,
+        out_specs=[HBM] * 2 + [VMEM],
+        out_shape=[line_shape] * 2 + [rows(8)],
         scratch_shapes=[
             late_scratch,
             late_scratch,
-            table_scratch,
-            states_scratch,
-            pltpu.SemaphoreType.DMA((2 * parts + 3,)),
+            pltpu.SemaphoreType.DMA((2 * parts + 2,)),
         ],
         compiler_params=KERNEL,
         cost_estimate=pl.CostEstimate(
             flops=elements, bytes_accessed=8 * seq * channels, transcendentals=0
         ),
-        name="last_outputs",
-    )(
-        q,
-        k,
-        v,
-        ct,
-        scanned,
-        skip,
-        early_keys,
-        early_values,
-        mine,
-        other,
-        from_scan,
-        after,
-        square,
-        share,
-    )
+        name="late_outputs",
+    )(q, k, v, ct, scanned, skip, early_keys, early_values, from_scan, after)
+    grad_residues = pl.pallas_call(
+        partial(clip_kernel, math.sqrt(channels * tp * modes), blocks),
+        out_shape=table_shape,
+        scratch_shapes=[pltpu.VMEM((2 * half, LANES), F32)],
+        compiler_params=KERNEL,
+        name="clip",
+    )(mine, other, after, *shares)
     return (operator_out, grad_queries, grad_keys, grad_values, grad_residues.T)
 
 

time: 29.3 us -> 31.9 us (1.089)
  starting transfers between devices: 9.68 us -> 11 us
  Pallas kernels: 15.8 us -> 16.5 us
  waiting for transfers between devices: 2.94 us -> 3.31 us
    ppermute x3 -> x2, starting transfers between devices: 3.55 us -> 4.94 us  [core_swap(): return lax.ppermute(value, ('ctx', 'tp'), pairs)]
    pallas_call x2 -> x4, Pallas kernels: 1.29 us -> 2.01 us  [the longest x1 1.2 us: shards(): pl.pallas_call(late_kernel, in_specs=[VMEM] * 10, out_specs=[HBM] * 2 + [...]
    ppermute x3 -> x2, waiting for transfers between devices: 0.32 us -> 0.71 us  [core_swap(): return lax.ppermute(value, ('ctx', 'tp'), pairs)]
  transfers between devices with their start and end apart: 8 -> 7, of which waited for: 4 -> 4; matrix products, arithmetic and copies ran while one was open for 0% -> 0% of each run, Pallas kernels for 36% -> 37%
where the time goes in v5:
time: 31.9 us; the launch traced here: 31.7 us
  Pallas kernels  16.5 us (52%)
  starting transfers between devices  11 us (34%)
  waiting for transfers between devices  3.31 us (10%)
  between operations  0.79 us (2%)
    ppermute x5, starting transfers between devices, swap(): return lax.ppermute(value, 'ctx', [(i, i ^ 1 << bit) for i in range(ctx)])  6.08 us
    ppermute x2, starting transfers between devices, core_swap(): return lax.ppermute(value, ('ctx', 'tp'), pairs)  4.94 us
    pallas_call x1, Pallas kernels, shards(): pl.pallas_call(send_kernel, in_specs=[HBM] * 7, out_specs=[VMEM] * 13, ou...  3.64 us
    ppermute x5, waiting for transfers between devices, swap(): return lax.ppermute(value, 'ctx', [(i, i ^ 1 << bit) for i in range(ctx)])  2.6 us
    pallas_call x1, Pallas kernels, shards(): pl.pallas_call(partial(first_local_kernel, modes), out_shape=[whole, rows...  2.36 us
    pallas_call x1, Pallas kernels, shards(): pl.pallas_call(partial(local_kernel, True, modes), out_shape=whole, compi...  2.32 us
    pallas_call x1, Pallas kernels, shards(): pl.pallas_call(keep_kernel, out_shape=[rows(3, half)] + [own_shape] * (2...  2.31 us
    pallas_call x1, Pallas kernels, forward_outputs(): pl.pallas_call(partial(forward_kernel, modes), out_shape=[line_shape] * 2...  1.25 us
  transfers between devices with their start and end apart: 7, of which 4 were waited for; matrix products, arithmetic and copies ran while one was open for 0% of the time, Pallas kernels for 37%

profile of v5, /device:TPU:0, one launch (start us, length us, event | category | flops | bytes accessed | tf_op | source)
XLA Modules:
  0.0 31.7 jit_solution(11500455617258621746)
XLA Ops:
  0.6 3.6 %sent_states.1 = (f32[3,128,128]{2,1,0:T(8,128)S(1)}, bf16[128,2048]{1,0:T(8,128)(2,1)S(1)}, bf16[128,2048]{1,0:T(8,128)(2,1)S(1)}, bf16[128,2048]{1,0:T(8,128)(...) custom-call(bf16[128,2048]{1,0:T(8,128)(2,1)} %q_hbm.1, ...), custom_call_target="tpu_custom_call" | custom-call | flops 12582912 | bytes 2097152 | tf_op jit(solution)/shard_map/sent_states/pallas_call | solution.py:731
  4.3 0.5 %collective-permute-start = (f32[3,128,128]{2,1,0:T(8,128)S(1)}, f32[3,128,128]{2,1,0:T(8,128)S(1)}, u32[]{:S(2)}, u32[]{:S(2)}) collective-permute-start(f32[3,128,128]{2,1,0:T(8,128)S(1)} %get-tuple-element.55), channel_id=1, source_target_pairs={{0,4},{4,0},{8,12},{12,8},{16,20},{20,16},{24,28},{28,24},{1,5},{5... | collective-permute-start | bytes 589832 | tf_op jit(solution)/shard_map/ppermute | solution.py:703
  4.8 2.3 %kept_states.1 = (f32[3,128,128]{2,1,0:T(8,128)S(1)}, f32[1,1024,128]{2,1,0:T(8,128)S(1)}, f32[1,1024,128]{2,1,0:T(8,128)S(1)}) custom-call(bf16[128,2048]{1,0:T(8,128)(2,1)S(1)} %get-tuple-element.43.q_ref, bf16[128,2048]{1,0:T(8,128)(2,1)S(1)} %get-tuple-element.44.k_ref, bf16[128,2048]{1,0:T(8,128)(2,1)S(1)} %get-tuple-element.45.v_ref, ...), custom_call_target="tpu_custom_call" | custom-call | flops 12582912 | bytes 2097152 | tf_op jit(solution)/shard_map/kept_states/pallas_call | solution.py:749
  7.1 0.0 collective-permute-done.got_ref.sibling_ref
  7.1 0.1 chip_states.1
  7.2 2.7 %collective-permute-start.1 = (bf16[3,128,128]{2,1,0:T(8,128)(2,1)S(1)}, bf16[3,128,128]{2,1,0:T(8,128)(2,1)S(1)}, u32[]{:S(2)}, u32[]{:S(2)}) collective-permute-start(bf16[3,128,128]{2,1,0:T(8,128)(2,1)S(1)} %get-tuple-element.59), channel_id=1, source_target_pairs={{0,8},{4,12},{8,0},{12,4},{16,24},{20,28},{24,16},{28,20},{1,9},{5... | collective-permute-start | bytes 294920 | tf_op jit(solution)/shard_map/ppermute | solution.py:703
  9.9 2.4 %local_conv.1 = (f32[2,1024,128]{2,1,0:T(8,128)S(1)}, f32[256,128]{1,0:T(8,128)S(1)}) custom-call(f32[1,1024,128]{2,1,0:T(8,128)S(1)} %get-tuple-element.48.gated_in.refs_0_, f32[1,1024,128]{2,1,0:T(8,128)S(1)} %get-tuple-element.51.refs_1_, f32[256,128]{1,0:T(8,128)S(1)} %get-tuple-element.47.decay_ref.refs_2_, ...), custom_call_target="tpu_custom_call" | custom-call | flops 16777216 | bytes 2097152 | tf_op jit(solution)/shard_map/local_conv/pallas_call | solution.py:777
  12.3 1.0 %collective-permute-done.1.got_ref = bf16[3,128,128]{2,1,0:T(8,128)(2,1)S(1)} collective-permute-done((bf16[3,128,128]{2,1,0:T(8,128)(2,1)S(1)}, bf16[3,128,128]{2,1,0:T(8,128)(2,1)S(1)}, u32[]{:S(2)}, u32[]{:S(2)}) %collective-permute-start.1) | collective-permute-done | bytes 98336 | tf_op jit(solution)/shard_map/ppermute | solution.py:703
  13.3 0.1 block_states.1
  13.4 2.8 %collective-permute-start.2 = (bf16[2,128,128]{2,1,0:T(8,128)(2,1)S(1)}, bf16[2,128,128]{2,1,0:T(8,128)(2,1)S(1)}, u32[]{:S(2)}, u32[]{:S(2)}) collective-permute-start(bf16[2,128,128]{2,1,0:T(8,128)(2,1)S(1)} %get-tuple-element.62), channel_id=1, source_target_pairs={{0,16},{4,20},{8,24},{12,28},{16,0},{20,4},{24,8},{28,12},{1,17},{... | collective-permute-start | bytes 196616 | tf_op jit(solution)/shard_map/ppermute | solution.py:703
  16.3 2.3 %local_adjoint.1.adj_ref = f32[2,1024,128]{2,1,0:T(8,128)S(1)} custom-call(f32[1,1024,128]{2,1,0:T(8,128)S(1)} %get-tuple-element.50.pulled_in.refs_0_, f32[1,1024,128]{2,1,0:T(8,128)S(1)} %get-tuple-element.63.refs_1_, f32[256,128]{1,0:T(8,128)S(1)} %get-tuple-element.47.decay_ref.refs_2_, f32[256,128]{1,0:T(8,128)S(1)} %get-tuple-element.57.refs_3_.coef_ref, ...), custom_call_target="tpu_custom_call" | custom-call | flops 16777216 | bytes 2097152 | tf_op jit(solution)/shard_map/local_adjoint/pallas_call | solution.py:792
  18.6 1.4 %collective-permute-done.2.got_ref = bf16[2,128,128]{2,1,0:T(8,128)(2,1)S(1)} collective-permute-done((bf16[2,128,128]{2,1,0:T(8,128)(2,1)S(1)}, bf16[2,128,128]{2,1,0:T(8,128)(2,1)S(1)}, u32[]{:S(2)}, u32[]{:S(2)}) %collective-permute-start.2) | collective-permute-done | bytes 65568 | tf_op jit(solution)/shard_map/ppermute | solution.py:703
  20.0 0.1 carries.1
  20.1 0.1 collective-permute-start.3
  20.2 1.2 %own_carries.1 = (f32[1,1024,128]{2,1,0:T(8,128)S(1)}, f32[1,1024,128]{2,1,0:T(8,128)S(1)}) custom-call(f32[2,1024,128]{2,1,0:T(8,128)S(1)} %get-tuple-element.60.conv_ref, f32[2,1024,128]{2,1,0:T(8,128)S(1)} %local_adjoint.1.adj_ref, f32[256,128]{1,0:T(8,128)S(1)} %get-tuple-element.47.decay_ref.refs_2_, f32[256,128]{1,0:T(8,128)S(1)} %get-tuple-element.57.refs_3_.coef_ref, ...), custom_call_target="tpu_custom_call" | custom-call | flops 8388608 | bytes 2097152 | tf_op jit(solution)/shard_map/own_carries/pallas_call | solution.py:812
  21.4 0.2 collective-permute-done.3.other_ref
  21.6 4.3 %collective-permute-start.5 = (f32[8,128]{1,0:T(8,128)S(1)}, f32[8,128]{1,0:T(8,128)S(1)}, u32[]{:S(2)}, u32[]{:S(2)}) collective-permute-start(f32[8,128]{1,0:T(8,128)S(1)} %square_sum.2.after_ref.refs_0_), channel_id=1, source_target_pairs={{0,3},{1,2},{2,1},{3,0},{8,11},{9,10},{10,9},{11,8},{16,19},{17,18... | collective-permute-start | bytes 12296 | tf_op jit(solution)/shard_map/ppermute | solution.py:898
  26.0 0.6 %collective-permute-start.4 = (f32[8,128]{1,0:T(8,128)S(1)}, f32[8,128]{1,0:T(8,128)S(1)}, u32[]{:S(2)}, u32[]{:S(2)}) collective-permute-start(f32[8,128]{1,0:T(8,128)S(1)} %square_sum.2.after_ref.refs_0_), channel_id=1, source_target_pairs={{0,1},{1,0},{2,3},{3,2},{4,6},{5,7},{6,4},{7,5},{8,9},{9,8},{10,11... | collective-permute-start | bytes 12296 | tf_op jit(solution)/shard_map/ppermute | solution.py:898
  26.6 1.2 %forward_outputs.1 = (bf16[128,2048]{1,0:T(8,128)(2,1)S(1)}, bf16[128,2048]{1,0:T(8,128)(2,1)S(1)}, f32[8,128]{1,0:T(8,128)S(1)}) custom-call(bf16[128,2048]{1,0:T(8,128)(2,1)S(1)} %get-tuple-element.43.q_ref, bf16[128,2048]{1,0:T(8,128)(2,1)S(1)} %get-tuple-element.44.k_ref, bf16[128,2048]{1,0:T(8,128)(2,1)S(1)} %get-tuple-element.45.v_ref, ...), custom_call_target="tpu_custom_call" | custom-call | flops 8388608 | bytes 4194304 | tf_op jit(solution)/shard_map/forward_outputs/pallas_call | solution.py:824
  27.8 1.1 %adjoint_outputs.1 = (bf16[128,2048]{1,0:T(8,128)(2,1)}, bf16[128,2048]{1,0:T(8,128)(2,1)}, f32[2,1024,128]{2,1,0:T(8,128)S(1)}, bf16[64,2048]{1,0:T(8,128)(2,1)...) custom-call(bf16[128,2048]{1,0:T(8,128)(2,1)S(1)} %get-tuple-element.43.q_ref, ...), custom_call_target="tpu_custom_call" | custom-call | flops 8388608 | bytes 2097152 | tf_op jit(solution)/shard_map/adjoint_outputs/pallas_call | solution.py:851
  28.9 0.0 collective-permute-done.5.refs_2_
  29.0 0.7 %collective-permute-done.4.refs_1_ = f32[8,128]{1,0:T(8,128)S(1)} collective-permute-done((f32[8,128]{1,0:T(8,128)S(1)}, f32[8,128]{1,0:T(8,128)S(1)}, u32[]{:S(2)}, u32[]{:S(2)}) %collective-permute-start.4) | collective-permute-done | bytes 4128 | tf_op jit(solution)/shard_map/ppermute | solution.py:898
  29.7 1.2 %late_outputs.1 = (bf16[128,2048]{1,0:T(8,128)(2,1)}, bf16[128,2048]{1,0:T(8,128)(2,1)}, f32[8,128]{1,0:T(8,128)S(1)}) custom-call(bf16[128,2048]{1,0:T(8,128)(2,1)S(1)} %get-tuple-element.43.q_ref, bf16[128,2048]{1,0:T(8,128)(2,1)S(1)} %get-tuple-element.44.k_ref, bf16[128,2048]{1,0:T(8,128)(2,1)S(1)} %get-tuple-element.45.v_ref, ...), custom_call_target="tpu_custom_call" | custom-call | flops 4194304 | bytes 2097152 | tf_op jit(solution)/shard_map/late_outputs/pallas_call | solution.py:918
  30.9 0.8 %clip.1 = f32[16,2048]{1,0:T(8,128)} custom-call(f32[392,128]{1,0:T(8,128)S(1)} %get-tuple-element.66.mine_ref, f32[392,128]{1,0:T(8,128)S(1)} %collective-permute-done.3.other_ref, f32[8,128]{1,0:T(8,128)S(1)} %get-tuple-element.80.after_ref, f32[8,128]{1,0:T(8,128)S(1)} %square_sum.3.after_ref.refs_0_, f32[8,128]{1,0:T(8,128)S(1)} %collective-permute-done.6.refs_1_), custom_call_target="tpu_custom_call" | custom-call | tf_op jit(solution)/shard_map/clip/pallas_call | solution.py:934
  (11 shorter events, 0.0 us)
Async XLA Ops:
  4.3 2.8 %collective-permute-start = (f32[3,128,128]{2,1,0:T(8,128)S(1)}, f32[3,128,128]{2,1,0:T(8,128)S(1)}, u32[]{:S(2)}, u32[]{:S(2)}) collective-permute-start(f32[3,128,128]{2,1,0:T(8,128)S(1)} %get-tuple-element.55), channel_id=1, source_target_pairs={{0,4},{4,0},{8,12},{12,8},{16,20},{20,16},{24,28},{28,24},{1,5},{5... | collective-permute-start | bytes 589832 | tf_op jit(solution)/shard_map/ppermute | solution.py:703
  7.2 6.1 %collective-permute-start.1 = (bf16[3,128,128]{2,1,0:T(8,128)(2,1)S(1)}, bf16[3,128,128]{2,1,0:T(8,128)(2,1)S(1)}, u32[]{:S(2)}, u32[]{:S(2)}) collective-permute-start(bf16[3,128,128]{2,1,0:T(8,128)(2,1)S(1)} %get-tuple-element.59), channel_id=1, source_target_pairs={{0,8},{4,12},{8,0},{12,4},{16,24},{20,28},{24,16},{28,20},{1,9},{5... | collective-permute-start | bytes 294920 | tf_op jit(solution)/shard_map/ppermute | solution.py:703
  13.4 6.5 %collective-permute-start.2 = (bf16[2,128,128]{2,1,0:T(8,128)(2,1)S(1)}, bf16[2,128,128]{2,1,0:T(8,128)(2,1)S(1)}, u32[]{:S(2)}, u32[]{:S(2)}) collective-permute-start(bf16[2,128,128]{2,1,0:T(8,128)(2,1)S(1)} %get-tuple-element.62), channel_id=1, source_target_pairs={{0,16},{4,20},{8,24},{12,28},{16,0},{20,4},{24,8},{28,12},{1,17},{... | collective-permute-start | bytes 196616 | tf_op jit(solution)/shard_map/ppermute | solution.py:703
  20.1 1.5 %collective-permute-start.3 = (f32[392,128]{1,0:T(8,128)S(1)}, f32[392,128]{1,0:T(8,128)S(1)}, u32[]{:S(2)}, u32[]{:S(2)}) collective-permute-start(f32[392,128]{1,0:T(8,128)S(1)} %get-tuple-element.64), channel_id=1, source_target_pairs={{0,4},{4,0},{8,12},{12,8},{16,20},{20,16},{24,28},{28,24},{1,5},{5... | collective-permute-start | bytes 602120 | tf_op jit(solution)/shard_map/ppermute | solution.py:703
  21.6 7.3 %collective-permute-start.5 = (f32[8,128]{1,0:T(8,128)S(1)}, f32[8,128]{1,0:T(8,128)S(1)}, u32[]{:S(2)}, u32[]{:S(2)}) collective-permute-start(f32[8,128]{1,0:T(8,128)S(1)} %square_sum.2.after_ref.refs_0_), channel_id=1, source_target_pairs={{0,3},{1,2},{2,1},{3,0},{8,11},{9,10},{10,9},{11,8},{16,19},{17,18... | collective-permute-start | bytes 12296 | tf_op jit(solution)/shard_map/ppermute | solution.py:898
  26.0 3.7 %collective-permute-start.4 = (f32[8,128]{1,0:T(8,128)S(1)}, f32[8,128]{1,0:T(8,128)S(1)}, u32[]{:S(2)}, u32[]{:S(2)}) collective-permute-start(f32[8,128]{1,0:T(8,128)S(1)} %square_sum.2.after_ref.refs_0_), channel_id=1, source_target_pairs={{0,1},{1,0},{2,3},{3,2},{4,6},{5,7},{6,4},{7,5},{8,9},{9,8},{10,11... | collective-permute-start | bytes 12296 | tf_op jit(solution)/shard_map/ppermute | solution.py:898
  29.7 1.2 %collective-permute-start.6 = (f32[8,128]{1,0:T(8,128)S(1)}, f32[8,128]{1,0:T(8,128)S(1)}, u32[]{:S(2)}, u32[]{:S(2)}) collective-permute-start(f32[8,128]{1,0:T(8,128)S(1)} %square_sum.3.after_ref.refs_0_), channel_id=1, source_target_pairs={{0,4},{4,0},{8,12},{12,8},{16,20},{20,16},{24,28},{28,24},{1,5},{5... | collective-permute-start | bytes 12296 | tf_op jit(solution)/shard_map/ppermute | solution.py:703

commit v6 on v4

--- a/solution.py
+++ b/solution.py
@@ -436,6 +436,19 @@
             lax.fori_loop(0, seq // UNROLL, body, first)
 
 
+def second_local_kernel(modes, *refs):
+    line_refs, refs = refs[:-11], refs[-11:]
+    decay_ref, coef_ref, q_ref, k_ref, v_ref, ct_ref, skip_ref, after_ref = refs[:8]
+    out_ref, gated_term, pulled_term = refs[8:]
+    local_kernel(True, modes, *line_refs, decay_ref, coef_ref, after_ref, out_ref)
+    pairs = ((k_ref, v_ref, gated_term), (ct_ref, q_ref, pulled_term))
+    for left, right, target in pairs:
+        for at in range(0, q_ref.shape[1], LANES):
+            cols = slice(at, at + LANES)
+            line = left[:, cols].astype(F32) * right[:, cols].astype(F32)
+            target[:, cols] = skip_ref[:, cols] * line.astype(jnp.bfloat16).astype(F32)
+
+
 def add_carries(reverse, unit, sub, decay_ref, coef_ref, states_ref, at_row, source, target, at):
     _, base, modes = unit
     seq = target.shape[1] // sub
@@ -503,10 +516,8 @@
         copy.wait()
 
 
-def line_outputs(
-    from_scan, left, right, scales, skip_ref, scanned, targets, which, done_with=None
-):
-    seq, channels = left.shape
+def line_outputs(from_scan, term, scales, scanned, targets, which, done_with=None):
+    seq, channels = term.shape
     blocks = scanned.shape[0]
     sub = channels // (blocks * LANES)
     part = math.gcd(seq, STEP_ROWS)
@@ -521,8 +532,7 @@
             for s in range(sub):
                 cols = slice((b * sub + s) * LANES, (b * sub + s + 1) * LANES)
                 own = ordered[s * part : (s + 1) * part, b * LANES : (b + 1) * LANES]
-                line = left[rows, cols].astype(F32) * right[rows, cols].astype(F32)
-                mixed = own + skip_ref[:, cols] * line.astype(jnp.bfloat16).astype(F32)
+                mixed = own + term[rows, cols]
                 for scale, target in zip(scales, targets):
                     target[to_rows, cols] = (scale[rows, cols].astype(F32) * mixed).astype(
                         jnp.bfloat16
@@ -534,12 +544,10 @@
 def forward_kernel(
     modes,
     q_ref,
-    k_ref,
-    v_ref,
     ct_ref,
+    term_ref,
     decay_ref,
     coef_ref,
-    skip_ref,
     other_ref,
     from_scan,
     conv_ref,
@@ -557,13 +565,11 @@
     )
     line_outputs(
         from_scan,
-        k_ref,
-        v_ref,
+        term_ref,
         (q_ref, ct_ref),
-        skip_ref,
         scanned,
         (out_ref, gq_ref),
-        range(k_ref.shape[0] // math.gcd(k_ref.shape[0], STEP_ROWS)),
+        range(q_ref.shape[0] // math.gcd(q_ref.shape[0], STEP_ROWS)),
     )
 
 
@@ -574,13 +580,11 @@
 
 def adjoint_kernel(
     modes,
-    q_ref,
     k_ref,
     v_ref,
-    ct_ref,
+    term_ref,
     decay_ref,
     coef_ref,
-    skip_ref,
     other_ref,
     from_scan,
     adj_ref,
@@ -608,22 +612,20 @@
     )
     line_outputs(
         from_scan,
-        ct_ref,
-        q_ref,
+        term_ref,
         (v_ref, k_ref),
-        skip_ref,
         scanned,
         (gk_ref, gv_ref),
-        early_parts(q_ref.shape[0])[0],
+        early_parts(k_ref.shape[0])[0],
     )
     for copy in copies:
         copy.wait()
 
 
 def last_outputs_kernel(limit, *refs):
-    q_ref, k_ref, v_ref, ct_ref, scanned, skip_ref, gk_early, gv_early = refs[:8]
-    mine_ref, other_ref, from_scan = refs[8:11]
-    share_refs = refs[12:-8]
+    k_ref, v_ref, term_ref, scanned, gk_early, gv_early = refs[:6]
+    mine_ref, other_ref, from_scan = refs[6:9]
+    share_refs = refs[10:-8]
     raw_hbm, gk_hbm, gv_hbm, gk_rows, gv_rows, raw_cols, states, sems = refs[-8:]
     copies = []
 
@@ -642,12 +644,10 @@
         start(gk_rows.at[at], gk_hbm.at[to])
         start(gv_rows.at[at], gv_hbm.at[to])
 
-    late = early_parts(q_ref.shape[0])[1]
+    late = early_parts(k_ref.shape[0])[1]
     if len(late) > 0:
         sides, targets = (v_ref, k_ref), (gk_rows, gv_rows)
-        line_outputs(
-            from_scan, ct_ref, q_ref, sides, skip_ref, scanned, targets, late, send
-        )
+        line_outputs(from_scan, term_ref, sides, scanned, targets, late, send)
     for copy in copies:
         copy.wait()
 
@@ -773,13 +773,14 @@
             name="block_states",
         )(block, got, row_rates, conv[0, :8])
         got = swap(packed, level + 1)
-    adj = pl.pallas_call(
-        partial(local_kernel, True, modes),
-        out_shape=whole,
+    term_shape = jax.ShapeDtypeStruct((seq, channels), F32)
+    adj, gated_term, pulled_term = pl.pallas_call(
+        partial(second_local_kernel, modes),
+        out_shape=[whole] + [term_shape] * 2,
         compiler_params=KERNEL,
         cost_estimate=local_cost,
         name="local_adjoint",
-    )(*pulled, row_decay, row_coefs, block[4, :8])
+    )(*pulled, row_decay, row_coefs, q, k, v, ct, skip, block[4, :8])
     mine, other, square = pl.pallas_call(
         partial(last_kernel, seq, levels - 1),
         out_shape=[rows(3 * half)] * 2 + [rows(8)],
@@ -816,12 +817,10 @@
             name="forward_outputs",
         )(
             q,
-            k,
-            v,
             ct,
+            gated_term,
             row_decay,
             row_coefs,
-            skip,
             other,
             from_scan,
             conv,
@@ -834,7 +833,7 @@
         results = (
             pl.pallas_call(
                 partial(adjoint_kernel, modes),
-                in_specs=[VMEM] * 14,
+                in_specs=[VMEM] * 12,
                 out_specs=[HBM] * 2 + [VMEM] * 4,
                 out_shape=[line_shape] * 2 + [whole] + [early_shape] * 2 + [rows(8)],
                 scratch_shapes=[pltpu.SemaphoreType.DMA((3,))],
@@ -844,13 +843,11 @@
                 ),
                 name="adjoint_outputs",
             )(
-                q,
                 k,
                 v,
-                ct,
+                pulled_term,
                 row_decay,
                 row_coefs,
-                skip,
                 other,
                 from_scan,
                 adj,
@@ -890,7 +887,7 @@
     operator_out, grad_queries, scanned, early_keys, early_values = kept["final"]
     grad_residues, grad_keys, grad_values = pl.pallas_call(
         partial(last_outputs_kernel, math.sqrt(channels * tp * modes)),
-        in_specs=[VMEM] * 14,
+        in_specs=[VMEM] * 12,
         out_specs=[HBM] * 3,
         out_shape=[table_shape] + [line_shape] * 2,
         scratch_shapes=[
@@ -906,12 +903,10 @@
         ),
         name="last_outputs",
     )(
-        q,
         k,
         v,
-        ct,
+        pulled_term,
         scanned,
-        skip,
         early_keys,
         early_values,
         mine,

time: 29.3 us -> 30.3 us (1.034)
  waiting for transfers between devices: 2.94 us -> 3.79 us
    ppermute x3, waiting for transfers between devices: 0.32 us -> 1.45 us  [tp_swap(): return lax.ppermute(value, 'tp', [(i, i ^ mask) for i in range(tp)])]
    pallas_call x2, Pallas kernels: 3.38 us -> 3.76 us  [the longest x1 2.7 us: shards(): pl.pallas_call(partial(second_local_kernel, modes), out_shape=[whole] + [...]
  transfers between devices with their start and end apart: 8 -> 8, of which waited for: 4 -> 5; matrix products, arithmetic and copies ran while one was open for 0% -> 0% of each run, Pallas kernels for 36% -> 36%
where the time goes in v6:
time: 30.3 us; the launch traced here: 30.1 us
  Pallas kernels  16 us (53%)
  starting transfers between devices  9.57 us (32%)
  waiting for transfers between devices  3.79 us (13%)
  between operations  0.76 us (3%)
    ppermute x5, starting transfers between devices, swap(): return lax.ppermute(value, 'ctx', [(i, i ^ 1 << bit) for i in range(ctx)])  6.02 us
    pallas_call x1, Pallas kernels, shards(): pl.pallas_call(send_kernel, in_specs=[HBM] * 7, out_specs=[VMEM] * 13, ou...  3.64 us
    ppermute x3, starting transfers between devices, tp_swap(): return lax.ppermute(value, 'tp', [(i, i ^ mask) for i in range(tp)])  3.55 us
    pallas_call x1, Pallas kernels, shards(): pl.pallas_call(partial(second_local_kernel, modes), out_shape=[whole] + [...  2.7 us
    pallas_call x1, Pallas kernels, shards(): pl.pallas_call(partial(first_local_kernel, modes), out_shape=[whole, rows...  2.36 us
    ppermute x5, waiting for transfers between devices, swap(): return lax.ppermute(value, 'ctx', [(i, i ^ 1 << bit) for i in range(ctx)])  2.34 us
    pallas_call x1, Pallas kernels, shards(): pl.pallas_call(keep_kernel, out_shape=[rows(3, half)] + [own_shape] * (2...  2.32 us
    ppermute x3, waiting for transfers between devices, tp_swap(): return lax.ppermute(value, 'tp', [(i, i ^ mask) for i in range(tp)])  1.45 us
  transfers between devices with their start and end apart: 8, of which 5 were waited for; matrix products, arithmetic and copies ran while one was open for 0% of the time, Pallas kernels for 36%

profile of v6, /device:TPU:0, one launch (start us, length us, event | category | flops | bytes accessed | tf_op | source)
XLA Modules:
  0.0 30.1 jit_solution(8786198551873783788)
XLA Ops:
  0.6 3.6 %sent_states.1 = (f32[3,128,128]{2,1,0:T(8,128)S(1)}, bf16[128,2048]{1,0:T(8,128)(2,1)S(1)}, bf16[128,2048]{1,0:T(8,128)(2,1)S(1)}, bf16[128,2048]{1,0:T(8,128)(...) custom-call(bf16[128,2048]{1,0:T(8,128)(2,1)} %q_hbm.1, ...), custom_call_target="tpu_custom_call" | custom-call | flops 12582912 | bytes 2097152 | tf_op jit(solution)/shard_map/sent_states/pallas_call | solution.py:715
  4.3 0.5 %collective-permute-start = (f32[3,128,128]{2,1,0:T(8,128)S(1)}, f32[3,128,128]{2,1,0:T(8,128)S(1)}, u32[]{:S(2)}, u32[]{:S(2)}) collective-permute-start(f32[3,128,128]{2,1,0:T(8,128)S(1)} %get-tuple-element.60), channel_id=1, source_target_pairs={{0,4},{4,0},{8,12},{12,8},{16,20},{20,16},{24,28},{28,24},{1,5},{5... | collective-permute-start | bytes 589832 | tf_op jit(solution)/shard_map/ppermute | solution.py:687
  4.8 2.3 %kept_states.1 = (f32[3,128,128]{2,1,0:T(8,128)S(1)}, f32[1,1024,128]{2,1,0:T(8,128)S(1)}, f32[1,1024,128]{2,1,0:T(8,128)S(1)}) custom-call(bf16[128,2048]{1,0:T(8,128)(2,1)S(1)} %get-tuple-element.50.q_ref.refs_4_, bf16[128,2048]{1,0:T(8,128)(2,1)S(1)} %get-tuple-element.47.k_ref.refs_5_.refs_0_, ...), custom_call_target="tpu_custom_call" | custom-call | flops 12582912 | bytes 2097152 | tf_op jit(solution)/shard_map/kept_states/pallas_call | solution.py:733
  7.1 0.0 collective-permute-done.got_ref.sibling_ref
  7.1 0.1 chip_states.1
  7.2 2.7 %collective-permute-start.1 = (bf16[3,128,128]{2,1,0:T(8,128)(2,1)S(1)}, bf16[3,128,128]{2,1,0:T(8,128)(2,1)S(1)}, u32[]{:S(2)}, u32[]{:S(2)}) collective-permute-start(bf16[3,128,128]{2,1,0:T(8,128)(2,1)S(1)} %get-tuple-element.64), channel_id=1, source_target_pairs={{0,8},{4,12},{8,0},{12,4},{16,24},{20,28},{24,16},{28,20},{1,9},{5... | collective-permute-start | bytes 294920 | tf_op jit(solution)/shard_map/ppermute | solution.py:687
  9.9 2.4 %local_conv.1 = (f32[2,1024,128]{2,1,0:T(8,128)S(1)}, f32[256,128]{1,0:T(8,128)S(1)}) custom-call(f32[1,1024,128]{2,1,0:T(8,128)S(1)} %get-tuple-element.54.gated_in.refs_0_, f32[1,1024,128]{2,1,0:T(8,128)S(1)} %get-tuple-element.56.refs_1_, f32[256,128]{1,0:T(8,128)S(1)} %get-tuple-element.52.decay_ref.refs_2_, ...), custom_call_target="tpu_custom_call" | custom-call | flops 16777216 | bytes 2097152 | tf_op jit(solution)/shard_map/local_conv/pallas_call | solution.py:761
  12.3 1.0 %collective-permute-done.1.got_ref = bf16[3,128,128]{2,1,0:T(8,128)(2,1)S(1)} collective-permute-done((bf16[3,128,128]{2,1,0:T(8,128)(2,1)S(1)}, bf16[3,128,128]{2,1,0:T(8,128)(2,1)S(1)}, u32[]{:S(2)}, u32[]{:S(2)}) %collective-permute-start.1) | collective-permute-done | bytes 98336 | tf_op jit(solution)/shard_map/ppermute | solution.py:687
  13.3 0.1 block_states.1
  13.4 2.8 %collective-permute-start.2 = (bf16[2,128,128]{2,1,0:T(8,128)(2,1)S(1)}, bf16[2,128,128]{2,1,0:T(8,128)(2,1)S(1)}, u32[]{:S(2)}, u32[]{:S(2)}) collective-permute-start(bf16[2,128,128]{2,1,0:T(8,128)(2,1)S(1)} %get-tuple-element.68), channel_id=1, source_target_pairs={{0,16},{4,20},{8,24},{12,28},{16,0},{20,4},{24,8},{28,12},{1,17},{... | collective-permute-start | bytes 196616 | tf_op jit(solution)/shard_map/ppermute | solution.py:687
  16.3 2.7 %local_adjoint.1 = (f32[2,1024,128]{2,1,0:T(8,128)S(1)}, f32[128,2048]{1,0:T(8,128)S(1)}, f32[128,2048]{1,0:T(8,128)S(1)}) custom-call(f32[1,1024,128]{2,1,0:T(8,128)S(1)} %get-tuple-element.49.pulled_in.refs_0_, f32[1,1024,128]{2,1,0:T(8,128)S(1)} %get-tuple-element.55.refs_1_, f32[256,128]{1,0:T(8,128)S(1)} %get-tuple-element.52.decay_ref.refs_2_, ...), custom_call_target="tpu_custom_call" | custom-call | flops 16777216 | bytes 2097152 | tf_op jit(solution)/shard_map/local_adjoint/pallas_call | solution.py:777
  19.0 1.0 %collective-permute-done.2.got_ref = bf16[2,128,128]{2,1,0:T(8,128)(2,1)S(1)} collective-permute-done((bf16[2,128,128]{2,1,0:T(8,128)(2,1)S(1)}, bf16[2,128,128]{2,1,0:T(8,128)(2,1)S(1)}, u32[]{:S(2)}, u32[]{:S(2)}) %collective-permute-start.2) | collective-permute-done | bytes 65568 | tf_op jit(solution)/shard_map/ppermute | solution.py:687
  20.0 0.1 carries.1
  20.1 1.6 %collective-permute-start.4 = (f32[8,128]{1,0:T(8,128)S(1)}, f32[8,128]{1,0:T(8,128)S(1)}, u32[]{:S(2)}, u32[]{:S(2)}) collective-permute-start(f32[8,128]{1,0:T(8,128)S(1)} %get-tuple-element.79.refs_0_), channel_id=1, source_target_pairs={{0,1},{1,0},{2,3},{3,2},{4,5},{5,4},{6,7},{7,6},{8,9},{9,8},{10,11... | collective-permute-start | bytes 12296 | tf_op jit(solution)/shard_map/ppermute | solution.py:873
  21.7 1.5 %collective-permute-start.5 = (f32[8,128]{1,0:T(8,128)S(1)}, f32[8,128]{1,0:T(8,128)S(1)}, u32[]{:S(2)}, u32[]{:S(2)}) collective-permute-start(f32[8,128]{1,0:T(8,128)S(1)} %get-tuple-element.79.refs_0_), channel_id=1, source_target_pairs={{0,2},{1,3},{2,0},{3,1},{4,6},{5,7},{6,4},{7,5},{8,10},{9,11},{10,... | collective-permute-start | bytes 12296 | tf_op jit(solution)/shard_map/ppermute | solution.py:873
  23.2 0.5 %collective-permute-start.6 = (f32[8,128]{1,0:T(8,128)S(1)}, f32[8,128]{1,0:T(8,128)S(1)}, u32[]{:S(2)}, u32[]{:S(2)}) collective-permute-start(f32[8,128]{1,0:T(8,128)S(1)} %get-tuple-element.79.refs_0_), channel_id=1, source_target_pairs={{0,3},{1,2},{2,1},{3,0},{4,7},{5,6},{6,5},{7,4},{8,11},{9,10},{10,... | collective-permute-start | bytes 12296 | tf_op jit(solution)/shard_map/ppermute | solution.py:873
  23.7 0.0 collective-permute-start.3
  23.7 1.2 %own_carries.1 = (f32[1,1024,128]{2,1,0:T(8,128)S(1)}, f32[1,1024,128]{2,1,0:T(8,128)S(1)}) custom-call(f32[2,1024,128]{2,1,0:T(8,128)S(1)} %get-tuple-element.65.conv_ref, f32[2,1024,128]{2,1,0:T(8,128)S(1)} %get-tuple-element.69.adj_ref, f32[256,128]{1,0:T(8,128)S(1)} %get-tuple-element.52.decay_ref.refs_2_, ...), custom_call_target="tpu_custom_call" | custom-call | flops 8388608 | bytes 2097152 | tf_op jit(solution)/shard_map/own_carries/pallas_call | solution.py:797
  24.9 0.2 collective-permute-done.3.other_ref.refs_7_
  25.1 1.1 %forward_outputs.1 = (bf16[128,2048]{1,0:T(8,128)(2,1)S(1)}, bf16[128,2048]{1,0:T(8,128)(2,1)S(1)}, f32[8,128]{1,0:T(8,128)S(1)}) custom-call(bf16[128,2048]{1,0:T(8,128)(2,1)S(1)} %get-tuple-element.50.q_ref.refs_4_, bf16[128,2048]{1,0:T(8,128)(2,1)S(1)} %get-tuple-element.51.ct_ref.refs_7_, f32[128,2048]{1,0:T(8,128)S(1)} %get-tuple-element.74.term_ref, ...), custom_call_target="tpu_custom_call" | custom-call | flops 8388608 | bytes 4194304 | tf_op jit(solution)/shard_map/forward_outputs/pallas_call | solution.py:809
  26.2 1.4 %collective-permute-done.6.refs_3_ = f32[8,128]{1,0:T(8,128)S(1)} collective-permute-done((f32[8,128]{1,0:T(8,128)S(1)}, f32[8,128]{1,0:T(8,128)S(1)}, u32[]{:S(2)}, u32[]{:S(2)}) %collective-permute-start.6) | collective-permute-done | bytes 4128 | tf_op jit(solution)/shard_map/ppermute | solution.py:873
  27.7 1.1 %adjoint_outputs.1 = (bf16[128,2048]{1,0:T(8,128)(2,1)}, bf16[128,2048]{1,0:T(8,128)(2,1)}, f32[2,1024,128]{2,1,0:T(8,128)S(1)}, bf16[64,2048]{1,0:T(8,128)(2,1)...) custom-call(bf16[128,2048]{1,0:T(8,128)(2,1)S(1)} %get-tuple-element.47.k_ref.refs_5_.refs_0_, ...), custom_call_target="tpu_custom_call" | custom-call | flops 8388608 | bytes 2097152 | tf_op jit(solution)/shard_map/adjoint_outputs/pallas_call | solution.py:834
  28.8 0.1 collective-permute-done.7.refs_11_
  28.9 1.3 %last_outputs.1 = (f32[16,2048]{1,0:T(8,128)}, bf16[128,2048]{1,0:T(8,128)(2,1)}, bf16[128,2048]{1,0:T(8,128)(2,1)}) custom-call(bf16[128,2048]{1,0:T(8,128)(2,1)S(1)} %get-tuple-element.47.k_ref.refs_5_.refs_0_, bf16[128,2048]{1,0:T(8,128)(2,1)S(1)} %get-tuple-element.48.v_ref.refs_6_.refs_1_, f32[128,2048]{1,0:T(8,128)S(1)} %get-tuple-element.67.term_ref.refs_2_, ...), custom_call_target="tpu_custom_call" | custom-call | flops 4194304 | bytes 2097152 | tf_op jit(solution)/shard_map/last_outputs/pallas_call | solution.py:888
  (10 shorter events, 0.0 us)
Async XLA Ops:
  4.3 2.8 %collective-permute-start = (f32[3,128,128]{2,1,0:T(8,128)S(1)}, f32[3,128,128]{2,1,0:T(8,128)S(1)}, u32[]{:S(2)}, u32[]{:S(2)}) collective-permute-start(f32[3,128,128]{2,1,0:T(8,128)S(1)} %get-tuple-element.60), channel_id=1, source_target_pairs={{0,4},{4,0},{8,12},{12,8},{16,20},{20,16},{24,28},{28,24},{1,5},{5... | collective-permute-start | bytes 589832 | tf_op jit(solution)/shard_map/ppermute | solution.py:687
  7.2 6.1 %collective-permute-start.1 = (bf16[3,128,128]{2,1,0:T(8,128)(2,1)S(1)}, bf16[3,128,128]{2,1,0:T(8,128)(2,1)S(1)}, u32[]{:S(2)}, u32[]{:S(2)}) collective-permute-start(bf16[3,128,128]{2,1,0:T(8,128)(2,1)S(1)} %get-tuple-element.64), channel_id=1, source_target_pairs={{0,8},{4,12},{8,0},{12,4},{16,24},{20,28},{24,16},{28,20},{1,9},{5... | collective-permute-start | bytes 294920 | tf_op jit(solution)/shard_map/ppermute | solution.py:687
  13.4 6.5 %collective-permute-start.2 = (bf16[2,128,128]{2,1,0:T(8,128)(2,1)S(1)}, bf16[2,128,128]{2,1,0:T(8,128)(2,1)S(1)}, u32[]{:S(2)}, u32[]{:S(2)}) collective-permute-start(bf16[2,128,128]{2,1,0:T(8,128)(2,1)S(1)} %get-tuple-element.68), channel_id=1, source_target_pairs={{0,16},{4,20},{8,24},{12,28},{16,0},{20,4},{24,8},{28,12},{1,17},{... | collective-permute-start | bytes 196616 | tf_op jit(solution)/shard_map/ppermute | solution.py:687
  20.1 6.1 %collective-permute-start.4 = (f32[8,128]{1,0:T(8,128)S(1)}, f32[8,128]{1,0:T(8,128)S(1)}, u32[]{:S(2)}, u32[]{:S(2)}) collective-permute-start(f32[8,128]{1,0:T(8,128)S(1)} %get-tuple-element.79.refs_0_), channel_id=1, source_target_pairs={{0,1},{1,0},{2,3},{3,2},{4,5},{5,4},{6,7},{7,6},{8,9},{9,8},{10,11... | collective-permute-start | bytes 12296 | tf_op jit(solution)/shard_map/ppermute | solution.py:873
  21.7 4.6 %collective-permute-start.5 = (f32[8,128]{1,0:T(8,128)S(1)}, f32[8,128]{1,0:T(8,128)S(1)}, u32[]{:S(2)}, u32[]{:S(2)}) collective-permute-start(f32[8,128]{1,0:T(8,128)S(1)} %get-tuple-element.79.refs_0_), channel_id=1, source_target_pairs={{0,2},{1,3},{2,0},{3,1},{4,6},{5,7},{6,4},{7,5},{8,10},{9,11},{10,... | collective-permute-start | bytes 12296 | tf_op jit(solution)/shard_map/ppermute | solution.py:873
  23.2 4.5 %collective-permute-start.6 = (f32[8,128]{1,0:T(8,128)S(1)}, f32[8,128]{1,0:T(8,128)S(1)}, u32[]{:S(2)}, u32[]{:S(2)}) collective-permute-start(f32[8,128]{1,0:T(8,128)S(1)} %get-tuple-element.79.refs_0_), channel_id=1, source_target_pairs={{0,3},{1,2},{2,1},{3,0},{4,7},{5,6},{6,5},{7,4},{8,11},{9,10},{10,... | collective-permute-start | bytes 12296 | tf_op jit(solution)/shard_map/ppermute | solution.py:873
  23.7 1.4 %collective-permute-start.3 = (f32[384,128]{1,0:T(8,128)S(1)}, f32[384,128]{1,0:T(8,128)S(1)}, u32[]{:S(2)}, u32[]{:S(2)}) collective-permute-start(f32[384,128]{1,0:T(8,128)S(1)} %get-tuple-element.70), channel_id=1, source_target_pairs={{0,4},{4,0},{8,12},{12,8},{16,20},{20,16},{24,28},{28,24},{1,5},{5... | collective-permute-start | bytes 589832 | tf_op jit(solution)/shard_map/ppermute | solution.py:687
  27.7 1.2 %collective-permute-start.7 = (f32[8,128]{1,0:T(8,128)S(1)}, f32[8,128]{1,0:T(8,128)S(1)}, u32[]{:S(2)}, u32[]{:S(2)}) collective-permute-start(f32[8,128]{1,0:T(8,128)S(1)} %square_sum.1.after_ref.refs_10_), channel_id=1, source_target_pairs={{0,4},{4,0},{8,12},{12,8},{16,20},{20,16},{24,28},{28,24},{1,5},{5... | collective-permute-start | bytes 12296 | tf_op jit(solution)/shard_map/ppermute | solution.py:687

commit v7 on v6

--- a/solution.py
+++ b/solution.py
@@ -874,7 +874,7 @@
 
     works = [add_own, forward_outputs]
     for bit in range(0, tp.bit_length() - 1, 2):
-        masks = [m << bit for m in (1, 2, 3) if m << bit < tp]
+        masks = [m << bit for m in (3, 2, 1) if m << bit < tp]
         shares = [tp_swap(square, mask) for mask in masks]
         after = square
         while works:

time: 30.3 us -> 29.3 us (0.967)
  waiting for transfers between devices: 3.79 us -> 2.83 us
    ppermute x3, waiting for transfers between devices: 1.45 us -> 0.49 us  [tp_swap(): return lax.ppermute(value, 'tp', [(i, i ^ mask) for i in range(tp)])]
  transfers between devices with their start and end apart: 8 -> 8, of which waited for: 5 -> 5; matrix products, arithmetic and copies ran while one was open for 0% -> 0% of each run, Pallas kernels for 36% -> 37%
where the time goes in v7:
time: 29.3 us; the launch traced here: 29.2 us
  Pallas kernels  16 us (55%)
  starting transfers between devices  9.57 us (33%)
  waiting for transfers between devices  2.83 us (10%)
  between operations  0.76 us (3%)
    ppermute x5, starting transfers between devices, swap(): return lax.ppermute(value, 'ctx', [(i, i ^ 1 << bit) for i in range(ctx)])  6.02 us
    pallas_call x1, Pallas kernels, shards(): pl.pallas_call(send_kernel, in_specs=[HBM] * 7, out_specs=[VMEM] * 13, ou...  3.64 us
    ppermute x3, starting transfers between devices, tp_swap(): return lax.ppermute(value, 'tp', [(i, i ^ mask) for i in range(tp)])  3.55 us
    pallas_call x1, Pallas kernels, shards(): pl.pallas_call(partial(second_local_kernel, modes), out_shape=[whole] + [...  2.7 us
    pallas_call x1, Pallas kernels, shards(): pl.pallas_call(partial(first_local_kernel, modes), out_shape=[whole, rows...  2.36 us
    ppermute x5, waiting for transfers between devices, swap(): return lax.ppermute(value, 'ctx', [(i, i ^ 1 << bit) for i in range(ctx)])  2.34 us
    pallas_call x1, Pallas kernels, shards(): pl.pallas_call(keep_kernel, out_shape=[rows(3, half)] + [own_shape] * (2...  2.32 us
    pallas_call x1, Pallas kernels, shards(): pl.pallas_call(partial(last_outputs_kernel, math.sqrt(channels * tp * mod...  1.26 us
  transfers between devices with their start and end apart: 8, of which 5 were waited for; matrix products, arithmetic and copies ran while one was open for 0% of the time, Pallas kernels for 37%

profile of v7, /device:TPU:0, one launch (start us, length us, event | category | flops | bytes accessed | tf_op | source)
XLA Modules:
  0.0 29.2 jit_solution(15529703669593698864)
XLA Ops:
  0.6 3.6 %sent_states.1 = (f32[3,128,128]{2,1,0:T(8,128)S(1)}, bf16[128,2048]{1,0:T(8,128)(2,1)S(1)}, bf16[128,2048]{1,0:T(8,128)(2,1)S(1)}, bf16[128,2048]{1,0:T(8,128)(...) custom-call(bf16[128,2048]{1,0:T(8,128)(2,1)} %q_hbm.1, ...), custom_call_target="tpu_custom_call" | custom-call | flops 12582912 | bytes 2097152 | tf_op jit(solution)/shard_map/sent_states/pallas_call | solution.py:715
  4.3 0.5 %collective-permute-start = (f32[3,128,128]{2,1,0:T(8,128)S(1)}, f32[3,128,128]{2,1,0:T(8,128)S(1)}, u32[]{:S(2)}, u32[]{:S(2)}) collective-permute-start(f32[3,128,128]{2,1,0:T(8,128)S(1)} %get-tuple-element.60), channel_id=1, source_target_pairs={{0,4},{4,0},{8,12},{12,8},{16,20},{20,16},{24,28},{28,24},{1,5},{5... | collective-permute-start | bytes 589832 | tf_op jit(solution)/shard_map/ppermute | solution.py:687
  4.8 2.3 %kept_states.1 = (f32[3,128,128]{2,1,0:T(8,128)S(1)}, f32[1,1024,128]{2,1,0:T(8,128)S(1)}, f32[1,1024,128]{2,1,0:T(8,128)S(1)}) custom-call(bf16[128,2048]{1,0:T(8,128)(2,1)S(1)} %get-tuple-element.50.q_ref.refs_4_, bf16[128,2048]{1,0:T(8,128)(2,1)S(1)} %get-tuple-element.47.k_ref.refs_5_.refs_0_, ...), custom_call_target="tpu_custom_call" | custom-call | flops 12582912 | bytes 2097152 | tf_op jit(solution)/shard_map/kept_states/pallas_call | solution.py:733
  7.1 0.0 collective-permute-done.got_ref.sibling_ref
  7.1 0.1 chip_states.1
  7.2 2.7 %collective-permute-start.1 = (bf16[3,128,128]{2,1,0:T(8,128)(2,1)S(1)}, bf16[3,128,128]{2,1,0:T(8,128)(2,1)S(1)}, u32[]{:S(2)}, u32[]{:S(2)}) collective-permute-start(bf16[3,128,128]{2,1,0:T(8,128)(2,1)S(1)} %get-tuple-element.64), channel_id=1, source_target_pairs={{0,8},{4,12},{8,0},{12,4},{16,24},{20,28},{24,16},{28,20},{1,9},{5... | collective-permute-start | bytes 294920 | tf_op jit(solution)/shard_map/ppermute | solution.py:687
  9.9 2.4 %local_conv.1 = (f32[2,1024,128]{2,1,0:T(8,128)S(1)}, f32[256,128]{1,0:T(8,128)S(1)}) custom-call(f32[1,1024,128]{2,1,0:T(8,128)S(1)} %get-tuple-element.54.gated_in.refs_0_, f32[1,1024,128]{2,1,0:T(8,128)S(1)} %get-tuple-element.56.refs_1_, f32[256,128]{1,0:T(8,128)S(1)} %get-tuple-element.52.decay_ref.refs_2_, ...), custom_call_target="tpu_custom_call" | custom-call | flops 16777216 | bytes 2097152 | tf_op jit(solution)/shard_map/local_conv/pallas_call | solution.py:761
  12.3 1.0 %collective-permute-done.1.got_ref = bf16[3,128,128]{2,1,0:T(8,128)(2,1)S(1)} collective-permute-done((bf16[3,128,128]{2,1,0:T(8,128)(2,1)S(1)}, bf16[3,128,128]{2,1,0:T(8,128)(2,1)S(1)}, u32[]{:S(2)}, u32[]{:S(2)}) %collective-permute-start.1) | collective-permute-done | bytes 98336 | tf_op jit(solution)/shard_map/ppermute | solution.py:687
  13.3 0.1 block_states.1
  13.4 2.8 %collective-permute-start.2 = (bf16[2,128,128]{2,1,0:T(8,128)(2,1)S(1)}, bf16[2,128,128]{2,1,0:T(8,128)(2,1)S(1)}, u32[]{:S(2)}, u32[]{:S(2)}) collective-permute-start(bf16[2,128,128]{2,1,0:T(8,128)(2,1)S(1)} %get-tuple-element.68), channel_id=1, source_target_pairs={{0,16},{4,20},{8,24},{12,28},{16,0},{20,4},{24,8},{28,12},{1,17},{... | collective-permute-start | bytes 196616 | tf_op jit(solution)/shard_map/ppermute | solution.py:687
  16.3 2.7 %local_adjoint.1 = (f32[2,1024,128]{2,1,0:T(8,128)S(1)}, f32[128,2048]{1,0:T(8,128)S(1)}, f32[128,2048]{1,0:T(8,128)S(1)}) custom-call(f32[1,1024,128]{2,1,0:T(8,128)S(1)} %get-tuple-element.49.pulled_in.refs_0_, f32[1,1024,128]{2,1,0:T(8,128)S(1)} %get-tuple-element.55.refs_1_, f32[256,128]{1,0:T(8,128)S(1)} %get-tuple-element.52.decay_ref.refs_2_, ...), custom_call_target="tpu_custom_call" | custom-call | flops 16777216 | bytes 2097152 | tf_op jit(solution)/shard_map/local_adjoint/pallas_call | solution.py:777
  19.0 1.0 %collective-permute-done.2.got_ref = bf16[2,128,128]{2,1,0:T(8,128)(2,1)S(1)} collective-permute-done((bf16[2,128,128]{2,1,0:T(8,128)(2,1)S(1)}, bf16[2,128,128]{2,1,0:T(8,128)(2,1)S(1)}, u32[]{:S(2)}, u32[]{:S(2)}) %collective-permute-start.2) | collective-permute-done | bytes 65568 | tf_op jit(solution)/shard_map/ppermute | solution.py:687
  20.0 0.1 carries.1
  20.1 2.5 %collective-permute-start.4 = (f32[8,128]{1,0:T(8,128)S(1)}, f32[8,128]{1,0:T(8,128)S(1)}, u32[]{:S(2)}, u32[]{:S(2)}) collective-permute-start(f32[8,128]{1,0:T(8,128)S(1)} %get-tuple-element.79.refs_0_), channel_id=1, source_target_pairs={{0,3},{1,2},{2,1},{3,0},{4,7},{5,6},{6,5},{7,4},{8,11},{9,10},{10,... | collective-permute-start | bytes 12296 | tf_op jit(solution)/shard_map/ppermute | solution.py:873
  22.6 0.5 %collective-permute-start.5 = (f32[8,128]{1,0:T(8,128)S(1)}, f32[8,128]{1,0:T(8,128)S(1)}, u32[]{:S(2)}, u32[]{:S(2)}) collective-permute-start(f32[8,128]{1,0:T(8,128)S(1)} %get-tuple-element.79.refs_0_), channel_id=1, source_target_pairs={{0,2},{1,3},{2,0},{3,1},{4,6},{5,7},{6,4},{7,5},{8,10},{9,11},{10,... | collective-permute-start | bytes 12296 | tf_op jit(solution)/shard_map/ppermute | solution.py:873
  23.1 0.5 %collective-permute-start.6 = (f32[8,128]{1,0:T(8,128)S(1)}, f32[8,128]{1,0:T(8,128)S(1)}, u32[]{:S(2)}, u32[]{:S(2)}) collective-permute-start(f32[8,128]{1,0:T(8,128)S(1)} %get-tuple-element.79.refs_0_), channel_id=1, source_target_pairs={{0,1},{1,0},{2,3},{3,2},{4,5},{5,4},{6,7},{7,6},{8,9},{9,8},{10,11... | collective-permute-start | bytes 12296 | tf_op jit(solution)/shard_map/ppermute | solution.py:873
  23.7 1.2 %own_carries.1 = (f32[1,1024,128]{2,1,0:T(8,128)S(1)}, f32[1,1024,128]{2,1,0:T(8,128)S(1)}) custom-call(f32[2,1024,128]{2,1,0:T(8,128)S(1)} %get-tuple-element.65.conv_ref, f32[2,1024,128]{2,1,0:T(8,128)S(1)} %get-tuple-element.69.adj_ref, f32[256,128]{1,0:T(8,128)S(1)} %get-tuple-element.52.decay_ref.refs_2_, ...), custom_call_target="tpu_custom_call" | custom-call | flops 8388608 | bytes 2097152 | tf_op jit(solution)/shard_map/own_carries/pallas_call | solution.py:797
  24.9 0.2 collective-permute-done.3.other_ref.refs_7_
  25.1 1.1 %forward_outputs.1 = (bf16[128,2048]{1,0:T(8,128)(2,1)S(1)}, bf16[128,2048]{1,0:T(8,128)(2,1)S(1)}, f32[8,128]{1,0:T(8,128)S(1)}) custom-call(bf16[128,2048]{1,0:T(8,128)(2,1)S(1)} %get-tuple-element.50.q_ref.refs_4_, bf16[128,2048]{1,0:T(8,128)(2,1)S(1)} %get-tuple-element.51.ct_ref.refs_7_, f32[128,2048]{1,0:T(8,128)S(1)} %get-tuple-element.74.term_ref, ...), custom_call_target="tpu_custom_call" | custom-call | flops 8388608 | bytes 4194304 | tf_op jit(solution)/shard_map/forward_outputs/pallas_call | solution.py:809
  26.2 0.0 collective-permute-done.4.refs_1_
  26.2 0.5 %collective-permute-done.6.refs_3_ = f32[8,128]{1,0:T(8,128)S(1)} collective-permute-done((f32[8,128]{1,0:T(8,128)S(1)}, f32[8,128]{1,0:T(8,128)S(1)}, u32[]{:S(2)}, u32[]{:S(2)}) %collective-permute-start.6) | collective-permute-done | bytes 4128 | tf_op jit(solution)/shard_map/ppermute | solution.py:873
  26.7 1.1 %adjoint_outputs.1 = (bf16[128,2048]{1,0:T(8,128)(2,1)}, bf16[128,2048]{1,0:T(8,128)(2,1)}, f32[2,1024,128]{2,1,0:T(8,128)S(1)}, bf16[64,2048]{1,0:T(8,128)(2,1)...) custom-call(bf16[128,2048]{1,0:T(8,128)(2,1)S(1)} %get-tuple-element.47.k_ref.refs_5_.refs_0_, ...), custom_call_target="tpu_custom_call" | custom-call | flops 8388608 | bytes 2097152 | tf_op jit(solution)/shard_map/adjoint_outputs/pallas_call | solution.py:834
  27.8 0.1 collective-permute-done.7.refs_11_
  27.9 1.3 %last_outputs.1 = (f32[16,2048]{1,0:T(8,128)}, bf16[128,2048]{1,0:T(8,128)(2,1)}, bf16[128,2048]{1,0:T(8,128)(2,1)}) custom-call(bf16[128,2048]{1,0:T(8,128)(2,1)S(1)} %get-tuple-element.47.k_ref.refs_5_.refs_0_, bf16[128,2048]{1,0:T(8,128)(2,1)S(1)} %get-tuple-element.48.v_ref.refs_6_.refs_1_, f32[128,2048]{1,0:T(8,128)S(1)} %get-tuple-element.67.term_ref.refs_2_, ...), custom_call_target="tpu_custom_call" | custom-call | flops 4194304 | bytes 2097152 | tf_op jit(solution)/shard_map/last_outputs/pallas_call | solution.py:888
  (10 shorter events, 0.0 us)
Async XLA Ops:
  4.3 2.8 %collective-permute-start = (f32[3,128,128]{2,1,0:T(8,128)S(1)}, f32[3,128,128]{2,1,0:T(8,128)S(1)}, u32[]{:S(2)}, u32[]{:S(2)}) collective-permute-start(f32[3,128,128]{2,1,0:T(8,128)S(1)} %get-tuple-element.60), channel_id=1, source_target_pairs={{0,4},{4,0},{8,12},{12,8},{16,20},{20,16},{24,28},{28,24},{1,5},{5... | collective-permute-start | bytes 589832 | tf_op jit(solution)/shard_map/ppermute | solution.py:687
  7.2 6.1 %collective-permute-start.1 = (bf16[3,128,128]{2,1,0:T(8,128)(2,1)S(1)}, bf16[3,128,128]{2,1,0:T(8,128)(2,1)S(1)}, u32[]{:S(2)}, u32[]{:S(2)}) collective-permute-start(bf16[3,128,128]{2,1,0:T(8,128)(2,1)S(1)} %get-tuple-element.64), channel_id=1, source_target_pairs={{0,8},{4,12},{8,0},{12,4},{16,24},{20,28},{24,16},{28,20},{1,9},{5... | collective-permute-start | bytes 294920 | tf_op jit(solution)/shard_map/ppermute | solution.py:687
  13.4 6.5 %collective-permute-start.2 = (bf16[2,128,128]{2,1,0:T(8,128)(2,1)S(1)}, bf16[2,128,128]{2,1,0:T(8,128)(2,1)S(1)}, u32[]{:S(2)}, u32[]{:S(2)}) collective-permute-start(bf16[2,128,128]{2,1,0:T(8,128)(2,1)S(1)} %get-tuple-element.68), channel_id=1, source_target_pairs={{0,16},{4,20},{8,24},{12,28},{16,0},{20,4},{24,8},{28,12},{1,17},{... | collective-permute-start | bytes 196616 | tf_op jit(solution)/shard_map/ppermute | solution.py:687
  20.1 6.1 %collective-permute-start.4 = (f32[8,128]{1,0:T(8,128)S(1)}, f32[8,128]{1,0:T(8,128)S(1)}, u32[]{:S(2)}, u32[]{:S(2)}) collective-permute-start(f32[8,128]{1,0:T(8,128)S(1)} %get-tuple-element.79.refs_0_), channel_id=1, source_target_pairs={{0,3},{1,2},{2,1},{3,0},{4,7},{5,6},{6,5},{7,4},{8,11},{9,10},{10,... | collective-permute-start | bytes 12296 | tf_op jit(solution)/shard_map/ppermute | solution.py:873
  22.6 3.6 %collective-permute-start.5 = (f32[8,128]{1,0:T(8,128)S(1)}, f32[8,128]{1,0:T(8,128)S(1)}, u32[]{:S(2)}, u32[]{:S(2)}) collective-permute-start(f32[8,128]{1,0:T(8,128)S(1)} %get-tuple-element.79.refs_0_), channel_id=1, source_target_pairs={{0,2},{1,3},{2,0},{3,1},{4,6},{5,7},{6,4},{7,5},{8,10},{9,11},{10,... | collective-permute-start | bytes 12296 | tf_op jit(solution)/shard_map/ppermute | solution.py:873
  23.1 3.6 %collective-permute-start.6 = (f32[8,128]{1,0:T(8,128)S(1)}, f32[8,128]{1,0:T(8,128)S(1)}, u32[]{:S(2)}, u32[]{:S(2)}) collective-permute-start(f32[8,128]{1,0:T(8,128)S(1)} %get-tuple-element.79.refs_0_), channel_id=1, source_target_pairs={{0,1},{1,0},{2,3},{3,2},{4,5},{5,4},{6,7},{7,6},{8,9},{9,8},{10,11... | collective-permute-start | bytes 12296 | tf_op jit(solution)/shard_map/ppermute | solution.py:873
  23.7 1.4 %collective-permute-start.3 = (f32[384,128]{1,0:T(8,128)S(1)}, f32[384,128]{1,0:T(8,128)S(1)}, u32[]{:S(2)}, u32[]{:S(2)}) collective-permute-start(f32[384,128]{1,0:T(8,128)S(1)} %get-tuple-element.70), channel_id=1, source_target_pairs={{0,4},{4,0},{8,12},{12,8},{16,20},{20,16},{24,28},{28,24},{1,5},{5... | collective-permute-start | bytes 589832 | tf_op jit(solution)/shard_map/ppermute | solution.py:687
  26.7 1.2 %collective-permute-start.7 = (f32[8,128]{1,0:T(8,128)S(1)}, f32[8,128]{1,0:T(8,128)S(1)}, u32[]{:S(2)}, u32[]{:S(2)}) collective-permute-start(f32[8,128]{1,0:T(8,128)S(1)} %square_sum.1.after_ref.refs_10_), channel_id=1, source_target_pairs={{0,4},{4,0},{8,12},{12,8},{16,20},{20,16},{24,28},{28,24},{1,5},{5... | collective-permute-start | bytes 12296 | tf_op jit(solution)/shard_map/ppermute | solution.py:687
